TPU v7x, 32 devices: a whole 2x2x4 slice. The times are simulated.
32 devices in a mesh: row: 4 (over y, x), col: 8 (over z, core).
Axes of the slice: x: 2, y: 2, z: 4, core: 2. Of those that a mesh axis runs over, the one named last changes fastest.
Arguments:
- tokens: bfloat16 [256, 10240], P('col', 'row'), may hold values from -6 to 6
- out_grad: bfloat16 [256, 10240], P('col', 'row'), may hold values from -3 to 3
- gate_weight: bfloat16 [10240, 26624], P('row', 'col'), may hold values from -0.0625 to 0.0625
- up_weight: bfloat16 [10240, 26624], P('row', 'col'), may hold values from -0.0625 to 0.0625
- down_weight: bfloat16 [26624, 10240], P('col', 'row'), may hold values from -0.0390625 to 0.0390625
- gate_mask: int32 [2560, 6656], P('row', 'col'), may hold values from 0 to 23
- up_mask: int32 [2560, 6656], P('row', 'col'), may hold values from 0 to 23
- down_mask: int32 [6656, 2560], P('col', 'row'), may hold values from 0 to 23
Outputs:
- input_grad: bfloat16 [256, 10240], P('col', 'row')
- gate_weight_grad: bfloat16 [10240, 26624], P('row', 'col')
- up_weight_grad: bfloat16 [10240, 26624], P('row', 'col')
- down_weight_grad: bfloat16 [26624, 10240], P('col', 'row')
Inputs may be any that keep to these rules, and one draw needn't show every extreme that they name: `gate_mask`: each entry is a pattern code as the first step defines, so every row and every column of each 4 by 4 block of a pruned weight keeps exactly two entries. `up_mask`: as for gate_mask. `down_mask`: as for gate_mask.
All inputs are finite; a program needn't handle non-finite values.
Results may differ from a plain program's by a relative error of at most 0.0049.
Values may be sent and summed in bfloat16 or wider, within the bound.
No kernel may reach another device: no remote copies, remote signals or barrier semaphores. Data moves between devices by JAX's collectives and lax.ppermute only.
A program may use at most 256 MiB of HBM per device.

v0:
```python
import jax
import jax.numpy as jnp
from jax import lax
from jax.sharding import PartitionSpec as P


def expand_mask(block_ids):
    lead_col = block_ids // 6
    second_rank = block_ids // 2 % 3
    third_rank = block_ids % 2
    second_col = second_rank + (second_rank >= lead_col).astype(jnp.int32)
    low_col = jnp.minimum(lead_col, second_col)
    high_col = jnp.maximum(lead_col, second_col)
    rest_low = jnp.where(low_col > 0, 0, jnp.where(high_col > 1, 1, 2)).astype(jnp.int32)
    rest_high = 6 - low_col - high_col - rest_low
    third_col = jnp.where(third_rank == 0, rest_low, rest_high)
    fourth_col = 6 - lead_col - second_col - third_col
    ordering = [lead_col, second_col, third_col, fourth_col]
    group_rows, group_cols = block_ids.shape
    col_position = lax.broadcasted_iota(jnp.int32, (group_rows, 4 * group_cols), 1) % 4
    row_list = []
    for local_row in range(4):
        current = jnp.repeat(ordering[local_row], 4, axis=1)
        following = jnp.repeat(ordering[(local_row + 1) % 4], 4, axis=1)
        row_list.append((current == col_position) | (following == col_position))
    pattern = jnp.stack(row_list, axis=1).reshape(4 * group_rows, 4 * group_cols)
    return pattern.astype(jnp.bfloat16)


def contract_last(left, right):
    return lax.dot_general(
        left, right, (((1,), (1,)), ((), ())), preferred_element_type=jnp.float32
    )


def contract_first(left, right):
    return lax.dot_general(
        left, right, (((0,), (0,)), ((), ())), preferred_element_type=jnp.float32
    )


def local(tokens, out_grad, gate_weight, up_weight, down_weight, gate_mask, up_mask, down_mask):
    gate_keep = expand_mask(gate_mask)
    up_keep = expand_mask(up_mask)
    down_keep = expand_mask(down_mask)
    gate_pruned = gate_weight * gate_keep
    up_pruned = up_weight * up_keep
    down_pruned = down_weight * down_keep
    panel_width = gate_pruned.shape[1]
    all_tokens, all_grads = (
        lax.all_gather(tokens, "col", axis=0, tiled=True),
        lax.all_gather(out_grad, "col", axis=0, tiled=True),
    )
    gate_sum = jnp.dot(all_tokens, gate_pruned, preferred_element_type=jnp.float32)
    up_sum = jnp.dot(all_tokens, up_pruned, preferred_element_type=jnp.float32)
    back_sum = contract_last(all_grads, down_pruned)
    shares = lax.psum_scatter(
        jnp.concatenate([gate_sum, up_sum, back_sum], axis=1),
        "row",
        scatter_dimension=0,
        tiled=True,
    )
    gate_sum = shares[:, :panel_width]
    up_sum = shares[:, panel_width : 2 * panel_width]
    back_sum = shares[:, 2 * panel_width :]
    logistic = jax.nn.sigmoid(gate_sum)
    swish_val = gate_sum * logistic
    hidden = swish_val * up_sum
    swiglu_up_grad = back_sum * swish_val
    swiglu_gate_grad = back_sum * up_sum * logistic * (1.0 + gate_sum * (1.0 - logistic))
    local_grads = jnp.concatenate([swiglu_gate_grad, swiglu_up_grad, hidden], axis=1).astype(
        jnp.bfloat16
    )
    all_local = lax.all_gather(local_grads, "row", axis=0, tiled=True)
    gate_grad = all_local[:, :panel_width]
    up_grad = all_local[:, panel_width : 2 * panel_width]
    hidden = all_local[:, 2 * panel_width :]
    input_grad = lax.psum_scatter(
        contract_last(gate_grad, gate_pruned) + contract_last(up_grad, up_pruned),
        "col",
        scatter_dimension=0,
        tiled=True,
    ).astype(jnp.bfloat16)
    gate_weight_grad = (contract_first(all_tokens, gate_grad) * gate_keep).astype(jnp.bfloat16)
    up_weight_grad = (contract_first(all_tokens, up_grad) * up_keep).astype(jnp.bfloat16)
    down_weight_grad = (contract_first(hidden, all_grads) * down_keep).astype(jnp.bfloat16)
    return (input_grad, gate_weight_grad, up_weight_grad, down_weight_grad)


def solution(mesh):
    in_specs = (
        P("col", "row"),
        P("col", "row"),
        P("row", "col"),
        P("row", "col"),
        P("col", "row"),
        P("row", "col"),
        P("row", "col"),
        P("col", "row"),
    )
    out_specs = (P("col", "row"), P("row", "col"), P("row", "col"), P("col", "row"))
    return jax.shard_map(local, mesh=mesh, in_specs=in_specs, out_specs=out_specs, check_vma=False)
```

profile of v0, /device:TPU:0, one launch (start us, length us, event | category | flops | bytes accessed | tf_op | source)
XLA Modules:
  0.0 876.8 jit_solution(1889266348678922096)
XLA Ops:
  178.4 12.9 %fusion.47 = (pred[640,1,3328]{0,2,1:T(8,128)(4,1)}, pred[640,1,3328]{0,2,1:T(8,128)(4,1)S(1)}, pred[640,1,3328]{0,2,1:T(8,128)(4,1)S(1)}, pred[640,1,3328]{0,2,1:T(8,128)(4,1)S(1)}, pred[640,1,3328]{0,2,1:T(8,128)(4,1)S(1)}) fusion(pred[640,1,3328]{0,2,1:T(8,128)(4,1)S(1)} %get-tuple-element.21, s32[640,1,3328]{0,2,1:T(8,128)} %reshape.906, ...), kind=kLoop, calls=%fused_computation.109 | loop fusion | flops 12779520 | bytes 38368512 | tf_op jit(solution)/shard_map/or | solution.py:25
  210.2 27.8 %copy.39 = pred[640,4,3328]{2,1,0:T(4,128)(4,1)} copy(pred[640,4,3328]{0,2,1:T(8,128)(4,1)} %pad_add_fusion.1) | data formatting | bytes 17039360 | tf_op jit(solution)/shard_map/stack | solution.py:26
  238.1 25.6 %reshape.903 = pred[2560,3328]{1,0:T(32,128)(4,1)} reshape(pred[640,4,3328]{2,1,0:T(4,128)(4,1)} %copy.39) | data formatting | bytes 17039360 | tf_op jit(solution)/shard_map/reshape | solution.py:26
  268.9 11.5 %reshape.910 = s32[832,1,2560]{0,2,1:T(8,128)} reshape(s32[832,640,4]{0,2,1:T(4,128)} %broadcast_in_dim.72) | data formatting | bytes 17039360 | tf_op jit(solution)/shard_map/reshape | solution.py:24
  288.1 11.5 %reshape.909 = s32[832,1,2560]{0,2,1:T(8,128)} reshape(s32[832,640,4]{0,2,1:T(4,128)} %broadcast_in_dim.71) | data formatting | bytes 17039360 | tf_op jit(solution)/shard_map/reshape | solution.py:23
  307.4 11.5 %reshape.911 = s32[832,1,2560]{0,2,1:T(8,128)} reshape(s32[832,640,4]{0,2,1:T(4,128)} %broadcast_in_dim.73) | data formatting | bytes 17039360 | tf_op jit(solution)/shard_map/reshape | solution.py:24
  326.5 11.5 %reshape.912 = s32[832,1,2560]{0,2,1:T(8,128)} reshape(s32[832,640,4]{0,2,1:T(4,128)} %broadcast_in_dim.74) | data formatting | bytes 17039360 | tf_op jit(solution)/shard_map/reshape | solution.py:24
  365.1 27.9 %copy.45 = pred[832,4,2560]{2,1,0:T(4,128)(4,1)} copy(pred[832,4,2560]{0,2,1:T(8,128)(4,1)} %pad_add_fusion) | data formatting | bytes 17039360 | tf_op jit(solution)/shard_map/stack | solution.py:26
  393.1 20.7 %reshape.913 = pred[3328,2560]{1,0:T(32,128)(4,1)} reshape(pred[832,4,2560]{2,1,0:T(4,128)(4,1)} %copy.45) | data formatting | bytes 17039360 | tf_op jit(solution)/shard_map/reshape | solution.py:26
  422.2 27.8 %copy.40 = pred[640,4,3328]{2,1,0:T(4,128)(4,1)} copy(pred[640,4,3328]{0,2,1:T(8,128)(4,1)} %pad_add_fusion.2) | data formatting | bytes 17039360 | tf_op jit(solution)/shard_map/stack | solution.py:26
  450.0 25.5 %reshape.908 = pred[2560,3328]{1,0:T(32,128)(4,1)} reshape(pred[640,4,3328]{2,1,0:T(4,128)(4,1)} %copy.40) | data formatting | bytes 17039360 | tf_op jit(solution)/shard_map/reshape | solution.py:26
  475.5 11.7 %fusion.9 = f32[256,3328]{0,1:T(8,128)S(1)} fusion(bf16[256,2560]{1,0:T(8,128)(2,1)} %all-gather.4.cloned.1.call-done, pred[2560,3328]{1,0:T(32,128)(4,1)} %reshape.908, bf16[2560,3328]{1,0:T(8,128)(2,1)} %param.11), kind=kOutput, calls=%fused_computation.30 | convolution fusion | flops 4370595840 | bytes 30277632 | tf_op jit(solution)/shard_map/dot_general | solution.py:55
  487.2 15.9 %fusion.10 = f32[256,3328]{0,1:T(8,128)} fusion(bf16[256,2560]{1,0:T(8,128)(2,1)S(1)} %copy-done.17, pred[2560,3328]{1,0:T(32,128)(4,1)} %reshape.903, bf16[2560,3328]{1,0:T(8,128)(2,1)} %param.10), kind=kOutput, calls=%fused_computation.31 | convolution fusion | flops 4370595840 | bytes 30277632 | tf_op jit(solution)/shard_map/dot_general | solution.py:54
  503.1 15.7 %fusion.11 = f32[256,3328]{0,1:T(8,128)} fusion(bf16[256,2560]{1,0:T(8,128)(2,1)} %all-gather.6.cloned.1.call-done, pred[3328,2560]{1,0:T(32,128)(4,1)} %reshape.913, bf16[3328,2560]{1,0:T(8,128)(2,1)} %param.12), kind=kOutput, calls=%fused_computation.32 | convolution fusion | flops 4370595840 | bytes 30277632 | tf_op jit(solution)/shard_map/dot_general | solution.py:31
  539.3 104.2 %reduce-scatter.7.cloned.1.call-done = f32[64,9984]{1,0:T(8,128)} async-done(((f32[256,9984]{1,0:T(8,128)}), f32[64,9984]{1,0:T(8,128)}) %reduce-scatter.7.cloned.1.call-update) | async-done | bytes 2555920 | tf_op jit(solution)/shard_map/reduce_scatter | solution.py:57
  646.7 60.4 %all-gather.8.cloned.1.call-done = bf16[256,9984]{1,0:T(8,128)(2,1)} async-done(((bf16[64,9984]{1,0:T(8,128)(2,1)}), bf16[256,9984]{1,0:T(8,128)(2,1)}) %all-gather.8.cloned.1.call-update) | async-done | bytes 5111824 | tf_op jit(solution)/shard_map/all_gather | solution.py:74
  707.2 12.9 %fusion.5 = f32[256,2560]{1,0:T(8,128)} fusion(pred[2560,3328]{1,0:T(32,128)(4,1)} %reshape.903, bf16[2560,3328]{1,0:T(8,128)(2,1)} %param.10, bf16[256,9984]{1,0:T(8,128)(2,1)} %all-gather.8.cloned.1.call-done), kind=kOutput, calls=%fused_computation.26 | convolution fusion | flops 4370595840 | bytes 29884416 | tf_op jit(solution)/shard_map/dot_general | solution.py:31
  720.1 13.2 %fusion.14 = f32[256,2560]{1,0:T(8,128)} fusion(f32[256,2560]{1,0:T(8,128)} %fusion.5, pred[2560,3328]{1,0:T(32,128)(4,1)} %reshape.908, bf16[2560,3328]{1,0:T(8,128)(2,1)} %param.11, bf16[256,9984]{1,0:T(8,128)(2,1)S(1)} %copy-done.16), kind=kOutput, calls=%fused_computation.33 | convolution fusion | flops 4371251200 | bytes 32505856 | tf_op jit(solution)/shard_map/dot_general | solution.py:31
  733.3 27.1 %copy.49 = pred[2560,3328]{0,1:T(32,128)(4,1)S(1)} copy(pred[2560,3328]{1,0:T(32,128)(4,1)} %reshape.903) | data formatting | bytes 17039360 | tf_op jit(solution)/shard_map/reshape | solution.py:26
  760.4 28.2 %copy.50 = pred[2560,3328]{0,1:T(32,128)(4,1)} copy(pred[2560,3328]{1,0:T(32,128)(4,1)} %reshape.908) | data formatting | bytes 17039360 | tf_op jit(solution)/shard_map/reshape | solution.py:26
  788.6 11.8 %fusion.1 = bf16[2560,3328]{0,1:T(8,128)(2,1)} fusion(bf16[256,2560]{1,0:T(8,128)(2,1)S(1)} %copy-done.18, pred[2560,3328]{0,1:T(32,128)(4,1)S(1)} %copy.49, bf16[256,9984]{1,0:T(8,128)(2,1)} %all-gather.8.cloned.1.call-done), kind=kOutput, calls=%fused_computation.12 | convolution fusion | flops 4396154880 | bytes 28573696 | tf_op jit(solution)/shard_map/dot_general | solution.py:37
  800.4 22.4 %copy.51 = bf16[2560,3328]{1,0:T(8,128)(2,1)} copy(bf16[2560,3328]{0,1:T(8,128)(2,1)} %fusion.1) | data formatting | bytes 34078720
  834.3 22.5 %copy.52 = bf16[2560,3328]{1,0:T(8,128)(2,1)} copy(bf16[2560,3328]{0,1:T(8,128)(2,1)} %fusion) | data formatting | bytes 34078720
  856.8 11.5 %multiply_convert_fusion = bf16[3328,2560]{1,0:T(8,128)(2,1)} fusion(bf16[256,2560]{1,0:T(8,128)(2,1)S(1)} %copy-done.19, pred[3328,2560]{1,0:T(32,128)(4,1)} %reshape.913, bf16[256,9984]{1,0:T(8,128)(2,1)} %all-gather.8.cloned.1.call-done), kind=kOutput, calls=%fused_computation.13 | convolution fusion | flops 4396154880 | bytes 28573696 | tf_op jit(solution)/shard_map/dot_general | solution.py:37
  (133 shorter events, 290.5 us)
Async XLA Ops:
  7.2 468.3 %all-gather.4.cloned.1.call-start = ((), (), s32[]{:S(2)}) async-start(), calls=%async_computation.2 | async-start | bytes 1474560 | tf_op jit(solution)/shard_map/all_gather | solution.py:51
  7.9 495.2 %all-gather.6.cloned.1.call-start = ((), (), s32[]{:S(2)}) async-start(), calls=%async_computation.3 | async-start | bytes 1474560 | tf_op jit(solution)/shard_map/all_gather | solution.py:52
  8.6 634.8 %reduce-scatter.7.cloned.1.call-start = ((), (), s32[]{:S(2)}) async-start(), calls=%async_computation.6 | async-start | bytes 12779520 | tf_op jit(solution)/shard_map/reduce_scatter | solution.py:57
  178.3 13.0 %slice-start.3 = ((s8[8519680]{0:T(1024)(128)(4,1)}), s8[4194304]{0:T(1024)(128)(4,1)S(1)}, s32[]{:S(2)}) async-start(s8[8519680]{0:T(1024)(128)(4,1)} %bitcast.47), calls=%async_computation.10 | async-start | bytes 8388608
  178.3 13.0 %slice-start.9 = ((s8[8519680]{0:T(1024)(128)(4,1)}), s8[4194304]{0:T(1024)(128)(4,1)S(1)}, s32[]{:S(2)}) async-start(s8[8519680]{0:T(1024)(128)(4,1)} %bitcast.51), calls=%async_computation.16 | async-start | bytes 8388608
  178.3 13.0 %slice-start.4 = ((s8[8519680]{0:T(1024)(128)(4,1)}), s8[4194304]{0:T(1024)(128)(4,1)S(1)}, s32[]{:S(2)}) async-start(s8[8519680]{0:T(1024)(128)(4,1)} %bitcast.47), calls=%async_computation.11 | async-start | bytes 8388608
  178.3 13.0 %slice-start.5 = ((s8[8519680]{0:T(1024)(128)(4,1)}), s8[131072]{0:T(1024)(128)(4,1)S(1)}, s32[]{:S(2)}) async-start(s8[8519680]{0:T(1024)(128)(4,1)} %bitcast.47), calls=%async_computation.12 | async-start | bytes 262144
  178.3 14.0 %slice-start.10 = ((s8[8519680]{0:T(1024)(128)(4,1)}), s8[4194304]{0:T(1024)(128)(4,1)S(1)}, s32[]{:S(2)}) async-start(s8[8519680]{0:T(1024)(128)(4,1)} %bitcast.51), calls=%async_computation.17 | async-start | bytes 8388608
  178.4 14.0 %slice-start.11 = ((s8[8519680]{0:T(1024)(128)(4,1)}), s8[131072]{0:T(1024)(128)(4,1)S(1)}, s32[]{:S(2)}) async-start(s8[8519680]{0:T(1024)(128)(4,1)} %bitcast.51), calls=%async_computation.18 | async-start | bytes 262144
  178.4 22.0 %slice-start.6 = ((s8[8519680]{0:T(1024)(128)(4,1)}), s8[4194304]{0:T(1024)(128)(4,1)S(1)}, s32[]{:S(2)}) async-start(s8[8519680]{0:T(1024)(128)(4,1)} %bitcast.49), calls=%async_computation.13 | async-start | bytes 8388608
  178.4 22.0 %slice-start.7 = ((s8[8519680]{0:T(1024)(128)(4,1)}), s8[4194304]{0:T(1024)(128)(4,1)S(1)}, s32[]{:S(2)}) async-start(s8[8519680]{0:T(1024)(128)(4,1)} %bitcast.49), calls=%async_computation.14 | async-start | bytes 8388608
  238.1 25.7 %copy-start = (s32[832,640]{0,1:T(8,128)S(1)}, s32[832,640]{0,1:T(8,128)}, u32[]{:S(2)}) copy-start(s32[832,640]{0,1:T(8,128)} %copy.42) | copy-start | bytes 6389764
  326.5 11.5 %copy-start.13 = (s32[2560]{0:T(1024)S(1)}, s32[2560]{0:T(1024)}, u32[]{:S(2)}) copy-start(s32[2560]{0:T(1024)} %get-tuple-element.63) | copy-start | bytes 30724
  326.5 11.5 %copy-start.14 = (s32[2560]{0:T(1024)S(1)}, s32[2560]{0:T(1024)}, u32[]{:S(2)}) copy-start(s32[2560]{0:T(1024)} %get-tuple-element.64) | copy-start | bytes 30724
  326.5 11.5 %copy-start.15 = (pred[2560]{0:T(1024)(128)(4,1)S(1)}, pred[2560]{0:T(1024)(128)(4,1)}, u32[]{:S(2)}) copy-start(pred[2560]{0:T(1024)(128)(4,1)} %fusion.40) | copy-start | bytes 7684
  338.0 16.4 %slice-start = ((s8[9175040]{0:T(1024)(128)(4,1)}), s8[4194304]{0:T(1024)(128)(4,1)S(1)}, s32[]{:S(2)}) async-start(s8[9175040]{0:T(1024)(128)(4,1)} %bitcast.45), calls=%async_computation.7 | async-start | bytes 8388608
  338.0 16.4 %slice-start.1 = ((s8[9175040]{0:T(1024)(128)(4,1)}), s8[786432]{0:T(1024)(128)(4,1)S(1)}, s32[]{:S(2)}) async-start(s8[9175040]{0:T(1024)(128)(4,1)} %bitcast.45), calls=%async_computation.8 | async-start | bytes 1572864
  393.1 20.7 %copy-start.1 = (pred[640,1,3328]{0,2,1:T(8,128)(4,1)S(1)}, pred[640,1,3328]{0,2,1:T(8,128)(4,1)}, u32[]{:S(2)}) copy-start(pred[640,1,3328]{0,2,1:T(8,128)(4,1)} %get-tuple-element.22) | copy-start | bytes 6389764
  475.5 11.7 %copy-start.17 = (bf16[256,2560]{1,0:T(8,128)(2,1)S(1)}, bf16[256,2560]{1,0:T(8,128)(2,1)}, u32[]{:S(2)}) copy-start(bf16[256,2560]{1,0:T(8,128)(2,1)} %all-gather.4.cloned.1.call-done) | copy-start | bytes 3932164
  539.2 168.0 %all-gather.8.cloned.1.call-start = ((), (), s32[]{:S(2)}) async-start(), calls=%async_computation.4 | async-start | bytes 6389760 | tf_op jit(solution)/shard_map/all_gather | solution.py:74
  646.7 221.5 %reduce-scatter.5.cloned.1.call-start = ((), (), s32[]{:S(2)}) async-start(), calls=%async_computation.5 | async-start | bytes 2949120 | tf_op jit(solution)/shard_map/reduce_scatter | solution.py:78
  707.2 12.9 %copy-start.16 = (bf16[256,9984]{1,0:T(8,128)(2,1)S(1)}, bf16[256,9984]{1,0:T(8,128)(2,1)}, u32[]{:S(2)}) copy-start(bf16[256,9984]{1,0:T(8,128)(2,1)} %all-gather.8.cloned.1.call-done) | copy-start | bytes 15335428
  760.4 28.2 %copy-start.18 = (bf16[256,2560]{1,0:T(8,128)(2,1)S(1)}, bf16[256,2560]{1,0:T(8,128)(2,1)}, u32[]{:S(2)}) copy-start(bf16[256,2560]{1,0:T(8,128)(2,1)} %all-gather.4.cloned.1.call-done) | copy-start | bytes 3932164
  834.3 22.5 %copy-start.19 = (bf16[256,2560]{1,0:T(8,128)(2,1)S(1)}, bf16[256,2560]{1,0:T(8,128)(2,1)}, u32[]{:S(2)}) copy-start(bf16[256,2560]{1,0:T(8,128)(2,1)} %all-gather.6.cloned.1.call-done) | copy-start | bytes 3932164
  (13 other events, 99.4 us)
Sparse Core Ops, SparseCore 0:
  9.6 26.1 all-gather.3
  37.5 22.9 all-gather.5
  539.3 104.0 reduce-scatter.6
  646.8 60.3 all-gather.7
  733.4 37.4 reduce-scatter.4
where the time goes:
time: 893 us; the launch traced here: 877 us
  local copies, waits for them, and re-layouts  465 us (52%)
  waiting for transfers between devices  166 us (19%)
  other arithmetic  127 us (14%)
  matrix products  104 us (12%)
  between operations  14.5 us (2%)
    reshape x5, local copies, waits for them, and re-layouts, expand_mask(): jnp.stack(row_list, axis=1).reshape(4 * group_rows, 4 * group_cols)  127 us
    reduce_scatter x1, waiting for transfers between devices, local(): lax.psum_scatter(jnp.concatenate([gate_sum, up_sum, back_sum], axis=1), '...  104 us
    reshape x9, local copies, waits for them, and re-layouts, expand_mask(): following = jnp.repeat(ordering[(local_row + 1) % 4], 4, axis=1)  95.6 us
    another operation x3, local copies, waits for them, and re-layouts, expand_mask(): jnp.stack(row_list, axis=1).reshape(4 * group_rows, 4 * group_cols)  83.6 us
    or x10, other arithmetic, expand_mask(): row_list.append((current == col_position) | (following == col_position))  61.8 us
    all_gather x1, waiting for transfers between devices, local(): all_local = lax.all_gather(local_grads, 'row', axis=0, tiled=True)  60.4 us
    unnamed x67, local copies, waits for them, and re-layouts  57.4 us
    broadcast_in_dim x9, local copies, waits for them, and re-layouts, expand_mask(): following = jnp.repeat(ordering[(local_row + 1) % 4], 4, axis=1)  45.1 us
  transfers between devices with their start and end apart: 5, of which 2 were waited for; matrix products, arithmetic and copies ran while one was open for 72% of the time, Pallas kernels for 0%

commit v1 on v0

--- a/solution.py
+++ b/solution.py
@@ -1,7 +1,17 @@
+import functools
+
 import jax
 import jax.numpy as jnp
 from jax import lax
+from jax.experimental import pallas as pl
+from jax.experimental.pallas import tpu as pltpu
 from jax.sharding import PartitionSpec as P
+
+BF16 = jnp.bfloat16
+F32 = jnp.float32
+TILE = 256
+PARTS = 4
+VMEM = 52 * 2**20
 
 
 def expand_mask(block_ids):
@@ -39,7 +49,7 @@
     )
 
 
-def local(tokens, out_grad, gate_weight, up_weight, down_weight, gate_mask, up_mask, down_mask):
+def local_any(tokens, out_grad, gate_weight, up_weight, down_weight, gate_mask, up_mask, down_mask):
     gate_keep = expand_mask(gate_mask)
     up_keep = expand_mask(up_mask)
     down_keep = expand_mask(down_mask)
@@ -87,6 +97,412 @@
     return (input_grad, gate_weight_grad, up_weight_grad, down_weight_grad)
 
 
+def _nibble_words():
+    table = []
+    for code in range(24):
+        rest = [0, 1, 2, 3]
+        order = [rest.pop(code // 6), rest.pop(code // 2 % 3), rest.pop(code % 2), rest[0]]
+        table.append([(1 << order[i]) | (1 << order[(i + 1) % 4]) for i in range(4)])
+    words = []
+    for i in range(4):
+        row = []
+        for third in range(3):
+            word = sum(table[8 * third + k][i] << (4 * k) for k in range(8))
+            row.append(word - (1 << 32) if word >= 1 << 31 else word)
+        words.append(row)
+    return words
+
+
+NIBBLES = _nibble_words()
+
+
+def _spread_rows(codes):
+    low, mid = codes < 8, codes < 16
+    shift = (codes & 7) * 4
+    out = []
+    for i in range(4):
+        a, b, c = NIBBLES[i]
+        word = jnp.where(low, jnp.int32(a), jnp.where(mid, jnp.int32(b), jnp.int32(c)))
+        nibble = lax.shift_right_logical(word, shift) & 15
+        out.append((nibble * 0x00204081) & 0x01010101)
+    return out
+
+
+def _interleave(words, lane_perm, row_perm):
+    rows = words[0].shape[0]
+    planes = [
+        jnp.concatenate(
+            [(lax.shift_right_logical(w, jnp.int32(8 * j)) & 255).astype(F32).astype(BF16) for j in range(4)], axis=1
+        )
+        for w in words
+    ]
+    wide = [jnp.dot(p, lane_perm, preferred_element_type=F32).astype(BF16) for p in planes]
+    step = row_perm.shape[0] // 4
+    out = []
+    for at in range(0, rows, step):
+        stacked = jnp.concatenate([w[at : at + step] for w in wide], axis=0)
+        mixed = jnp.dot(row_perm, stacked, preferred_element_type=F32).astype(jnp.int32)
+        out.append(jnp.where(mixed > 127, mixed - 256, mixed).astype(jnp.int8))
+    return out
+
+
+def _pack_rows_kernel(gate_ref, up_ref, lane_ref, row_ref, out_ref):
+    rows = gate_ref.shape[0] // 4
+    words = [None] * 4
+    for s in range(8):
+        ref, q = (gate_ref, s) if s < 4 else (up_ref, s - 4)
+        spread = _spread_rows(ref[q * rows : (q + 1) * rows, :])
+        for i in range(4):
+            part = spread[i] << s if s else spread[i]
+            words[i] = part if words[i] is None else words[i] | part
+    at = 0
+    for block in _interleave(words, lane_ref[...], row_ref[...]):
+        out_ref[at : at + block.shape[0], :] = block
+        at += block.shape[0]
+
+
+def _pack_cols_kernel(groups, codes_ref, lane_ref, row_ref, out_ref):
+    words = [None] * 4
+    for q in range(groups):
+        spread = _spread_rows(codes_ref[:, q * 128 : (q + 1) * 128])
+        for i in range(4):
+            part = spread[i] << q if q else spread[i]
+            words[i] = part if words[i] is None else words[i] | part
+    at = 0
+    for block in _interleave(words, lane_ref[...], row_ref[...]):
+        out_ref[at : at + block.shape[0], :] = block
+        at += block.shape[0]
+
+
+def _permutation(n):
+    source = lax.broadcasted_iota(jnp.int32, (n, n), 0)
+    target = lax.broadcasted_iota(jnp.int32, (n, n), 1)
+    return (source == (target % 4) * (n // 4) + target // 4).astype(BF16)
+
+
+def pack_masks(gate_mask, up_mask, down_mask):
+    lanes = _permutation(512)
+    code_rows, code_cols = gate_mask.shape
+    row_perm = _permutation(128).T
+    gate_up = pl.pallas_call(
+        _pack_rows_kernel,
+        grid=(pl.cdiv(code_cols, 128),),
+        in_specs=[
+            pl.BlockSpec((code_rows, 128), lambda j: (0, j)),
+            pl.BlockSpec((code_rows, 128), lambda j: (0, j)),
+            pl.BlockSpec((512, 512), lambda j: (0, 0)),
+            pl.BlockSpec((128, 128), lambda j: (0, 0)),
+        ],
+        out_specs=pl.BlockSpec((code_rows, 512), lambda j: (0, j)),
+        out_shape=jax.ShapeDtypeStruct((code_rows, 4 * code_cols), jnp.int8),
+        compiler_params=pltpu.CompilerParams(vmem_limit_bytes=VMEM),
+        cost_estimate=pl.CostEstimate(flops=3 * 10**9, bytes_accessed=10**7, transcendentals=0),
+        name="pack_gate_up",
+    )(gate_mask, up_mask, lanes, row_perm)
+    down_rows, down_cols = down_mask.shape
+    block = TILE // 4
+    row_perm = _permutation(TILE).T
+    down = pl.pallas_call(
+        functools.partial(_pack_cols_kernel, down_cols // 128),
+        grid=(down_rows // block,),
+        in_specs=[
+            pl.BlockSpec((block, down_cols), lambda j: (j, 0)),
+            pl.BlockSpec((512, 512), lambda j: (0, 0)),
+            pl.BlockSpec((TILE, TILE), lambda j: (0, 0)),
+        ],
+        out_specs=pl.BlockSpec((TILE, 512), lambda j: (j, 0)),
+        out_shape=jax.ShapeDtypeStruct((4 * down_rows, 512), jnp.int8),
+        compiler_params=pltpu.CompilerParams(vmem_limit_bytes=VMEM),
+        cost_estimate=pl.CostEstimate(flops=2 * 10**9, bytes_accessed=5 * 10**6, transcendentals=0),
+        name="pack_down",
+    )(down_mask, lanes, row_perm)
+    return gate_up, down
+
+
+def _bit(packed, s):
+    scale = -(2.0**-7) if s == 7 else 2.0**-s
+    return (packed & jnp.int8(-128 if s == 7 else 1 << s)).astype(BF16) * BF16(scale)
+
+
+def _rows_keep(packed, first):
+    return jnp.concatenate([_bit(packed, first + q) for q in range(4)], axis=0)
+
+
+def _cols_keep(packed, groups):
+    return jnp.concatenate([_bit(packed, q) for q in range(groups)], axis=1)
+
+
+def _store_sums(at, sums, own_ref, to_x_ref, to_y_ref, mix_ref):
+    quarter = sums.shape[0] // 4
+    half = quarter // 2
+    cut = lambda k, n=1: sums[k * half : (k + n) * half]
+    own_ref[at] = cut(0, 2)
+    to_x_ref[at, :half] = cut(2).astype(BF16)
+    to_x_ref[at, half:] = cut(6).astype(BF16)
+    to_y_ref[at, :half] = cut(5).astype(BF16)
+    to_y_ref[at, half:] = cut(7).astype(BF16)
+    mix_ref[at] = cut(3, 2)
+
+
+def _gate_up_kernel(tok_ref, gate_ref, up_ref, mask_ref, *out_refs):
+    packed = mask_ref[...]
+    tok = tok_ref[...]
+    for at, ref in enumerate((gate_ref, up_ref)):
+        pruned = ref[...] * _rows_keep(packed, 4 * at)
+        _store_sums(at, jnp.dot(tok, pruned, preferred_element_type=F32), *out_refs)
+
+
+def _back_kernel(grad_ref, down_ref, mask_ref, *out_refs):
+    groups = down_ref.shape[1] // 512
+    pruned = down_ref[...] * _cols_keep(mask_ref[...], groups)
+    _store_sums(0, contract_last(grad_ref[...], pruned), *out_refs)
+
+
+def _sum_outs(n, rows, width):
+    quarter = rows // 4
+    spec = pl.BlockSpec((n, quarter, TILE), lambda j: (0, 0, j))
+    shape = lambda t: jax.ShapeDtypeStruct((n, quarter, width), t)
+    return [spec] * 4, [shape(F32), shape(BF16), shape(BF16), shape(F32)]
+
+
+def gate_up_sums(tok, gate_weight, up_weight, gate_up_bits, first, count):
+    rows, depth = tok.shape
+    specs, shapes = _sum_outs(2, rows, count * TILE)
+    return pl.pallas_call(
+        _gate_up_kernel,
+        grid=(count,),
+        in_specs=[
+            pl.BlockSpec((rows, depth), lambda j: (0, 0)),
+            pl.BlockSpec((depth, TILE), lambda j: (0, j + first)),
+            pl.BlockSpec((depth, TILE), lambda j: (0, j + first)),
+            pl.BlockSpec((depth // 4, TILE), lambda j: (0, j + first)),
+        ],
+        out_specs=specs,
+        out_shape=shapes,
+        compiler_params=pltpu.CompilerParams(vmem_limit_bytes=VMEM),
+        cost_estimate=pl.CostEstimate(
+            flops=4 * rows * depth * count * TILE, bytes_accessed=4 * depth * count * TILE, transcendentals=0
+        ),
+        name="gate_up_sums",
+    )(tok, gate_weight, up_weight, gate_up_bits)
+
+
+def back_sums(grads, down_weight, down_bits, first, count):
+    rows, depth = grads.shape
+    specs, shapes = _sum_outs(1, rows, count * TILE)
+    return pl.pallas_call(
+        _back_kernel,
+        grid=(count,),
+        in_specs=[
+            pl.BlockSpec((rows, depth), lambda j: (0, 0)),
+            pl.BlockSpec((TILE, depth), lambda j: (j + first, 0)),
+            pl.BlockSpec((TILE, 512), lambda j: (j + first, 0)),
+        ],
+        out_specs=specs,
+        out_shape=shapes,
+        compiler_params=pltpu.CompilerParams(vmem_limit_bytes=VMEM),
+        cost_estimate=pl.CostEstimate(
+            flops=2 * rows * depth * count * TILE, bytes_accessed=2 * depth * count * TILE, transcendentals=0
+        ),
+        name="back_sums",
+    )(grads, down_weight, down_bits)
+
+
+def _swap(value, bit):
+    return lax.ppermute(value, "row", [(i, i ^ bit) for i in range(4)])
+
+
+def reduce_rows(sums):
+    own, to_x, to_y, mix = sums
+    half = own.shape[1] // 2
+    from_x, from_y = _swap(to_x, 1), _swap(to_y, 2)
+    mixed_x = (mix[:, :half] + from_y[:, half:]).astype(BF16)
+    mixed_y = (mix[:, half:] + from_x[:, half:]).astype(BF16)
+    second_x, second_y = _swap(mixed_x, 1), _swap(mixed_y, 2)
+    first_half = own[:, :half] + from_x[:, :half] + second_y
+    second_half = own[:, half:] + from_y[:, :half] + second_x
+    return jnp.concatenate([first_half, second_half], axis=1)
+
+
+def gather_rows(block):
+    half = block.shape[1] // 2
+    from_x, from_y = _swap(block, 1), _swap(block, 2)
+    diag_a, diag_b = _swap(from_x[:, :half], 2), _swap(from_y[:, half:], 1)
+    return block, from_x, from_y, diag_a, diag_b
+
+
+def swiglu_back(gate_sum, up_sum, back_sum):
+    logistic = jax.nn.sigmoid(gate_sum)
+    swish_val = gate_sum * logistic
+    hidden = swish_val * up_sum
+    up_grad = back_sum * swish_val
+    gate_grad = back_sum * up_sum * logistic * (1.0 + gate_sum * (1.0 - logistic))
+    return jnp.stack([gate_grad, up_grad, hidden]).astype(BF16)
+
+
+def _all_rows(refs, at):
+    return jnp.concatenate([ref[at] for ref in refs], axis=0)
+
+
+def _input_grad_part(block_refs, gate_ref, up_ref, gate_keep, up_keep):
+    return contract_last(_all_rows(block_refs, 0), gate_ref[...] * gate_keep) + contract_last(
+        _all_rows(block_refs, 1), up_ref[...] * up_keep
+    )
+
+
+def _weight_grads(tok_ref, grad_ref, block_refs, gate_keep, up_keep, down_keep, gate_out, up_out, down_out):
+    tok = tok_ref[...]
+    gate_out[...] = contract_first(tok, _all_rows(block_refs, 0)).astype(BF16) * gate_keep
+    up_out[...] = contract_first(tok, _all_rows(block_refs, 1)).astype(BF16) * up_keep
+    down_out[...] = contract_first(_all_rows(block_refs, 2), grad_ref[...]).astype(BF16) * down_keep
+
+
+def _backward_kernel(with_acc, with_input, with_weights, n_alias, *refs):
+    refs = list(refs)
+    block_refs = [refs.pop(0) for _ in range(5)]
+    bits = refs.pop(0)[...]
+    gate_keep, up_keep = _rows_keep(bits, 0), _rows_keep(bits, 4)
+    if with_input:
+        gate_ref, up_ref = refs.pop(0), refs.pop(0)
+        acc_ref = refs.pop(0) if with_acc else None
+    if with_weights:
+        tok_ref, grad_ref, down_bits = refs.pop(0), refs.pop(0), refs.pop(0)
+        down_keep = _cols_keep(down_bits[...], grad_ref.shape[1] // 512)
+        refs = refs[n_alias:]
+    if with_input:
+        sum_ref = refs.pop(0)
+        part = _input_grad_part(block_refs, gate_ref, up_ref, gate_keep, up_keep)
+
+        @pl.when(pl.program_id(0) == 0)
+        def _():
+            sum_ref[...] = part + acc_ref[...] if with_acc else part
+
+        @pl.when(pl.program_id(0) > 0)
+        def _():
+            sum_ref[...] += part
+
+    if with_weights:
+        _weight_grads(tok_ref, grad_ref, block_refs, gate_keep, up_keep, down_keep, *refs)
+
+
+def backward(blocks, gate_up_bits, first, count, inputs=None, weights=None):
+    args, specs, out_specs, shapes, aliases = list(blocks), [], [], [], {}
+    half = blocks[0].shape[1] // 2
+    for block in blocks:
+        specs.append(pl.BlockSpec((3, block.shape[1], TILE), lambda j: (0, 0, j)))
+    rows = 8 * half
+    depth = 4 * gate_up_bits.shape[0]
+    width = gate_up_bits.shape[1]
+    args.append(gate_up_bits)
+    specs.append(pl.BlockSpec((depth // 4, TILE), lambda j: (0, j + first)))
+    column_block = pl.BlockSpec((depth, TILE), lambda j: (0, j + first))
+    whole = pl.BlockSpec((rows, depth), lambda j: (0, 0))
+    flops = moved = 0
+    if inputs is not None:
+        gate_weight, up_weight, acc = inputs
+        args += [gate_weight, up_weight]
+        specs += [column_block, column_block]
+        if acc is not None:
+            args.append(acc)
+            specs.append(whole)
+        out_specs.append(whole)
+        shapes.append(jax.ShapeDtypeStruct((rows, depth), F32))
+        flops += 4 * rows * depth * count * TILE
+        moved += 4 * depth * count * TILE
+    n_alias = 0
+    if weights is not None:
+        tok, grads, down_bits, so_far = weights
+        args += [tok, grads, down_bits]
+        specs += [whole, whole, pl.BlockSpec((TILE, 512), lambda j: (j + first, 0))]
+        if so_far is not None:
+            n_alias = 3
+            for k, value in enumerate(so_far):
+                aliases[len(args)] = len(shapes) + k
+                args.append(value)
+                specs.append(pl.BlockSpec(memory_space=pl.ANY))
+        out_specs += [column_block, column_block, pl.BlockSpec((TILE, depth), lambda j: (j + first, 0))]
+        shapes += [jax.ShapeDtypeStruct((depth, width), BF16)] * 2 + [jax.ShapeDtypeStruct((width, depth), BF16)]
+        flops += 6 * rows * depth * count * TILE
+        moved += 6 * depth * count * TILE
+    return pl.pallas_call(
+        functools.partial(
+            _backward_kernel, inputs is not None and inputs[2] is not None, inputs is not None, weights is not None, n_alias
+        ),
+        grid=(count,),
+        in_specs=specs,
+        out_specs=out_specs,
+        out_shape=shapes,
+        input_output_aliases=aliases,
+        compiler_params=pltpu.CompilerParams(vmem_limit_bytes=VMEM),
+        cost_estimate=pl.CostEstimate(flops=flops, bytes_accessed=moved, transcendentals=0),
+        name="backward",
+    )(*args)
+
+
+def _col_swap(value, bits):
+    return lax.ppermute(value, "col", [(i, i ^ bits) for i in range(8)])
+
+
+def gather_tokens(value, order):
+    mine = jnp.stack([value] + [_col_swap(value, 2 * k) for k in (1, 2, 3)])
+    theirs = _col_swap(mine, 1)
+    groups = []
+    for p in range(4):
+        for part in (mine, theirs):
+            groups.append(lax.dynamic_index_in_dim(part, p ^ order, 0, keepdims=False))
+    return jnp.concatenate(groups, axis=0)
+
+
+def scatter_tokens(partial, order):
+    depth = partial.shape[1]
+    rows = partial.shape[0] // 8
+    split = partial.reshape(4, 2, rows, depth)
+    pair = split[:, 0] + _col_swap(split[:, 1], 1)
+    total = lax.dynamic_index_in_dim(pair, order, 0, keepdims=False)
+    for k in (1, 2, 3):
+        sent = lax.dynamic_index_in_dim(pair, k ^ order, 0, keepdims=False).astype(BF16)
+        total = total + _col_swap(sent, 2 * k)
+    return total.astype(BF16)
+
+
+def local_tiled(tokens, out_grad, gate_weight, up_weight, down_weight, gate_mask, up_mask, down_mask):
+    order = lax.axis_index("row") ^ (lax.axis_index("col") // 2)
+    tok = gather_tokens(tokens, order)
+    gate_up_bits, down_bits = pack_masks(gate_mask, up_mask, down_mask)
+    grads = gather_tokens(out_grad, order)
+    tiles = gate_weight.shape[1] // TILE
+    cuts = [tiles * k // PARTS for k in range(PARTS + 1)]
+    chunks = [(a, b - a) for a, b in zip(cuts[:-1], cuts[1:])]
+    blocks = []
+    gate_up = [reduce_rows(gate_up_sums(tok, gate_weight, up_weight, gate_up_bits, *c)) for c in chunks]
+    back = [reduce_rows(back_sums(grads, down_weight, down_bits, *c)) for c in chunks]
+    for gu, b in zip(gate_up, back):
+        blocks.append(gather_rows(swiglu_back(gu[0], gu[1], b[0])))
+    acc, outs = None, None
+    for k, c in enumerate(chunks):
+        inputs = (gate_weight, up_weight, acc)
+        weights = (tok, grads, down_bits, outs)
+        if k < PARTS - 1:
+            acc, *outs = backward(blocks[k], gate_up_bits, *c, inputs=inputs, weights=weights)
+        else:
+            (acc,) = backward(blocks[k], gate_up_bits, *c, inputs=inputs)
+            outs = backward(blocks[k], gate_up_bits, *c, weights=weights)
+    return (scatter_tokens(acc, order), *outs)
+
+
+def tiled_fits(mesh, depth, width, token_rows):
+    return (
+        mesh.shape["row"] == 4
+        and mesh.shape["col"] == 8
+        and depth % 1280 == 0
+        and depth // 512 <= 7
+        and depth % 512 == 0
+        and width % TILE == 0
+        and width // TILE >= PARTS
+        and token_rows % 256 == 0
+    )
+
+
 def solution(mesh):
     in_specs = (
         P("col", "row"),
@@ -99,4 +515,12 @@
         P("col", "row"),
     )
     out_specs = (P("col", "row"), P("row", "col"), P("row", "col"), P("col", "row"))
-    return jax.shard_map(local, mesh=mesh, in_specs=in_specs, out_specs=out_specs, check_vma=False)
+
+    def run(tokens, out_grad, gate_weight, *rest):
+        depth = gate_weight.shape[0] // mesh.shape["row"]
+        width = gate_weight.shape[1] // mesh.shape["col"]
+        body = local_tiled if tiled_fits(mesh, depth, width, tokens.shape[0]) else local_any
+        mapped = jax.shard_map(body, mesh=mesh, in_specs=in_specs, out_specs=out_specs, check_vma=False)
+        return mapped(tokens, out_grad, gate_weight, *rest)
+
+    return run

time: 893 us -> 261 us (0.29); the launches traced: 877 us -> 260 us
  local copies, waits for them, and re-layouts: 465 us -> 9.76 us
  Pallas kernels: 0 us -> 128 us
  other arithmetic: 127 us -> 2.99 us
  waiting for transfers between devices: 166 us -> 60.7 us
  matrix products: 104 us -> 0 us
  starting transfers between devices: 0.2 us -> 56.5 us
  between operations: 14.5 us -> 1.34 us
    reshape x17 -> x0, local copies, waits for them, and re-layouts: 255 us -> none  [the longest x5 127 us: expand_mask(): jnp.stack(row_list, axis=1).reshape(4 * group_rows, 4 * group_cols)]
    pallas_call x0 -> x15, Pallas kernels: none -> 128 us  [the longest x5 58.4 us: backward(): pl.pallas_call(functools.partial(_backward_kernel, inputs is not None and...]
    reduce_scatter x2 -> x0, waiting for transfers between devices: 104 us -> none  [the longest x1 104 us: local(): lax.psum_scatter(jnp.concatenate([gate_sum, up_sum, back_sum], axis=1), '...]
    dot_general x8 -> x0, matrix products: 104 us -> none  [the longest x3 41.8 us: contract_last(): lax.dot_general(left, right, (((1,), (1,)), ((), ())), preferred_element_...]
    another operation x3 -> x0, local copies, waits for them, and re-layouts: 83.6 us -> none  [expand_mask(): jnp.stack(row_list, axis=1).reshape(4 * group_rows, 4 * group_cols)]
    or x10 -> x0, other arithmetic: 61.8 us -> none  [expand_mask(): row_list.append((current == col_position) | (following == col_position))]
    ppermute x0 -> x60, waiting for transfers between devices: none -> 60.7 us  [the longest x48 45.9 us: _swap(): return lax.ppermute(value, 'row', [(i, i ^ bit) for i in range(4)])]
    all_gather x3 -> x0, waiting for transfers between devices: 60.4 us -> none  [the longest x1 60.4 us: local(): all_local = lax.all_gather(local_grads, 'row', axis=0, tiled=True)]
  transfers between devices with their start and end apart: 5 -> 60, of which waited for: 2 -> 26; matrix products, arithmetic and copies ran while one was open for 72% -> 3% of each run, Pallas kernels for 0% -> 32%
where the time goes in v1:
time: 261 us; the launch traced here: 260 us
  Pallas kernels  128 us (49%)
  waiting for transfers between devices  60.7 us (23%)
  starting transfers between devices  56.5 us (22%)
  local copies, waits for them, and re-layouts  9.76 us (4%)
  other arithmetic  2.99 us (1%)
    pallas_call x5, Pallas kernels, backward(): pl.pallas_call(functools.partial(_backward_kernel, inputs is not None and...  58.4 us
    ppermute x48, waiting for transfers between devices, _swap(): return lax.ppermute(value, 'row', [(i, i ^ bit) for i in range(4)])  45.9 us
    ppermute x48, starting transfers between devices, _swap(): return lax.ppermute(value, 'row', [(i, i ^ bit) for i in range(4)])  41.8 us
    pallas_call x4, Pallas kernels, gate_up_sums(): pl.pallas_call(_gate_up_kernel, grid=(count,), in_specs=[pl.BlockSpec((ro...  26 us
    pallas_call x4, Pallas kernels, back_sums(): pl.pallas_call(_back_kernel, grid=(count,), in_specs=[pl.BlockSpec((rows,...  17.4 us
    ppermute x12, waiting for transfers between devices, _col_swap(): return lax.ppermute(value, 'col', [(i, i ^ bits) for i in range(8)])  14.8 us
    ppermute x12, starting transfers between devices, _col_swap(): return lax.ppermute(value, 'col', [(i, i ^ bits) for i in range(8)])  14.7 us
    pallas_call x1, Pallas kernels, pack_masks(): pl.pallas_call(_pack_rows_kernel, grid=(pl.cdiv(code_cols, 128),), in_spe...  13.4 us
  transfers between devices with their start and end apart: 60, of which 26 were waited for; matrix products, arithmetic and copies ran while one was open for 3% of the time, Pallas kernels for 32%

profile of v1, /device:TPU:0, one launch (start us, length us, event | category | flops | bytes accessed | tf_op | source)
XLA Modules:
  0.0 259.7 jit_solution(3359108256740773834)
XLA Ops:
  6.8 3.9 %collective-permute-start.10 = (bf16[32,2560]{1,0:T(8,128)(2,1)}, bf16[32,2560]{1,0:T(8,128)(2,1)S(1)}, u32[]{:S(2)}, u32[]{:S(2)}) collective-permute-start(bf16[32,2560]{1,0:T(8,128)(2,1)} %param.8), channel_id=1, source_target_pairs={{0,6},{1,7},{2,4},{3,5},{4,2},{5,3},{6,0},{7,1},{8,14},{9,15},{10,... | collective-permute-start | bytes 491528 | tf_op jit(solution)/shard_map/ppermute | solution.py:443
  10.8 3.3 %copy.21.gate_ref = s32[640,832]{1,0:T(8,128)} copy(s32[640,832]{0,1:T(8,128)} %param.13) | data formatting | bytes 4259840 | tf_op args[5]
  16.4 13.4 %pack_gate_up.1.mask_ref.refs_5_ = s8[640,3328]{1,0:T(32,128)(4,1)} custom-call(s32[640,832]{1,0:T(8,128)} %copy.21.gate_ref, s32[640,832]{1,0:T(8,128)} %copy.22.up_ref, bf16[512,512]{1,0:T(8,128)(2,1)S(1)} %fusion.1.lane_ref, bf16[128,128]{1,0:T(8,128)(2,1)S(1)} %fusion.17.row_ref), custom_call_target="tpu_custom_call" | custom-call | flops 3000000000 | bytes 10000000 | tf_op jit(solution)/shard_map/pack_gate_up/pallas_call | solution.py:187
  30.1 13.1 %pack_down.1.mask_ref.refs_10_.refs_11_.refs_8_ = s8[3328,512]{1,0:T(32,128)(4,1)} custom-call(s32[832,640]{1,0:T(8,128)} %codes_ref.1, bf16[512,512]{1,0:T(8,128)(2,1)S(1)} %fusion.1.lane_ref, bf16[256,256]{1,0:T(8,128)(2,1)S(1)} %fusion.7.row_ref), custom_call_target="tpu_custom_call" | custom-call | flops 2000000000 | bytes 5000000 | tf_op jit(solution)/shard_map/pack_down/pallas_call | solution.py:205
  43.4 7.0 %collective-permute-done.2 = bf16[32,2560]{1,0:T(8,128)(2,1)S(1)} collective-permute-done((bf16[32,2560]{1,0:T(8,128)(2,1)S(1)}, bf16[32,2560]{1,0:T(8,128)(2,1)S(1)}, u32[]{:S(2)}, u32[]{:S(2)}) %collective-permute-start.2) | collective-permute-done | bytes 163872 | tf_op jit(solution)/shard_map/ppermute | solution.py:443
  54.0 6.2 %gate_up_sums.7 = (f32[2,64,768]{2,1,0:T(8,128)S(1)}, bf16[2,64,768]{2,1,0:T(8,128)(2,1)S(1)}, bf16[2,64,768]{2,1,0:T(8,128)(2,1)S(1)}, f32[2,64,768]{2,1,0:T(8,128)S(1)}) custom-call(bf16[256,2560]{1,0:T(8,128)(2,1)} %copy-done.2, bf16[2560,3328]{1,0:T(8,128)(2,1)} %refs_6_.7, bf16[2560,3328]{1,0:T(8,128)(2,1)} %refs_7_.7, ...), custom_call_target="tpu_custom_call" | custom-call | flops 2013265920 | bytes 7864320 | tf_op jit(solution)/shard_map/gate_up_sums/pallas_call | solution.py:271
  60.1 6.3 %gate_up_sums.6 = (f32[2,64,768]{2,1,0:T(8,128)S(1)}, bf16[2,64,768]{2,1,0:T(8,128)(2,1)S(1)}, bf16[2,64,768]{2,1,0:T(8,128)(2,1)S(1)}, f32[2,64,768]{2,1,0:T(8,128)S(1)}) custom-call(bf16[256,2560]{1,0:T(8,128)(2,1)} %copy-done.2, bf16[2560,3328]{1,0:T(8,128)(2,1)} %refs_6_.7, bf16[2560,3328]{1,0:T(8,128)(2,1)} %refs_7_.7, ...), custom_call_target="tpu_custom_call" | custom-call | flops 2013265920 | bytes 7864320 | tf_op jit(solution)/shard_map/gate_up_sums/pallas_call | solution.py:271
  66.4 6.3 %gate_up_sums.5 = (f32[2,64,768]{2,1,0:T(8,128)S(1)}, bf16[2,64,768]{2,1,0:T(8,128)(2,1)S(1)}, bf16[2,64,768]{2,1,0:T(8,128)(2,1)S(1)}, f32[2,64,768]{2,1,0:T(8,128)S(1)}) custom-call(bf16[256,2560]{1,0:T(8,128)(2,1)} %copy-done.2, bf16[2560,3328]{1,0:T(8,128)(2,1)} %refs_6_.7, bf16[2560,3328]{1,0:T(8,128)(2,1)} %refs_7_.7, ...), custom_call_target="tpu_custom_call" | custom-call | flops 2013265920 | bytes 7864320 | tf_op jit(solution)/shard_map/gate_up_sums/pallas_call | solution.py:271
  72.7 7.4 %gate_up_sums.4 = (f32[2,64,1024]{2,1,0:T(8,128)S(1)}, bf16[2,64,1024]{2,1,0:T(8,128)(2,1)S(1)}, bf16[2,64,1024]{2,1,0:T(8,128)(2,1)S(1)}, f32[2,64,1024]{2,1,0:T(8,128)S(1)}) custom-call(bf16[256,2560]{1,0:T(8,128)(2,1)} %copy-done.2, bf16[2560,3328]{1,0:T(8,128)(2,1)} %refs_6_.7, bf16[2560,3328]{1,0:T(8,128)(2,1)} %refs_7_.7, ...), custom_call_target="tpu_custom_call" | custom-call | flops 2684354560 | bytes 10485760 | tf_op jit(solution)/shard_map/gate_up_sums/pallas_call | solution.py:271
  80.2 4.3 %back_sums.7 = (f32[1,64,768]{2,1,0:T(8,128)S(1)}, bf16[1,64,768]{2,1,0:T(8,128)(2,1)S(1)}, bf16[1,64,768]{2,1,0:T(8,128)(2,1)S(1)}, f32[1,64,768]{2,1,0:T(8,128)S(1)}) custom-call(bf16[256,2560]{1,0:T(8,128)(2,1)S(1)} %bitcast_dynamic-update-slice_fusion.8.grad_ref.refs_9_.refs_10_.refs_7_, bf16[3328,2560]{1,0:T(8,128)(2,1)} %down_ref.7, ...), custom_call_target="tpu_custom_call" | custom-call | flops 1006632960 | bytes 3932160 | tf_op jit(solution)/shard_map/back_sums/pallas_call | solution.py:293
  84.5 5.4 %back_sums.4 = (f32[1,64,1024]{2,1,0:T(8,128)S(1)}, bf16[1,64,1024]{2,1,0:T(8,128)(2,1)S(1)}, bf16[1,64,1024]{2,1,0:T(8,128)(2,1)S(1)}, f32[1,64,1024]{2,1,0:T(8,128)S(1)}) custom-call(bf16[256,2560]{1,0:T(8,128)(2,1)} %copy-done, bf16[3328,2560]{1,0:T(8,128)(2,1)} %down_ref.7, s8[3328,512]{1,0:T(32,128)(4,1)} %pack_down.1.mask_ref.refs_10_.refs_11_.refs_8_), custom_call_target="tpu_custom_call" | custom-call | flops 1342177280 | bytes 5242880 | tf_op jit(solution)/shard_map/back_sums/pallas_call | solution.py:293
  94.3 3.8 %back_sums.6 = (f32[1,64,768]{2,1,0:T(8,128)S(1)}, bf16[1,64,768]{2,1,0:T(8,128)(2,1)S(1)}, bf16[1,64,768]{2,1,0:T(8,128)(2,1)S(1)}, f32[1,64,768]{2,1,0:T(8,128)S(1)}) custom-call(bf16[256,2560]{1,0:T(8,128)(2,1)S(1)} %copy-done.1, bf16[3328,2560]{1,0:T(8,128)(2,1)} %down_ref.7, s8[3328,512]{1,0:T(32,128)(4,1)} %pack_down.1.mask_ref.refs_10_.refs_11_.refs_8_), custom_call_target="tpu_custom_call" | custom-call | flops 1006632960 | bytes 3932160 | tf_op jit(solution)/shard_map/back_sums/pallas_call | solution.py:293
  100.7 4.0 %back_sums.5 = (f32[1,64,768]{2,1,0:T(8,128)S(1)}, bf16[1,64,768]{2,1,0:T(8,128)(2,1)S(1)}, bf16[1,64,768]{2,1,0:T(8,128)(2,1)S(1)}, f32[1,64,768]{2,1,0:T(8,128)S(1)}) custom-call(bf16[256,2560]{1,0:T(8,128)(2,1)S(1)} %copy-done.1, bf16[3328,2560]{1,0:T(8,128)(2,1)} %down_ref.7, s8[3328,512]{1,0:T(32,128)(4,1)} %pack_down.1.mask_ref.refs_10_.refs_11_.refs_8_), custom_call_target="tpu_custom_call" | custom-call | flops 1006632960 | bytes 3932160 | tf_op jit(solution)/shard_map/back_sums/pallas_call | solution.py:293
  106.9 4.0 %collective-permute-done.32 = bf16[1,64,768]{2,1,0:T(8,128)(2,1)S(1)} collective-permute-done((bf16[1,64,768]{2,1,0:T(8,128)(2,1)S(1)}, bf16[1,64,768]{2,1,0:T(8,128)(2,1)S(1)}, u32[]{:S(2)}, u32[]{:S(2)}) %collective-permute-start.32) | collective-permute-done | bytes 98336 | tf_op jit(solution)/shard_map/ppermute | solution.py:312
  111.9 3.6 %collective-permute-done.20 = bf16[1,64,768]{2,1,0:T(8,128)(2,1)S(1)} collective-permute-done((bf16[1,64,768]{2,1,0:T(8,128)(2,1)S(1)}, bf16[1,64,768]{2,1,0:T(8,128)(2,1)S(1)}, u32[]{:S(2)}, u32[]{:S(2)}) %collective-permute-start.20) | collective-permute-done | bytes 98336 | tf_op jit(solution)/shard_map/ppermute | solution.py:312
  116.7 4.2 %collective-permute-done.4 = bf16[1,64,1024]{2,1,0:T(8,128)(2,1)S(1)} collective-permute-done((bf16[1,64,1024]{2,1,0:T(8,128)(2,1)S(1)}, bf16[1,64,1024]{2,1,0:T(8,128)(2,1)S(1)}, u32[]{:S(2)}, u32[]{:S(2)}) %collective-permute-start.4) | collective-permute-done | bytes 131104 | tf_op jit(solution)/shard_map/ppermute | solution.py:312
  144.8 6.8 %collective-permute-done.5 = bf16[1,32,1024]{2,1,0:T(8,128)(2,1)S(1)} collective-permute-done((bf16[1,32,1024]{2,1,0:T(8,128)(2,1)S(1)}, bf16[1,32,1024]{2,1,0:T(8,128)(2,1)S(1)}, u32[]{:S(2)}, u32[]{:S(2)}) %collective-permute-start.5) | collective-permute-done | bytes 65568 | tf_op jit(solution)/shard_map/ppermute | solution.py:312
  165.9 5.0 %collective-permute-done.52.refs_1_ = bf16[3,64,768]{2,1,0:T(8,128)(2,1)S(1)} collective-permute-done((bf16[3,64,768]{2,1,0:T(8,128)(2,1)S(1)}, bf16[3,64,768]{2,1,0:T(8,128)(2,1)S(1)}, u32[]{:S(2)}, u32[]{:S(2)}) %collective-permute-start.52) | collective-permute-done | bytes 294944 | tf_op jit(solution)/shard_map/ppermute | solution.py:312
  185.2 12.6 %backward.5 = (f32[256,2560]{1,0:T(8,128)}, bf16[2560,3328]{1,0:T(8,128)(2,1)}, bf16[2560,3328]{1,0:T(8,128)(2,1)}, bf16[3328,2560]{1,0:T(8,128)(2,1)}) custom-call(bf16[3,64,768]{2,1,0:T(8,128)(2,1)S(1)} %pad_maximum_fusion.5.refs_0_, bf16[3,64,768]{2,1,0:T(8,128)(2,1)S(1)} %collective-permute-done.52.refs_1_, ...), custom_call_target="tpu_custom_call" | custom-call | flops 5033164800 | bytes 19660800 | tf_op jit(solution)/shard_map/backward/pallas_call | solution.py:427
  199.0 13.5 %backward.6 = (f32[256,2560]{1,0:T(8,128)}, bf16[2560,3328]{1,0:T(8,128)(2,1)}, bf16[2560,3328]{1,0:T(8,128)(2,1)}, bf16[3328,2560]{1,0:T(8,128)(2,1)}) custom-call(bf16[3,64,768]{2,1,0:T(8,128)(2,1)S(1)} %pad_maximum_fusion.4.refs_0_, ...), custom_call_target="tpu_custom_call", output_to_operand_aliasing={{1}: (12, {}), {2}: (13, {}), {3}: (14, {})} | custom-call | flops 5033164800 | bytes 19660800 | tf_op jit(solution)/shard_map/backward/pallas_call | solution.py:427
  214.5 13.7 %backward.7 = (f32[256,2560]{1,0:T(8,128)}, bf16[2560,3328]{1,0:T(8,128)(2,1)}, bf16[2560,3328]{1,0:T(8,128)(2,1)}, bf16[3328,2560]{1,0:T(8,128)(2,1)}) custom-call(bf16[3,64,768]{2,1,0:T(8,128)(2,1)S(1)} %pad_maximum_fusion.3.refs_0_, ...), custom_call_target="tpu_custom_call", output_to_operand_aliasing={{1}: (12, {}), {2}: (13, {}), {3}: (14, {})} | custom-call | flops 5033164800 | bytes 19660800 | tf_op jit(solution)/shard_map/backward/pallas_call | solution.py:427
  228.2 9.8 %backward.8 = f32[256,2560]{1,0:T(8,128)} custom-call(bf16[3,64,1024]{2,1,0:T(8,128)(2,1)S(1)} %pad_maximum_fusion.2.refs_0_, bf16[3,64,1024]{2,1,0:T(8,128)(2,1)S(1)} %collective-permute-done.16.refs_1_, bf16[3,64,1024]{2,1,0:T(8,128)(2,1)S(1)} %collective-permute-done.17.refs_2_, bf16[3,32,1024]{2,1,0:T(8,128)(2,1)S(1)} %collective-permute-done.18.refs_3_, ...), custom_call_target="tpu_custom_call" | custom-call | flops 2684354560 | bytes 10485760 | tf_op jit(solution)/shard_map/backward/pallas_call | solution.py:427
  244.2 3.2 %collective-permute-start.59 = (bf16[32,2560]{1,0:T(8,128)(2,1)S(1)}, bf16[32,2560]{1,0:T(8,128)(2,1)S(1)}, u32[]{:S(2)}, u32[]{:S(2)}) collective-permute-start(bf16[32,2560]{1,0:T(8,128)(2,1)S(1)} %get-tuple-element.99), channel_id=1, source_target_pairs={{0,6},{1,7},{2,4},{3,5},{4,2},{5,3},{6,0},{7,1},{8,14},{9,15},{10,... | collective-permute-start | bytes 491528 | tf_op jit(solution)/shard_map/ppermute | solution.py:443
  247.4 8.9 %backward.9 = (bf16[2560,3328]{1,0:T(8,128)(2,1)}, bf16[2560,3328]{1,0:T(8,128)(2,1)}, bf16[3328,2560]{1,0:T(8,128)(2,1)}) custom-call(bf16[3,64,1024]{2,1,0:T(8,128)(2,1)S(1)} %pad_maximum_fusion.2.refs_0_, bf16[3,64,1024]{2,1,0:T(8,128)(2,1)S(1)} %collective-permute-done.16.refs_1_, ...), custom_call_target="tpu_custom_call", output_to_operand_aliasing={{0}: (9, {}), {1}: (10, {}), {2}: (11, {})} | custom-call | flops 4026531840 | bytes 15728640 | tf_op jit(solution)/shard_map/backward/pallas_call | solution.py:427
  (192 shorter events, 89.0 us)
Async XLA Ops:
  0.6 42.7 %collective-permute-start = (bf16[32,2560]{1,0:T(8,128)(2,1)}, bf16[32,2560]{1,0:T(8,128)(2,1)S(1)}, u32[]{:S(2)}, u32[]{:S(2)}) collective-permute-start(bf16[32,2560]{1,0:T(8,128)(2,1)} %param.9), channel_id=1, source_target_pairs={{0,2},{1,3},{2,0},{3,1},{4,6},{5,7},{6,4},{7,5},{8,10},{9,11},{10,... | collective-permute-start | bytes 491528 | tf_op jit(solution)/shard_map/ppermute | solution.py:443
  3.7 39.7 %collective-permute-start.1 = (bf16[32,2560]{1,0:T(8,128)(2,1)}, bf16[32,2560]{1,0:T(8,128)(2,1)S(1)}, u32[]{:S(2)}, u32[]{:S(2)}) collective-permute-start(bf16[32,2560]{1,0:T(8,128)(2,1)} %param.9), channel_id=1, source_target_pairs={{0,4},{1,5},{2,6},{3,7},{4,0},{5,1},{6,2},{7,3},{8,12},{9,13},{10,... | collective-permute-start | bytes 491528 | tf_op jit(solution)/shard_map/ppermute | solution.py:443
  6.3 36.8 %collective-permute-start.8 = (bf16[32,2560]{1,0:T(8,128)(2,1)}, bf16[32,2560]{1,0:T(8,128)(2,1)S(1)}, u32[]{:S(2)}, u32[]{:S(2)}) collective-permute-start(bf16[32,2560]{1,0:T(8,128)(2,1)} %param.8), channel_id=1, source_target_pairs={{0,2},{1,3},{2,0},{3,1},{4,6},{5,7},{6,4},{7,5},{8,10},{9,11},{10,... | collective-permute-start | bytes 491528 | tf_op jit(solution)/shard_map/ppermute | solution.py:443
  6.8 36.4 %collective-permute-start.9 = (bf16[32,2560]{1,0:T(8,128)(2,1)}, bf16[32,2560]{1,0:T(8,128)(2,1)S(1)}, u32[]{:S(2)}, u32[]{:S(2)}) collective-permute-start(bf16[32,2560]{1,0:T(8,128)(2,1)} %param.8), channel_id=1, source_target_pairs={{0,4},{1,5},{2,6},{3,7},{4,0},{5,1},{6,2},{7,3},{8,12},{9,13},{10,... | collective-permute-start | bytes 491528 | tf_op jit(solution)/shard_map/ppermute | solution.py:443
  6.8 36.4 %collective-permute-start.10 = (bf16[32,2560]{1,0:T(8,128)(2,1)}, bf16[32,2560]{1,0:T(8,128)(2,1)S(1)}, u32[]{:S(2)}, u32[]{:S(2)}) collective-permute-start(bf16[32,2560]{1,0:T(8,128)(2,1)} %param.8), channel_id=1, source_target_pairs={{0,6},{1,7},{2,4},{3,5},{4,2},{5,3},{6,0},{7,1},{8,14},{9,15},{10,... | collective-permute-start | bytes 491528 | tf_op jit(solution)/shard_map/ppermute | solution.py:443
  89.9 14.8 %collective-permute-start.44 = (bf16[1,64,768]{2,1,0:T(8,128)(2,1)S(1)}, bf16[1,64,768]{2,1,0:T(8,128)(2,1)S(1)}, u32[]{:S(2)}, u32[]{:S(2)}) collective-permute-start(bf16[1,64,768]{2,1,0:T(8,128)(2,1)S(1)} %get-tuple-element.76), channel_id=1, source_target_pairs={{0,8},{8,0},{16,24},{24,16},{1,9},{9,1},{17,25},{25,17},{2,10},{10... | collective-permute-start | bytes 294920 | tf_op jit(solution)/shard_map/ppermute | solution.py:312
  91.5 13.8 %collective-permute-start.46 = (bf16[1,64,768]{2,1,0:T(8,128)(2,1)S(1)}, bf16[1,64,768]{2,1,0:T(8,128)(2,1)S(1)}, u32[]{:S(2)}, u32[]{:S(2)}) collective-permute-start(bf16[1,64,768]{2,1,0:T(8,128)(2,1)S(1)} %get-tuple-element.78), channel_id=1, source_target_pairs={{0,16},{8,24},{16,0},{24,8},{1,17},{9,25},{17,1},{25,9},{2,18},{10... | collective-permute-start | bytes 294920 | tf_op jit(solution)/shard_map/ppermute | solution.py:312
  98.1 37.7 %collective-permute-start.48 = (bf16[2,64,768]{2,1,0:T(8,128)(2,1)S(1)}, bf16[2,64,768]{2,1,0:T(8,128)(2,1)S(1)}, u32[]{:S(2)}, u32[]{:S(2)}) collective-permute-start(bf16[2,64,768]{2,1,0:T(8,128)(2,1)S(1)} %get-tuple-element.80), channel_id=1, source_target_pairs={{0,8},{8,0},{16,24},{24,16},{1,9},{9,1},{17,25},{25,17},{2,10},{10... | collective-permute-start | bytes 589832 | tf_op jit(solution)/shard_map/ppermute | solution.py:312
  98.7 37.8 %collective-permute-start.50 = (bf16[2,64,768]{2,1,0:T(8,128)(2,1)S(1)}, bf16[2,64,768]{2,1,0:T(8,128)(2,1)S(1)}, u32[]{:S(2)}, u32[]{:S(2)}) collective-permute-start(bf16[2,64,768]{2,1,0:T(8,128)(2,1)S(1)} %get-tuple-element.82), channel_id=1, source_target_pairs={{0,16},{8,24},{16,0},{24,8},{1,17},{9,25},{17,1},{25,9},{2,18},{10... | collective-permute-start | bytes 589832 | tf_op jit(solution)/shard_map/ppermute | solution.py:312
  99.2 39.3 %collective-permute-start.36 = (bf16[2,64,768]{2,1,0:T(8,128)(2,1)S(1)}, bf16[2,64,768]{2,1,0:T(8,128)(2,1)S(1)}, u32[]{:S(2)}, u32[]{:S(2)}) collective-permute-start(bf16[2,64,768]{2,1,0:T(8,128)(2,1)S(1)} %get-tuple-element.72), channel_id=1, source_target_pairs={{0,8},{8,0},{16,24},{24,16},{1,9},{9,1},{17,25},{25,17},{2,10},{10... | collective-permute-start | bytes 589832 | tf_op jit(solution)/shard_map/ppermute | solution.py:312
  136.5 15.9 %collective-permute-start.12 = (bf16[2,64,1024]{2,1,0:T(8,128)(2,1)S(1)}, bf16[2,64,1024]{2,1,0:T(8,128)(2,1)S(1)}, u32[]{:S(2)}, u32[]{:S(2)}) collective-permute-start(bf16[2,64,1024]{2,1,0:T(8,128)(2,1)S(1)} %get-tuple-element.56), channel_id=1, source_target_pairs={{0,8},{8,0},{16,24},{24,16},{1,9},{9,1},{17,25},{25,17},{2,10},{10... | collective-permute-start | bytes 786440 | tf_op jit(solution)/shard_map/ppermute | solution.py:312
  138.5 15.3 %collective-permute-start.14 = (bf16[2,64,1024]{2,1,0:T(8,128)(2,1)S(1)}, bf16[2,64,1024]{2,1,0:T(8,128)(2,1)S(1)}, u32[]{:S(2)}, u32[]{:S(2)}) collective-permute-start(bf16[2,64,1024]{2,1,0:T(8,128)(2,1)S(1)} %get-tuple-element.58), channel_id=1, source_target_pairs={{0,16},{8,24},{16,0},{24,8},{1,17},{9,25},{17,1},{25,9},{2,18},{10... | collective-permute-start | bytes 786440 | tf_op jit(solution)/shard_map/ppermute | solution.py:312
  162.1 13.8 %collective-permute-start.40 = (bf16[3,64,768]{2,1,0:T(8,128)(2,1)S(1)}, bf16[3,64,768]{2,1,0:T(8,128)(2,1)S(1)}, u32[]{:S(2)}, u32[]{:S(2)}) collective-permute-start(bf16[3,64,768]{2,1,0:T(8,128)(2,1)S(1)} %pad_maximum_fusion.4.refs_0_), channel_id=1, source_target_pairs={{0,8},{8,0},{16,24},{24,16},{1,9},{9,1},{17,25},{25,17},{2,10},{10... | collective-permute-start | bytes 884744 | tf_op jit(solution)/shard_map/ppermute | solution.py:312
  164.5 14.5 %collective-permute-start.28 = (bf16[3,64,768]{2,1,0:T(8,128)(2,1)S(1)}, bf16[3,64,768]{2,1,0:T(8,128)(2,1)S(1)}, u32[]{:S(2)}, u32[]{:S(2)}) collective-permute-start(bf16[3,64,768]{2,1,0:T(8,128)(2,1)S(1)} %pad_maximum_fusion.3.refs_0_), channel_id=1, source_target_pairs={{0,8},{8,0},{16,24},{24,16},{1,9},{9,1},{17,25},{25,17},{2,10},{10... | collective-permute-start | bytes 884744 | tf_op jit(solution)/shard_map/ppermute | solution.py:312
  177.5 35.0 %collective-permute-start.16 = (bf16[3,64,1024]{2,1,0:T(8,128)(2,1)S(1)}, bf16[3,64,1024]{2,1,0:T(8,128)(2,1)S(1)}, u32[]{:S(2)}, u32[]{:S(2)}) collective-permute-start(bf16[3,64,1024]{2,1,0:T(8,128)(2,1)S(1)} %pad_maximum_fusion.2.refs_0_), channel_id=1, source_target_pairs={{0,8},{8,0},{16,24},{24,16},{1,9},{9,1},{17,25},{25,17},{2,10},{10... | collective-permute-start | bytes 1179656 | tf_op jit(solution)/shard_map/ppermute | solution.py:312
  179.0 35.1 %collective-permute-start.17 = (bf16[3,64,1024]{2,1,0:T(8,128)(2,1)S(1)}, bf16[3,64,1024]{2,1,0:T(8,128)(2,1)S(1)}, u32[]{:S(2)}, u32[]{:S(2)}) collective-permute-start(bf16[3,64,1024]{2,1,0:T(8,128)(2,1)S(1)} %pad_maximum_fusion.2.refs_0_), channel_id=1, source_target_pairs={{0,16},{8,24},{16,0},{24,8},{1,17},{9,25},{17,1},{25,9},{2,18},{10... | collective-permute-start | bytes 1179656 | tf_op jit(solution)/shard_map/ppermute | solution.py:312
  182.2 15.7 %collective-permute-start.42 = (bf16[3,32,768]{2,1,0:T(8,128)(2,1)S(1)}, bf16[3,32,768]{2,1,0:T(8,128)(2,1)S(1)}, u32[]{:S(2)}, u32[]{:S(2)}) collective-permute-start(bf16[3,32,768]{2,1,0:T(8,128)(2,1)S(1)} %slice.362), channel_id=1, source_target_pairs={{0,16},{8,24},{16,0},{24,8},{1,17},{9,25},{17,1},{25,9},{2,18},{10... | collective-permute-start | bytes 442376 | tf_op jit(solution)/shard_map/ppermute | solution.py:312
  183.8 15.3 %collective-permute-start.43 = (bf16[3,32,768]{2,1,0:T(8,128)(2,1)S(1)}, bf16[3,32,768]{2,1,0:T(8,128)(2,1)S(1)}, u32[]{:S(2)}, u32[]{:S(2)}) collective-permute-start(bf16[3,32,768]{2,1,0:T(8,128)(2,1)S(1)} %slice.363), channel_id=1, source_target_pairs={{0,8},{8,0},{16,24},{24,16},{1,9},{9,1},{17,25},{25,17},{2,10},{10... | collective-permute-start | bytes 442376 | tf_op jit(solution)/shard_map/ppermute | solution.py:312
  184.1 30.4 %collective-permute-start.30 = (bf16[3,32,768]{2,1,0:T(8,128)(2,1)S(1)}, bf16[3,32,768]{2,1,0:T(8,128)(2,1)S(1)}, u32[]{:S(2)}, u32[]{:S(2)}) collective-permute-start(bf16[3,32,768]{2,1,0:T(8,128)(2,1)S(1)} %slice.350), channel_id=1, source_target_pairs={{0,16},{8,24},{16,0},{24,8},{1,17},{9,25},{17,1},{25,9},{2,18},{10... | collective-permute-start | bytes 442376 | tf_op jit(solution)/shard_map/ppermute | solution.py:312
  197.9 16.6 %collective-permute-start.31 = (bf16[3,32,768]{2,1,0:T(8,128)(2,1)S(1)}, bf16[3,32,768]{2,1,0:T(8,128)(2,1)S(1)}, u32[]{:S(2)}, u32[]{:S(2)}) collective-permute-start(bf16[3,32,768]{2,1,0:T(8,128)(2,1)S(1)} %slice.351), channel_id=1, source_target_pairs={{0,8},{8,0},{16,24},{24,16},{1,9},{9,1},{17,25},{25,17},{2,10},{10... | collective-permute-start | bytes 442376 | tf_op jit(solution)/shard_map/ppermute | solution.py:312
  212.5 15.7 %collective-permute-start.18 = (bf16[3,32,1024]{2,1,0:T(8,128)(2,1)S(1)}, bf16[3,32,1024]{2,1,0:T(8,128)(2,1)S(1)}, u32[]{:S(2)}, u32[]{:S(2)}) collective-permute-start(bf16[3,32,1024]{2,1,0:T(8,128)(2,1)S(1)} %slice.338), channel_id=1, source_target_pairs={{0,16},{8,24},{16,0},{24,8},{1,17},{9,25},{17,1},{25,9},{2,18},{10... | collective-permute-start | bytes 589832 | tf_op jit(solution)/shard_map/ppermute | solution.py:312
  214.1 14.1 %collective-permute-start.19 = (bf16[3,32,1024]{2,1,0:T(8,128)(2,1)S(1)}, bf16[3,32,1024]{2,1,0:T(8,128)(2,1)S(1)}, u32[]{:S(2)}, u32[]{:S(2)}) collective-permute-start(bf16[3,32,1024]{2,1,0:T(8,128)(2,1)S(1)} %slice.339), channel_id=1, source_target_pairs={{0,8},{8,0},{16,24},{24,16},{1,9},{9,1},{17,25},{25,17},{2,10},{10... | collective-permute-start | bytes 589832 | tf_op jit(solution)/shard_map/ppermute | solution.py:312
  244.2 14.7 %collective-permute-start.58 = (bf16[32,2560]{1,0:T(8,128)(2,1)S(1)}, bf16[32,2560]{1,0:T(8,128)(2,1)S(1)}, u32[]{:S(2)}, u32[]{:S(2)}) collective-permute-start(bf16[32,2560]{1,0:T(8,128)(2,1)S(1)} %get-tuple-element.100), channel_id=1, source_target_pairs={{0,4},{1,5},{2,6},{3,7},{4,0},{5,1},{6,2},{7,3},{8,12},{9,13},{10,... | collective-permute-start | bytes 491528 | tf_op jit(solution)/shard_map/ppermute | solution.py:443
  244.2 14.7 %collective-permute-start.59 = (bf16[32,2560]{1,0:T(8,128)(2,1)S(1)}, bf16[32,2560]{1,0:T(8,128)(2,1)S(1)}, u32[]{:S(2)}, u32[]{:S(2)}) collective-permute-start(bf16[32,2560]{1,0:T(8,128)(2,1)S(1)} %get-tuple-element.99), channel_id=1, source_target_pairs={{0,6},{1,7},{2,4},{3,5},{4,2},{5,3},{6,0},{7,1},{8,14},{9,15},{10,... | collective-permute-start | bytes 491528 | tf_op jit(solution)/shard_map/ppermute | solution.py:443
  (43 other events, 300.3 us)

commit v2 on v0

--- a/solution.py
+++ b/solution.py
@@ -1,7 +1,22 @@
+import functools
+
 import jax
 import jax.numpy as jnp
 from jax import lax
+from jax.experimental import pallas as pl
+from jax.experimental.pallas import tpu as pltpu
 from jax.sharding import PartitionSpec as P
+
+BF16 = jnp.bfloat16
+F32 = jnp.float32
+COST = pl.CostEstimate(flops=10**10, bytes_accessed=10**8, transcendentals=0)
+TILE = 256
+ANY = pl.BlockSpec(memory_space=pl.ANY)
+HBM = pl.BlockSpec(memory_space=pltpu.HBM)
+WHOLE = pl.BlockSpec(memory_space=pltpu.VMEM)
+GATE_UP_CUTS = (6, 13)
+BACK_CUTS = (6, 13)
+GRAD_CUTS = (4, 8, 13)
 
 
 def expand_mask(block_ids):
@@ -39,7 +54,7 @@
     )
 
 
-def local(tokens, out_grad, gate_weight, up_weight, down_weight, gate_mask, up_mask, down_mask):
+def local_any(tokens, out_grad, gate_weight, up_weight, down_weight, gate_mask, up_mask, down_mask):
     gate_keep = expand_mask(gate_mask)
     up_keep = expand_mask(up_mask)
     down_keep = expand_mask(down_mask)
@@ -87,6 +102,583 @@
     return (input_grad, gate_weight_grad, up_weight_grad, down_weight_grad)
 
 
+def _spread_rows(codes):
+    byte = lambda k: jnp.int32(1 << (8 * k))
+    is0, is01, is012 = codes < 6, codes < 12, codes < 18
+    first = jnp.where(is0, byte(0), jnp.where(is01, byte(1), jnp.where(is012, byte(2), byte(3))))
+    rest = codes - jnp.where(is0, 0, jnp.where(is01, 6, jnp.where(is012, 12, 18)))
+    low = jnp.where(is0, byte(1), byte(0))
+    mid = jnp.where(is01, byte(2), byte(1))
+    high = jnp.where(is012, byte(3), byte(2))
+    early, late = rest < 2, rest < 4
+    second = jnp.where(early, low, jnp.where(late, mid, high))
+    third = jnp.where((rest & 1) == 0, jnp.where(early, mid, low), jnp.where(late, high, mid))
+    return first | second, second | third
+
+
+def _interleave(words, count, lane_perm, row_perm):
+    rows = words[0].shape[0]
+    wide = []
+    for w in words:
+        planes = [(lax.shift_right_logical(w, jnp.int32(8 * j)) & 255).astype(F32).astype(BF16) for j in range(4)]
+        wide.append(jnp.dot(jnp.concatenate(planes, axis=1), lane_perm, preferred_element_type=F32).astype(BF16))
+    step = row_perm.shape[0] // 4
+    local_row = lax.broadcasted_iota(jnp.int32, (4 * step, 512), 0) % 4
+    bias = 128 if count == 8 else 0
+    base = jnp.where(local_row < 2, -bias, (1 << count) - 1 - bias)
+    out = []
+    for at in range(0, rows, step):
+        stacked = jnp.concatenate([w[at : at + step] for w in wide], axis=0)
+        mixed = jnp.dot(row_perm, stacked, preferred_element_type=F32).astype(jnp.int32)
+        out.append((mixed + base).astype(jnp.int8))
+    return out
+
+
+def _words(pieces):
+    words = None
+    for s, codes in enumerate(pieces):
+        part = [w << s if s else w for w in _spread_rows(codes)]
+        words = part if words is None else [a | b for a, b in zip(words, part)]
+    return words
+
+
+def _pack_rows_kernel(gate_ref, up_ref, lane_ref, row_ref, out_ref):
+    rows = gate_ref.shape[1] // 4
+    pieces = []
+    for ref in (gate_ref, up_ref):
+        codes = ref[...].T
+        pieces += [codes[q * rows : (q + 1) * rows, :] for q in range(4)]
+    at = 0
+    for block in _interleave(_words(pieces), len(pieces), lane_ref[...], row_ref[...]):
+        out_ref[at : at + block.shape[0], :] = block
+        at += block.shape[0]
+
+
+def _pack_cols_kernel(codes_ref, lane_ref, row_ref, *refs):
+    out_ref = refs[-1]
+    block = row_ref.shape[0] // 4
+    lanes, rows = lane_ref[...], row_ref[...]
+
+    def step(t, carry):
+        codes = codes_ref[pl.ds(pl.multiple_of(t * block, block), block), :]
+        pieces = [codes[:, q : q + 128] for q in range(0, codes.shape[1], 128)]
+        (packed,) = _interleave(_words(pieces), len(pieces), lanes, rows)
+        out_ref[pl.ds(pl.multiple_of(t * 4 * block, 4 * block), 4 * block), :] = packed
+        return carry
+
+    lax.fori_loop(0, codes_ref.shape[0] // block, step, 0)
+
+
+def _lane_permutation():
+    source = lax.broadcasted_iota(jnp.int32, (512, 512), 0)
+    target = lax.broadcasted_iota(jnp.int32, (512, 512), 1)
+    return (source == (target % 4) * 128 + target // 4).astype(BF16)
+
+
+def _row_permutation(n):
+    target = lax.broadcasted_iota(jnp.int32, (4 * n, 2 * n), 0)
+    source = lax.broadcasted_iota(jnp.int32, (4 * n, 2 * n), 1)
+    hit = source == (target % 2) * n + target // 4
+    return jnp.where(hit, jnp.where(target % 4 < 2, 1, -1), 0).astype(BF16)
+
+
+def pack_gate_up(gate_mask, up_mask):
+    code_rows, code_cols = gate_mask.shape
+    return pl.pallas_call(
+        _pack_rows_kernel,
+        grid=(pl.cdiv(code_cols, 128),),
+        in_specs=[
+            pl.BlockSpec((128, code_rows), lambda j: (j, 0)),
+            pl.BlockSpec((128, code_rows), lambda j: (j, 0)),
+            pl.BlockSpec((512, 512), lambda j: (0, 0)),
+            pl.BlockSpec((128, 64), lambda j: (0, 0)),
+        ],
+        out_specs=pl.BlockSpec((code_rows, 512), lambda j: (0, j)),
+        out_shape=jax.ShapeDtypeStruct((code_rows, 4 * code_cols), jnp.int8),
+        compiler_params=pltpu.CompilerParams(vmem_limit_bytes=46 * 2**20),
+        cost_estimate=COST,
+        name="pack_gate_up",
+    )(gate_mask.T, up_mask.T, _lane_permutation(), _row_permutation(32))
+
+
+def pack_down(down_mask, after):
+    return pl.pallas_call(
+        _pack_cols_kernel,
+        in_specs=[WHOLE] * 3 + [ANY] * len(after),
+        out_specs=WHOLE,
+        out_shape=jax.ShapeDtypeStruct((4 * down_mask.shape[0], 512), jnp.int8),
+        compiler_params=pltpu.CompilerParams(vmem_limit_bytes=46 * 2**20),
+        cost_estimate=COST,
+        name="pack_down",
+    )(down_mask, _lane_permutation(), _row_permutation(TILE // 4), *after)
+
+
+def _bit(packed, s):
+    if s == 7:
+        return BF16(1) + (packed & jnp.int8(-128)).astype(BF16) * BF16(2.0**-7)
+    return (packed & jnp.int8(1 << s)).astype(BF16) * BF16(2.0**-s)
+
+
+def _rows_keep(packed, first):
+    return jnp.concatenate([_bit(packed, first + q) for q in range(4)], axis=0)
+
+
+def _cols_keep(packed, groups):
+    return jnp.concatenate([_bit(packed, q) for q in range(groups)], axis=1)
+
+
+def _tile(t):
+    return pl.ds(pl.multiple_of(t * TILE, TILE), TILE)
+
+
+class _Loads:
+    def __init__(self, panels, bufs, sems, first, count):
+        self.panels, self.bufs, self.sems, self.first, self.count = panels, bufs, sems, first, count
+
+    def copy(self, k, t):
+        panel, by_rows = self.panels[k]
+        at = pl.ds(pl.multiple_of((self.first + t) * TILE, TILE), TILE)
+        source = panel.at[at, :] if by_rows else panel.at[:, at]
+        return pltpu.make_async_copy(source, self.bufs[k].at[t], self.sems.at[k, t])
+
+    def start(self):
+        for t in range(self.count):
+            for k in range(len(self.panels)):
+                self.copy(k, t).start()
+
+    def copy_out(self, k, t):
+        panel, by_rows = self.panels[k]
+        at = pl.ds(pl.multiple_of((self.first + t) * TILE, TILE), TILE)
+        target = panel.at[at, :] if by_rows else panel.at[:, at]
+        return pltpu.make_async_copy(self.bufs[k].at[t], target, self.sems.at[k, t])
+
+    def wait_out(self):
+        for t in range(self.count):
+            for k in range(len(self.panels)):
+                self.copy_out(k, t).wait()
+
+    def wait(self, t):
+        for k in range(len(self.panels)):
+            self.copy(k, t).wait()
+
+
+def _load_scratch(panels, count):
+    shapes = []
+    for panel, by_rows in panels:
+        block = (TILE, panel.shape[1]) if by_rows else (panel.shape[0], TILE)
+        shapes.append(pltpu.VMEM((count, *block), panel.dtype))
+    return shapes, pltpu.SemaphoreType.DMA((len(panels), count))
+
+
+def _store_sums(at, t, sums, own_ref, to_x_ref, to_y_ref, mix_ref):
+    half = sums.shape[0] // 8
+    cut = lambda k, n=1: sums[k * half : (k + n) * half]
+    lanes = _tile(t)
+    own_ref[at, :, lanes] = cut(0, 2)
+    to_x_ref[at, :half, lanes] = cut(2).astype(BF16)
+    to_x_ref[at, half:, lanes] = cut(6).astype(BF16)
+    to_y_ref[at, :half, lanes] = cut(5).astype(BF16)
+    to_y_ref[at, half:, lanes] = cut(7).astype(BF16)
+    mix_ref[at, :, lanes] = cut(3, 2)
+
+
+def _gate_up_kernel(first, count, n_after, tok_ref, gate_any, up_any, bits_any, *refs):
+    out_refs, (gate_buf, up_buf, bits_buf, sems) = refs[n_after : n_after + 4], refs[n_after + 4 :]
+    loads = _Loads(
+        [(gate_any, False), (up_any, False), (bits_any, False)], (gate_buf, up_buf, bits_buf), sems, first, count
+    )
+    loads.start()
+
+    def step(t, carry):
+        loads.wait(t)
+        packed = bits_buf[t]
+        for at, buf in enumerate((gate_buf, up_buf)):
+            pruned = buf[t] * _rows_keep(packed, 4 * at)
+            _store_sums(at, t, jnp.dot(tok_ref[...], pruned, preferred_element_type=F32), *out_refs)
+        return carry
+
+    lax.fori_loop(0, count, step, 0)
+
+
+def _back_kernel(first, count, n_after, grad_ref, down_any, bits_any, *refs):
+    out_refs, (down_buf, bits_buf, sems) = refs[n_after : n_after + 4], refs[n_after + 4 :]
+    loads = _Loads([(down_any, True), (bits_any, True)], (down_buf, bits_buf), sems, first, count)
+    loads.start()
+    groups = grad_ref.shape[1] // 512
+
+    def step(t, carry):
+        loads.wait(t)
+        pruned = down_buf[t] * _cols_keep(bits_buf[t], groups)
+        _store_sums(0, t, contract_last(grad_ref[...], pruned), *out_refs)
+        return carry
+
+    lax.fori_loop(0, count, step, 0)
+
+
+def _sum_shapes(n, rows, width):
+    shape = lambda t: jax.ShapeDtypeStruct((n, rows // 4, width), t)
+    return [shape(F32), shape(BF16), shape(BF16), shape(F32)]
+
+
+def gate_up_sums(tok, gate_weight, up_weight, gate_up_bits, first, count, after=()):
+    rows, depth = tok.shape
+    bufs, sems = _load_scratch([(gate_weight, False), (up_weight, False), (gate_up_bits, False)], count)
+    return pl.pallas_call(
+        functools.partial(_gate_up_kernel, first, count, len(after)),
+        in_specs=[WHOLE, HBM, HBM, HBM] + [ANY] * len(after),
+        out_specs=[WHOLE] * 4,
+        out_shape=_sum_shapes(2, rows, count * TILE),
+        scratch_shapes=[*bufs, sems],
+        compiler_params=pltpu.CompilerParams(vmem_limit_bytes=46 * 2**20),
+        cost_estimate=COST,
+        name="gate_up_sums",
+    )(tok, gate_weight, up_weight, gate_up_bits, *after)
+
+
+def back_sums(grads, down_weight, down_bits, first, count, after=()):
+    rows, depth = grads.shape
+    bufs, sems = _load_scratch([(down_weight, True), (down_bits, True)], count)
+    return pl.pallas_call(
+        functools.partial(_back_kernel, first, count, len(after)),
+        in_specs=[WHOLE, HBM, HBM] + [ANY] * len(after),
+        out_specs=[WHOLE] * 4,
+        out_shape=_sum_shapes(1, rows, count * TILE),
+        scratch_shapes=[*bufs, sems],
+        compiler_params=pltpu.CompilerParams(vmem_limit_bytes=46 * 2**20),
+        cost_estimate=COST,
+        name="back_sums",
+    )(grads, down_weight, down_bits, *after)
+
+
+def _swap(value, bit):
+    return lax.ppermute(value, "row", [(i, i ^ bit) for i in range(4)])
+
+
+def _widen(parts):
+    return jnp.concatenate(parts, axis=2) if len(parts) > 1 else parts[0]
+
+
+class Reduction:
+    def __init__(self):
+        self.sums, self.received = [], []
+
+    def first(self, sums):
+        _, to_x, to_y, _ = sums
+        self.sums.append(sums)
+        self.received.append((_swap(to_x, 1), _swap(to_y, 2)))
+
+    def mixed(self):
+        half = self.sums[0][0].shape[1] // 2
+        pairs = list(zip(self.sums, self.received))
+        self.mixed_x = _widen([(s[3][:, :half] + r[1][:, half:]).astype(BF16) for s, r in pairs])
+        self.mixed_y = _widen([(s[3][:, half:] + r[0][:, half:]).astype(BF16) for s, r in pairs])
+
+    def second(self):
+        self.second_x, self.second_y = _swap(self.mixed_x, 1), _swap(self.mixed_y, 2)
+
+    def hold_first(self, until):
+        self.received[-1] = _hold(self.received[-1], until)
+
+    def hold_second(self, until):
+        self.second_x, self.second_y = _hold((self.second_x, self.second_y), until)
+
+    def total(self):
+        half = self.sums[0][0].shape[1] // 2
+        pairs = list(zip(self.sums, self.received))
+        first_half = _widen([s[0][:, :half] + r[0][:, :half] for s, r in pairs]) + self.second_y
+        second_half = _widen([s[0][:, half:] + r[1][:, :half] for s, r in pairs]) + self.second_x
+        return jnp.concatenate([first_half, second_half], axis=1)
+
+
+def _hold(values, until):
+    return lax.optimization_barrier((values, until))[0]
+
+
+class Gathering:
+    def __init__(self, block):
+        self.block = block
+
+    def first(self):
+        self.from_x, self.from_y = _swap(self.block, 1), _swap(self.block, 2)
+
+    def hold_first(self, until):
+        self.from_x, self.from_y = _hold((self.from_x, self.from_y), until)
+
+    def cut(self):
+        half = self.block.shape[1] // 2
+        self.cut_x, self.cut_y = self.from_x[:, :half], self.from_y[:, half:]
+
+    def second(self):
+        diag_a, diag_b = _swap(self.cut_x, 2), _swap(self.cut_y, 1)
+        self.blocks = (self.block, self.from_x, self.from_y, diag_a, diag_b)
+
+
+def swiglu(gate_sum, up_sum):
+    return (gate_sum * jax.nn.sigmoid(gate_sum) * up_sum).astype(BF16)
+
+
+def swiglu_back(gate_sum, up_sum, back_sum):
+    logistic = jax.nn.sigmoid(gate_sum)
+    up_grad = back_sum * (gate_sum * logistic)
+    gate_grad = back_sum * up_sum * logistic * (1.0 + gate_sum * (1.0 - logistic))
+    return jnp.stack([gate_grad, up_grad]).astype(BF16)
+
+
+def _backward_kernel(first, count, with_acc, with_input, with_weights, n_alias, n_after, *refs):
+    refs = list(refs)
+    take = lambda n: [refs.pop(0) for _ in range(n)]
+    block_refs = take(5)
+    panels = [(ref, False) for ref in take(1)]
+    if with_input:
+        panels += [(ref, False) for ref in take(2)]
+        acc_refs = take(2) if with_acc else []
+    if with_weights:
+        (tok_ref,) = take(1)
+        take(n_alias)
+    take(n_after)
+    sum_refs = take(2) if with_input else []
+    outs = take(2) if with_weights else []
+    bufs = take(len(panels))
+    out_bufs = take(2) if with_weights else []
+    load_sems = refs.pop(0)
+    loads = _Loads(panels, bufs, load_sems, first, count)
+    stores = _Loads([(ref, False) for ref in outs], out_bufs, refs.pop(0), first, count) if with_weights else None
+    loads.start()
+    if with_input:
+        for k, ref in enumerate(sum_refs):
+            ref[...] = acc_refs[k][...] if with_acc else jnp.zeros_like(ref)
+
+    def step(t, carry):
+        loads.wait(t)
+        lanes = _tile(t)
+        rows_of = lambda k: jnp.concatenate([ref[k, :, lanes] for ref in block_refs], axis=0)
+        packed = bufs[0][t]
+        gate_keep, up_keep = _rows_keep(packed, 0), _rows_keep(packed, 4)
+        gate_grad, up_grad = rows_of(0), rows_of(1)
+        if with_weights:
+            tok = tok_ref[...]
+            out_bufs[0][t] = contract_first(tok, gate_grad).astype(BF16) * gate_keep
+            stores.copy_out(0, t).start()
+            out_bufs[1][t] = contract_first(tok, up_grad).astype(BF16) * up_keep
+            stores.copy_out(1, t).start()
+        if with_input:
+            part = contract_last(gate_grad, bufs[1][t] * gate_keep) + contract_last(up_grad, bufs[2][t] * up_keep)
+            half = sum_refs[0].shape[1]
+            for p in range(4):
+                for k, ref in enumerate(sum_refs):
+                    ref[p] += part[(2 * p + k) * half : (2 * p + k + 1) * half]
+        return carry
+
+    lax.fori_loop(0, count, step, 0)
+    if with_weights:
+        stores.wait_out()
+
+
+def backward(blocks, gate_up_bits, first, count, inputs=None, weights=None, after=()):
+    args, specs, shapes, out_specs, aliases = list(blocks), [WHOLE] * 5, [], [], {}
+    rows = 4 * blocks[0].shape[1]
+    depth = 4 * gate_up_bits.shape[0]
+    width = gate_up_bits.shape[1]
+    panels, outs = [(gate_up_bits, False)], []
+    args.append(gate_up_bits)
+    specs.append(HBM)
+    if inputs is not None:
+        gate_weight, up_weight, acc = inputs
+        panels += [(gate_weight, False), (up_weight, False)]
+        args += [gate_weight, up_weight]
+        specs += [HBM, HBM]
+        if acc is not None:
+            args += acc
+            specs += [WHOLE] * 2
+        shapes += [jax.ShapeDtypeStruct((4, rows // 8, depth), F32)] * 2
+        out_specs += [WHOLE] * 2
+    n_alias = 0
+    if weights is not None:
+        tok, so_far = weights
+        args.append(tok)
+        specs.append(WHOLE)
+        if so_far is not None:
+            n_alias = 2
+            for k, value in enumerate(so_far):
+                aliases[len(args)] = len(shapes) + k
+                args.append(value)
+                specs.append(HBM)
+        outs = [jax.ShapeDtypeStruct((depth, width), BF16)] * 2
+        shapes += outs
+        out_specs += [HBM] * 2
+    bufs, sems = _load_scratch(panels, count)
+    scratch = [*bufs, sems]
+    if weights is not None:
+        out_bufs, out_sems = _load_scratch([(out, False) for out in outs], count)
+        scratch = [*bufs, *out_bufs, sems, out_sems]
+    args += list(after)
+    specs += [ANY] * len(after)
+    return pl.pallas_call(
+        functools.partial(
+            _backward_kernel,
+            first,
+            count,
+            inputs is not None and inputs[2] is not None,
+            inputs is not None,
+            weights is not None,
+            n_alias,
+            len(after),
+        ),
+        in_specs=specs,
+        out_specs=out_specs,
+        out_shape=shapes,
+        scratch_shapes=scratch,
+        input_output_aliases=aliases,
+        compiler_params=pltpu.CompilerParams(vmem_limit_bytes=46 * 2**20),
+        cost_estimate=COST,
+        name="backward",
+    )(*args)
+
+
+def _down_grad_kernel(count, n_after, *refs):
+    block_refs, (grad_ref, bits_any), (out_any, bits_buf, out_buf, sems, out_sems) = refs[:5], refs[5:7], refs[7 + n_after :]
+    loads = _Loads([(bits_any, True)], [bits_buf], sems, 0, count)
+    stores = _Loads([(out_any, True)], [out_buf], out_sems, 0, count)
+    loads.start()
+
+    def step(t, carry):
+        loads.wait(t)
+        hidden = jnp.concatenate([ref[0, :, _tile(t)] for ref in block_refs], axis=0)
+        keep = _cols_keep(bits_buf[t], grad_ref.shape[1] // 512)
+        out_buf[t] = contract_first(hidden, grad_ref[...]).astype(BF16) * keep
+        stores.copy_out(0, t).start()
+        return carry
+
+    lax.fori_loop(0, count, step, 0)
+    stores.wait_out()
+
+
+def down_grad(blocks, grads, down_bits, after=()):
+    width, depth = down_bits.shape[0], grads.shape[1]
+    count = width // TILE
+    out = jax.ShapeDtypeStruct((width, depth), BF16)
+    (bits_buf,), sems = _load_scratch([(down_bits, True)], count)
+    (out_buf,), out_sems = _load_scratch([(out, True)], count)
+    return pl.pallas_call(
+        functools.partial(_down_grad_kernel, count, len(after)),
+        in_specs=[WHOLE] * 6 + [HBM] + [ANY] * len(after),
+        out_specs=HBM,
+        out_shape=out,
+        scratch_shapes=[bits_buf, out_buf, sems, out_sems],
+        compiler_params=pltpu.CompilerParams(vmem_limit_bytes=46 * 2**20),
+        cost_estimate=COST,
+        name="down_grad",
+    )(*blocks, grads, down_bits, *after)
+
+
+def _col_swap(value, bits):
+    return lax.ppermute(value, "col", [(i, i ^ bits) for i in range(8)])
+
+
+def gather_groups(value):
+    return [value] + [_col_swap(value, 2 * k) for k in (1, 2, 3)]
+
+
+def order_groups(mine, theirs, order):
+    groups = []
+    for p in range(4):
+        for part in (mine, theirs):
+            groups.append(lax.dynamic_index_in_dim(part, p ^ order, 0, keepdims=False))
+    return jnp.concatenate(groups, axis=0)
+
+
+def chunks_of(tiles, cuts):
+    ends = [0] + [(tiles * c + 6) // 13 for c in cuts]
+    return [(a, b - a) for a, b in zip(ends[:-1], ends[1:])]
+
+
+def local_tiled(tokens, out_grad, gate_weight, up_weight, down_weight, gate_mask, up_mask, down_mask):
+    order = lax.axis_index("row") ^ (lax.axis_index("col") // 2)
+    tiles = gate_weight.shape[1] // TILE
+    gate_up_bits = pack_gate_up(gate_mask, up_mask)
+    tok_mine, gate_up_bits = lax.optimization_barrier((gather_groups(tokens), gate_up_bits))
+    tok_mine = jnp.stack(tok_mine)
+    tok_theirs = _col_swap(tok_mine, 1)
+    tok = order_groups(tok_mine, tok_theirs, order)
+    gate_up = lambda c, after: gate_up_sums(tok, gate_weight, up_weight, gate_up_bits, *c, after=after)
+    back = lambda c, after: back_sums(grads, down_weight, down_bits, *c, after=after)
+    gate_up_red, back_red = Reduction(), Reduction()
+
+    cuts = chunks_of(tiles, GATE_UP_CUTS)
+    sums0 = gate_up(cuts[0], [])
+    gate_up_red.first(sums0)
+    sums1 = gate_up(cuts[1], [sums0[0]])
+    gate_up_red.hold_first(sums1[0])
+    gate_up_red.first(sums1)
+    grad_mine = gather_groups(_hold(out_grad, sums1[0]))
+    down_bits = pack_down(down_mask, [sums1[0], *gate_up_red.received[0]])
+    gate_up_red.hold_first(down_bits)
+    grad_mine = jnp.stack(_hold(grad_mine, down_bits))
+    grad_theirs = _col_swap(grad_mine, 1)
+    gate_up_red.mixed()
+    gate_up_red.second()
+    grads = order_groups(grad_mine, grad_theirs, order)
+    cuts = chunks_of(tiles, BACK_CUTS)
+    sums0 = back(cuts[0], [gate_up_red.mixed_x, gate_up_red.mixed_y])
+    back_red.first(sums0)
+    sums1 = back(cuts[1], [sums0[0]])
+    back_red.hold_first(sums1[0])
+    gate_up_red.hold_second(sums1[0])
+    back_red.first(sums1)
+    gate_up_total = gate_up_red.total()
+    hidden = Gathering(swiglu(*gate_up_total)[None])
+    gate_up_total = _hold(gate_up_total, hidden.block)
+    hidden.first()
+    hidden.cut()
+    hidden.second()
+    back_red.mixed()
+    back_red.second()
+    block = swiglu_back(*gate_up_total, *back_red.total())
+    chunks = chunks_of(tiles, GRAD_CUTS)
+    gath = [Gathering(block[:, :, a * TILE : (a + n) * TILE]) for a, n in chunks]
+    gath[0].first()
+    gath[1].first()
+    down_out = down_grad(hidden.blocks, grads, down_bits, [gath[0].block, gath[1].block])
+    gath[0].hold_first(down_out)
+    gath[1].hold_first(down_out)
+    gath[0].cut()
+    gath[0].second()
+    gath[1].cut()
+    gath[1].second()
+    gath[2].block = _hold(gath[2].block, down_out)
+    gath[2].first()
+    pair = (gate_weight, up_weight)
+    acc = backward(gath[0].blocks, gate_up_bits, *chunks[0], inputs=(*pair, None), after=[gath[1].cut_x, gath[1].cut_y])
+    gath[2].hold_first(acc[0])
+    gath[2].cut()
+    gath[2].second()
+    acc = backward(gath[1].blocks, gate_up_bits, *chunks[1], inputs=(*pair, acc), after=[gath[2].cut_x, gath[2].cut_y])
+    acc = backward(gath[2].blocks, gate_up_bits, *chunks[2], inputs=(*pair, acc))
+    pairs = acc[0] + _col_swap(acc[1], 1)
+    own = lax.dynamic_index_in_dim(pairs, order, 0, keepdims=False)
+    sent = [lax.dynamic_index_in_dim(pairs, k ^ order, 0, keepdims=False).astype(BF16) for k in (1, 2, 3)]
+    received = [_col_swap(value, 2 * k) for k, value in zip((1, 2, 3), sent)]
+    outs = backward(gath[0].blocks, gate_up_bits, *chunks[0], weights=(tok, None), after=sent)
+    outs = backward(gath[1].blocks, gate_up_bits, *chunks[1], weights=(tok, outs))
+    outs = backward(gath[2].blocks, gate_up_bits, *chunks[2], weights=(tok, outs))
+    for value in received:
+        own = own + value
+    return (own.astype(BF16), *outs, down_out)
+
+
+def tiled_fits(mesh, depth, width, token_rows):
+    return (
+        mesh.shape["row"] == 4
+        and mesh.shape["col"] == 8
+        and depth % 1280 == 0
+        and depth // 512 <= 7
+        and depth % 512 == 0
+        and width % TILE == 0
+        and width // TILE >= 13
+        and token_rows % 256 == 0
+    )
+
+
 def solution(mesh):
     in_specs = (
         P("col", "row"),
@@ -99,4 +691,12 @@
         P("col", "row"),
     )
     out_specs = (P("col", "row"), P("row", "col"), P("row", "col"), P("col", "row"))
-    return jax.shard_map(local, mesh=mesh, in_specs=in_specs, out_specs=out_specs, check_vma=False)
+
+    def run(tokens, out_grad, gate_weight, *rest):
+        depth = gate_weight.shape[0] // mesh.shape["row"]
+        width = gate_weight.shape[1] // mesh.shape["col"]
+        body = local_tiled if tiled_fits(mesh, depth, width, tokens.shape[0]) else local_any
+        mapped = jax.shard_map(body, mesh=mesh, in_specs=in_specs, out_specs=out_specs, check_vma=False)
+        return mapped(tokens, out_grad, gate_weight, *rest)
+
+    return run

time: 893 us -> 166 us (0.19); the launches traced: 877 us -> 166 us
  local copies, waits for them, and re-layouts: 465 us -> 3.7 us
  waiting for transfers between devices: 166 us -> 28.8 us
  other arithmetic: 127 us -> 3.68 us
  matrix products: 104 us -> 0 us
  Pallas kernels: 0 us -> 86.3 us
  starting transfers between devices: 0.2 us -> 42.1 us
  between operations: 14.5 us -> 1.42 us
    reshape x17 -> x0, local copies, waits for them, and re-layouts: 255 us -> none  [the longest x5 127 us: expand_mask(): jnp.stack(row_list, axis=1).reshape(4 * group_rows, 4 * group_cols)]
    reduce_scatter x2 -> x0, waiting for transfers between devices: 104 us -> none  [the longest x1 104 us: local(): lax.psum_scatter(jnp.concatenate([gate_sum, up_sum, back_sum], axis=1), '...]
    dot_general x8 -> x0, matrix products: 104 us -> none  [the longest x3 41.8 us: contract_last(): lax.dot_general(left, right, (((1,), (1,)), ((), ())), preferred_element_...]
    pallas_call x0 -> x13, Pallas kernels: none -> 86.3 us  [the longest x6 34 us: backward(): pl.pallas_call(functools.partial(_backward_kernel, first, count, inputs i...]
    another operation x3 -> x0, local copies, waits for them, and re-layouts: 83.6 us -> none  [expand_mask(): jnp.stack(row_list, axis=1).reshape(4 * group_rows, 4 * group_cols)]
    or x10 -> x0, other arithmetic: 61.8 us -> none  [expand_mask(): row_list.append((current == col_position) | (following == col_position))]
    all_gather x3 -> x0, waiting for transfers between devices: 60.4 us -> none  [the longest x1 60.4 us: local(): all_local = lax.all_gather(local_grads, 'row', axis=0, tiled=True)]
    broadcast_in_dim x12 -> x0, local copies, waits for them, and re-layouts: 60.1 us -> none  [the longest x9 45.1 us: expand_mask(): following = jnp.repeat(ordering[(local_row + 1) % 4], 4, axis=1)]
  transfers between devices with their start and end apart: 5 -> 40, of which waited for: 2 -> 9; matrix products, arithmetic and copies ran while one was open for 72% -> 2% of each run, Pallas kernels for 0% -> 44%
where the time goes in v2:
time: 166 us
  Pallas kernels  86.3 us (52%)
  starting transfers between devices  42.1 us (25%)
  waiting for transfers between devices  28.8 us (17%)
  local copies, waits for them, and re-layouts  3.7 us (2%)
  other arithmetic  3.68 us (2%)
    pallas_call x6, Pallas kernels, backward(): pl.pallas_call(functools.partial(_backward_kernel, first, count, inputs i...  34 us
    ppermute x28, starting transfers between devices, _swap(): return lax.ppermute(value, 'row', [(i, i ^ bit) for i in range(4)])  28.2 us
    ppermute x28, waiting for transfers between devices, _swap(): return lax.ppermute(value, 'row', [(i, i ^ bit) for i in range(4)])  19.4 us
    pallas_call x2, Pallas kernels, gate_up_sums(): pl.pallas_call(functools.partial(_gate_up_kernel, first, count, len(after...  15.2 us
    ppermute x12, starting transfers between devices, _col_swap(): return lax.ppermute(value, 'col', [(i, i ^ bits) for i in range(8)])  13.9 us
    pallas_call x1, Pallas kernels, down_grad(): pl.pallas_call(functools.partial(_down_grad_kernel, count, len(after)), i...  10.4 us
    pallas_call x2, Pallas kernels, back_sums(): pl.pallas_call(functools.partial(_back_kernel, first, count, len(after)),...  10 us
    ppermute x12, waiting for transfers between devices, _col_swap(): return lax.ppermute(value, 'col', [(i, i ^ bits) for i in range(8)])  9.44 us
  transfers between devices with their start and end apart: 40, of which 9 were waited for; matrix products, arithmetic and copies ran while one was open for 2% of the time, Pallas kernels for 44%

profile of v2, /device:TPU:0, one launch (start us, length us, event | category | flops | bytes accessed | tf_op | source)
XLA Modules:
  0.0 166.1 jit_solution(7735654880593415650)
XLA Ops:
  0.6 4.1 %collective-permute-start.1 = (bf16[32,2560]{1,0:T(8,128)(2,1)}, bf16[32,2560]{1,0:T(8,128)(2,1)S(1)}, u32[]{:S(2)}, u32[]{:S(2)}) collective-permute-start(bf16[32,2560]{1,0:T(8,128)(2,1)} %param.8), channel_id=1, source_target_pairs={{0,4},{1,5},{2,6},{3,7},{4,0},{5,1},{6,2},{7,3},{8,12},{9,13},{10,... | collective-permute-start | bytes 491528 | tf_op jit(solution)/shard_map/ppermute | solution.py:575
  10.0 8.9 %pack_gate_up.1.bits_any.refs_5_ = s8[640,3328]{1,0:T(32,128)(4,1)S(1)} custom-call(s32[832,640]{1,0:T(8,128)S(1)} %bitcast.56, s32[832,640]{1,0:T(8,128)S(1)} %bitcast.57, bf16[512,512]{1,0:T(8,128)(2,1)S(1)} %fusion.lane_ref, bf16[128,64]{1,0:T(8,128)(2,1)S(1)} %select_convert_fusion.1.row_ref), custom_call_target="tpu_custom_call" | custom-call | flops 10000000000 | bytes 100000000 | tf_op jit(solution)/shard_map/pack_gate_up/pallas_call | solution.py:187
  21.4 7.1 %gate_up_sums.2 = (f32[2,64,1536]{2,1,0:T(8,128)S(1)}, bf16[2,64,1536]{2,1,0:T(8,128)(2,1)S(1)}, bf16[2,64,1536]{2,1,0:T(8,128)(2,1)S(1)}, f32[2,64,1536]{2,1,0:T(8,128)S(1)}) custom-call(bf16[256,2560]{1,0:T(8,128)(2,1)S(1)} %bitcast_dynamic-update-slice_fusion.8.tok_ref.refs_6_, bf16[2560,3328]{1,0:T(8,128)(2,1)} %refs_6_.5, bf16[2560,3328]{1,0:T(8,128)(2,1)} %refs_7_.5, ...), custom_call_target="tpu_custom_call" | custom-call | flops 10000000000 | bytes 100000000 | tf_op jit(solution)/shard_map/gate_up_sums/pallas_call | solution.py:326
  28.5 1.8 %collective-permute-start.7 = (bf16[2,64,1536]{2,1,0:T(8,128)(2,1)S(1)}, bf16[2,64,1536]{2,1,0:T(8,128)(2,1)S(1)}, u32[]{:S(2)}, u32[]{:S(2)}) collective-permute-start(bf16[2,64,1536]{2,1,0:T(8,128)(2,1)S(1)} %get-tuple-element.66), channel_id=1, source_target_pairs={{0,8},{8,0},{16,24},{24,16},{1,9},{9,1},{17,25},{25,17},{2,10},{10... | collective-permute-start | bytes 1179656 | tf_op jit(solution)/shard_map/ppermute | solution.py:354
  31.8 8.1 %gate_up_sums.3 = (f32[2,64,1792]{2,1,0:T(8,128)S(1)}, bf16[2,64,1792]{2,1,0:T(8,128)(2,1)S(1)}, bf16[2,64,1792]{2,1,0:T(8,128)(2,1)S(1)}, f32[2,64,1792]{2,1,0:T(8,128)S(1)}) custom-call(bf16[256,2560]{1,0:T(8,128)(2,1)S(1)} %bitcast_dynamic-update-slice_fusion.8.tok_ref.refs_6_, bf16[2560,3328]{1,0:T(8,128)(2,1)} %refs_6_.5, bf16[2560,3328]{1,0:T(8,128)(2,1)} %refs_7_.5, ...), custom_call_target="tpu_custom_call" | custom-call | flops 10000000000 | bytes 100000000 | tf_op jit(solution)/shard_map/gate_up_sums/pallas_call | solution.py:326
  40.0 3.7 %collective-permute-start.6 = (bf16[32,2560]{1,0:T(8,128)(2,1)S(1)}, bf16[32,2560]{1,0:T(8,128)(2,1)S(1)}, u32[]{:S(2)}, u32[]{:S(2)}) collective-permute-start(bf16[32,2560]{1,0:T(8,128)(2,1)S(1)} %copy-done.8), channel_id=1, source_target_pairs={{0,6},{1,7},{2,4},{3,5},{4,2},{5,3},{6,0},{7,1},{8,14},{9,15},{10,... | collective-permute-start | bytes 491528 | tf_op jit(solution)/shard_map/ppermute | solution.py:575
  45.3 7.8 %pack_down.1.bits_any.refs_6_ = s8[3328,512]{1,0:T(32,128)(4,1)S(1)} custom-call(s32[832,640]{1,0:T(8,128)S(1)} %copy-done.4, bf16[512,512]{1,0:T(8,128)(2,1)S(1)} %fusion.lane_ref, bf16[256,128]{1,0:T(8,128)(2,1)S(1)} %select_convert_fusion.row_ref, f32[2,64,1792]{2,1,0:T(8,128)S(1)} %get-tuple-element.64.refs_0_, ...), custom_call_target="tpu_custom_call" | custom-call | flops 10000000000 | bytes 100000000 | tf_op jit(solution)/shard_map/pack_down/pallas_call | solution.py:205
  53.2 4.5 %collective-permute-done.5 = bf16[32,2560]{1,0:T(8,128)(2,1)S(1)} collective-permute-done((bf16[32,2560]{1,0:T(8,128)(2,1)S(1)}, bf16[32,2560]{1,0:T(8,128)(2,1)S(1)}, u32[]{:S(2)}, u32[]{:S(2)}) %collective-permute-start.5) | collective-permute-done | bytes 163872 | tf_op jit(solution)/shard_map/ppermute | solution.py:575
  60.1 4.7 %back_sums.2 = (f32[1,64,1536]{2,1,0:T(8,128)S(1)}, bf16[1,64,1536]{2,1,0:T(8,128)(2,1)S(1)}, bf16[1,64,1536]{2,1,0:T(8,128)(2,1)S(1)}, f32[1,64,1536]{2,1,0:T(8,128)S(1)}) custom-call(bf16[256,2560]{1,0:T(8,128)(2,1)S(1)} %bitcast_dynamic-update-slice_fusion.grad_ref.refs_5_, bf16[3328,2560]{1,0:T(8,128)(2,1)} %down_any.3, ...), custom_call_target="tpu_custom_call" | custom-call | flops 10000000000 | bytes 100000000 | tf_op jit(solution)/shard_map/back_sums/pallas_call | solution.py:341
  67.5 5.3 %back_sums.3 = (f32[1,64,1792]{2,1,0:T(8,128)S(1)}, bf16[1,64,1792]{2,1,0:T(8,128)(2,1)S(1)}, bf16[1,64,1792]{2,1,0:T(8,128)(2,1)S(1)}, f32[1,64,1792]{2,1,0:T(8,128)S(1)}) custom-call(bf16[256,2560]{1,0:T(8,128)(2,1)S(1)} %bitcast_dynamic-update-slice_fusion.grad_ref.refs_5_, bf16[3328,2560]{1,0:T(8,128)(2,1)} %down_any.3, ...), custom_call_target="tpu_custom_call" | custom-call | flops 10000000000 | bytes 100000000 | tf_op jit(solution)/shard_map/back_sums/pallas_call | solution.py:341
  77.5 12.1 %collective-permute-done.14 = bf16[1,64,1792]{2,1,0:T(8,128)(2,1)S(1)} collective-permute-done((bf16[1,64,1792]{2,1,0:T(8,128)(2,1)S(1)}, bf16[1,64,1792]{2,1,0:T(8,128)(2,1)S(1)}, u32[]{:S(2)}, u32[]{:S(2)}) %collective-permute-start.14) | collective-permute-done | bytes 229408 | tf_op jit(solution)/shard_map/ppermute | solution.py:354
  94.1 3.7 %collective-permute-done.15 = bf16[1,32,3328]{2,1,0:T(8,128)(2,1)S(1)} collective-permute-done((bf16[1,32,3328]{2,1,0:T(8,128)(2,1)S(1)}, bf16[1,32,3328]{2,1,0:T(8,128)(2,1)S(1)}, u32[]{:S(2)}, u32[]{:S(2)}) %collective-permute-start.15) | collective-permute-done | bytes 213024 | tf_op jit(solution)/shard_map/ppermute | solution.py:354
  104.0 10.4 %down_grad.1 = bf16[3328,2560]{1,0:T(8,128)(2,1)} custom-call(bf16[1,64,3328]{2,1,0:T(8,128)(2,1)S(1)} %fusion.4.refs_0_, bf16[1,64,3328]{2,1,0:T(8,128)(2,1)S(1)} %collective-permute-done.20.refs_1_, bf16[1,64,3328]{2,1,0:T(8,128)(2,1)S(1)} %collective-permute-done.21.refs_2_, bf16[1,32,3328]{2,1,0:T(8,128)(2,1)S(1)} %collective-permute-done.22.refs_3_, ...), custom_call_target="tpu_custom_call" | custom-call | flops 10000000000 | bytes 100000000 | tf_op jit(solution)/shard_map/down_grad/pallas_call | solution.py:562
  114.5 2.0 %collective-permute-start.29 = (bf16[2,32,1024]{2,1,0:T(8,128)(2,1)S(1)}, bf16[2,32,1024]{2,1,0:T(8,128)(2,1)S(1)}, u32[]{:S(2)}, u32[]{:S(2)}) collective-permute-start(bf16[2,32,1024]{2,1,0:T(8,128)(2,1)S(1)} %slice.167), channel_id=1, source_target_pairs={{0,8},{8,0},{16,24},{24,16},{1,9},{9,1},{17,25},{25,17},{2,10},{10... | collective-permute-start | bytes 393224 | tf_op jit(solution)/shard_map/ppermute | solution.py:354
  118.8 2.0 %collective-permute-start.35 = (bf16[2,32,1024]{2,1,0:T(8,128)(2,1)S(1)}, bf16[2,32,1024]{2,1,0:T(8,128)(2,1)S(1)}, u32[]{:S(2)}, u32[]{:S(2)}) collective-permute-start(bf16[2,32,1024]{2,1,0:T(8,128)(2,1)S(1)} %slice.169.refs_9_), channel_id=1, source_target_pairs={{0,8},{8,0},{16,24},{24,16},{1,9},{9,1},{17,25},{25,17},{2,10},{10... | collective-permute-start | bytes 393224 | tf_op jit(solution)/shard_map/ppermute | solution.py:354
  121.0 1.8 %collective-permute-start.34 = (bf16[2,32,1024]{2,1,0:T(8,128)(2,1)S(1)}, bf16[2,32,1024]{2,1,0:T(8,128)(2,1)S(1)}, u32[]{:S(2)}, u32[]{:S(2)}) collective-permute-start(bf16[2,32,1024]{2,1,0:T(8,128)(2,1)S(1)} %slice.168.refs_8_), channel_id=1, source_target_pairs={{0,16},{8,24},{16,0},{24,8},{1,17},{9,25},{17,1},{25,9},{2,18},{10... | collective-permute-start | bytes 393224 | tf_op jit(solution)/shard_map/ppermute | solution.py:354
  122.8 5.4 %backward.6 = (f32[4,32,2560]{2,1,0:T(8,128)S(1)}, f32[4,32,2560]{2,1,0:T(8,128)S(1)}) custom-call(bf16[2,64,1024]{2,1,0:T(8,128)(2,1)S(1)} %get-tuple-element.124.refs_7_.refs_0_, bf16[2,64,1024]{2,1,0:T(8,128)(2,1)S(1)} %collective-permute-done.26.refs_1_, bf16[2,64,1024]{2,1,0:T(8,128)(2,1)S(1)} %collective-permute-done.27.refs_2_, ...), custom_call_target="tpu_custom_call" | custom-call | flops 10000000000 | bytes 100000000 | tf_op jit(solution)/shard_map/backward/pallas_call | solution.py:516
  129.8 5.5 %backward.7 = (f32[4,32,2560]{2,1,0:T(8,128)S(1)}, f32[4,32,2560]{2,1,0:T(8,128)S(1)}) custom-call(bf16[2,64,1024]{2,1,0:T(8,128)(2,1)S(1)} %get-tuple-element.123.refs_8_.refs_0_, bf16[2,64,1024]{2,1,0:T(8,128)(2,1)S(1)} %collective-permute-done.30.refs_1_, bf16[2,64,1024]{2,1,0:T(8,128)(2,1)S(1)} %collective-permute-done.31.refs_2_, ...), custom_call_target="tpu_custom_call" | custom-call | flops 10000000000 | bytes 100000000 | tf_op jit(solution)/shard_map/backward/pallas_call | solution.py:516
  135.4 6.6 %backward.8 = (f32[4,32,2560]{2,1,0:T(8,128)S(1)}, f32[4,32,2560]{2,1,0:T(8,128)S(1)}) custom-call(bf16[2,64,1280]{2,1,0:T(8,128)(2,1)S(1)} %fusion.5.refs_0_, bf16[2,64,1280]{2,1,0:T(8,128)(2,1)S(1)} %collective-permute-done.24.refs_1_, bf16[2,64,1280]{2,1,0:T(8,128)(2,1)S(1)} %collective-permute-done.25.refs_2_, ...), custom_call_target="tpu_custom_call" | custom-call | flops 10000000000 | bytes 100000000 | tf_op jit(solution)/shard_map/backward/pallas_call | solution.py:516
  142.1 3.0 %collective-permute-done.36 = f32[4,32,2560]{2,1,0:T(8,128)S(1)} collective-permute-done((f32[4,32,2560]{2,1,0:T(8,128)S(1)}, f32[4,32,2560]{2,1,0:T(8,128)S(1)}, u32[]{:S(2)}, u32[]{:S(2)}) %collective-permute-start.36) | collective-permute-done | bytes 1310752 | tf_op jit(solution)/shard_map/ppermute | solution.py:575
  145.4 2.6 %collective-permute-start.39 = (bf16[32,2560]{1,0:T(8,128)(2,1)S(1)}, bf16[32,2560]{1,0:T(8,128)(2,1)S(1)}, u32[]{:S(2)}, u32[]{:S(2)}) collective-permute-start(bf16[32,2560]{1,0:T(8,128)(2,1)S(1)} %get-tuple-element.115.refs_9_), channel_id=1, source_target_pairs={{0,6},{1,7},{2,4},{3,5},{4,2},{5,3},{6,0},{7,1},{8,14},{9,15},{10,... | collective-permute-start | bytes 491528 | tf_op jit(solution)/shard_map/ppermute | solution.py:575
  148.9 5.2 %backward.9 = (bf16[2560,3328]{1,0:T(8,128)(2,1)}, bf16[2560,3328]{1,0:T(8,128)(2,1)}) custom-call(bf16[2,64,1024]{2,1,0:T(8,128)(2,1)S(1)} %get-tuple-element.124.refs_7_.refs_0_, bf16[2,64,1024]{2,1,0:T(8,128)(2,1)S(1)} %collective-permute-done.26.refs_1_, bf16[2,64,1024]{2,1,0:T(8,128)(2,1)S(1)} %collective-permute-done.27.refs_2_, ...), custom_call_target="tpu_custom_call" | custom-call | flops 10000000000 | bytes 100000000 | tf_op jit(solution)/shard_map/backward/pallas_call | solution.py:516
  154.0 5.2 %backward.10 = (bf16[2560,3328]{1,0:T(8,128)(2,1)}, bf16[2560,3328]{1,0:T(8,128)(2,1)}) custom-call(bf16[2,64,1024]{2,1,0:T(8,128)(2,1)S(1)} %get-tuple-element.123.refs_8_.refs_0_, bf16[2,64,1024]{2,1,0:T(8,128)(2,1)S(1)} %collective-permute-done.30.refs_1_, ...), custom_call_target="tpu_custom_call", output_to_operand_aliasing={{0}: (7, {}), {1}: (8, {})} | custom-call | flops 10000000000 | bytes 100000000 | tf_op jit(solution)/shard_map/backward/pallas_call | solution.py:516
  159.2 6.1 %backward.11 = (bf16[2560,3328]{1,0:T(8,128)(2,1)}, bf16[2560,3328]{1,0:T(8,128)(2,1)}) custom-call(bf16[2,64,1280]{2,1,0:T(8,128)(2,1)S(1)} %fusion.5.refs_0_, bf16[2,64,1280]{2,1,0:T(8,128)(2,1)S(1)} %collective-permute-done.24.refs_1_, bf16[2,64,1280]{2,1,0:T(8,128)(2,1)S(1)} %collective-permute-done.25.refs_2_, ...), custom_call_target="tpu_custom_call", output_to_operand_aliasing={{0}: (7, {}), {1}: (8, {})} | custom-call | flops 10000000000 | bytes 100000000 | tf_op jit(solution)/shard_map/backward/pallas_call | solution.py:516
  (149 shorter events, 37.2 us)
Async XLA Ops:
  0.6 18.3 %collective-permute-start.1 = (bf16[32,2560]{1,0:T(8,128)(2,1)}, bf16[32,2560]{1,0:T(8,128)(2,1)S(1)}, u32[]{:S(2)}, u32[]{:S(2)}) collective-permute-start(bf16[32,2560]{1,0:T(8,128)(2,1)} %param.8), channel_id=1, source_target_pairs={{0,4},{1,5},{2,6},{3,7},{4,0},{5,1},{6,2},{7,3},{8,12},{9,13},{10,... | collective-permute-start | bytes 491528 | tf_op jit(solution)/shard_map/ppermute | solution.py:575
  4.7 14.2 %collective-permute-start = (bf16[32,2560]{1,0:T(8,128)(2,1)}, bf16[32,2560]{1,0:T(8,128)(2,1)S(1)}, u32[]{:S(2)}, u32[]{:S(2)}) collective-permute-start(bf16[32,2560]{1,0:T(8,128)(2,1)} %param.8), channel_id=1, source_target_pairs={{0,2},{1,3},{2,0},{3,1},{4,6},{5,7},{6,4},{7,5},{8,10},{9,11},{10,... | collective-permute-start | bytes 491528 | tf_op jit(solution)/shard_map/ppermute | solution.py:575
  6.3 12.6 %collective-permute-start.2 = (bf16[32,2560]{1,0:T(8,128)(2,1)}, bf16[32,2560]{1,0:T(8,128)(2,1)S(1)}, u32[]{:S(2)}, u32[]{:S(2)}) collective-permute-start(bf16[32,2560]{1,0:T(8,128)(2,1)} %param.8), channel_id=1, source_target_pairs={{0,6},{1,7},{2,4},{3,5},{4,2},{5,3},{6,0},{7,1},{8,14},{9,15},{10,... | collective-permute-start | bytes 491528 | tf_op jit(solution)/shard_map/ppermute | solution.py:575
  28.5 15.9 %collective-permute-start.7 = (bf16[2,64,1536]{2,1,0:T(8,128)(2,1)S(1)}, bf16[2,64,1536]{2,1,0:T(8,128)(2,1)S(1)}, u32[]{:S(2)}, u32[]{:S(2)}) collective-permute-start(bf16[2,64,1536]{2,1,0:T(8,128)(2,1)S(1)} %get-tuple-element.66), channel_id=1, source_target_pairs={{0,8},{8,0},{16,24},{24,16},{1,9},{9,1},{17,25},{25,17},{2,10},{10... | collective-permute-start | bytes 1179656 | tf_op jit(solution)/shard_map/ppermute | solution.py:354
  30.3 14.7 %collective-permute-start.8 = (bf16[2,64,1536]{2,1,0:T(8,128)(2,1)S(1)}, bf16[2,64,1536]{2,1,0:T(8,128)(2,1)S(1)}, u32[]{:S(2)}, u32[]{:S(2)}) collective-permute-start(bf16[2,64,1536]{2,1,0:T(8,128)(2,1)S(1)} %get-tuple-element.67), channel_id=1, source_target_pairs={{0,16},{8,24},{16,0},{24,8},{1,17},{9,25},{17,1},{25,9},{2,18},{10... | collective-permute-start | bytes 1179656 | tf_op jit(solution)/shard_map/ppermute | solution.py:354
  40.0 13.2 %collective-permute-start.6 = (bf16[32,2560]{1,0:T(8,128)(2,1)S(1)}, bf16[32,2560]{1,0:T(8,128)(2,1)S(1)}, u32[]{:S(2)}, u32[]{:S(2)}) collective-permute-start(bf16[32,2560]{1,0:T(8,128)(2,1)S(1)} %copy-done.8), channel_id=1, source_target_pairs={{0,6},{1,7},{2,4},{3,5},{4,2},{5,3},{6,0},{7,1},{8,14},{9,15},{10,... | collective-permute-start | bytes 491528 | tf_op jit(solution)/shard_map/ppermute | solution.py:575
  43.6 14.0 %collective-permute-start.5 = (bf16[32,2560]{1,0:T(8,128)(2,1)S(1)}, bf16[32,2560]{1,0:T(8,128)(2,1)S(1)}, u32[]{:S(2)}, u32[]{:S(2)}) collective-permute-start(bf16[32,2560]{1,0:T(8,128)(2,1)S(1)} %copy-done.8), channel_id=1, source_target_pairs={{0,4},{1,5},{2,6},{3,7},{4,0},{5,1},{6,2},{7,3},{8,12},{9,13},{10,... | collective-permute-start | bytes 491528 | tf_op jit(solution)/shard_map/ppermute | solution.py:575
  43.6 14.0 %collective-permute-start.4 = (bf16[32,2560]{1,0:T(8,128)(2,1)S(1)}, bf16[32,2560]{1,0:T(8,128)(2,1)S(1)}, u32[]{:S(2)}, u32[]{:S(2)}) collective-permute-start(bf16[32,2560]{1,0:T(8,128)(2,1)S(1)} %copy-done.8), channel_id=1, source_target_pairs={{0,2},{1,3},{2,0},{3,1},{4,6},{5,7},{6,4},{7,5},{8,10},{9,11},{10,... | collective-permute-start | bytes 491528 | tf_op jit(solution)/shard_map/ppermute | solution.py:575
  44.4 13.6 %collective-permute-start.10 = (bf16[2,64,1792]{2,1,0:T(8,128)(2,1)S(1)}, bf16[2,64,1792]{2,1,0:T(8,128)(2,1)S(1)}, u32[]{:S(2)}, u32[]{:S(2)}) collective-permute-start(bf16[2,64,1792]{2,1,0:T(8,128)(2,1)S(1)} %get-tuple-element.76), channel_id=1, source_target_pairs={{0,8},{8,0},{16,24},{24,16},{1,9},{9,1},{17,25},{25,17},{2,10},{10... | collective-permute-start | bytes 1376264 | tf_op jit(solution)/shard_map/ppermute | solution.py:354
  45.0 13.1 %collective-permute-start.11 = (bf16[2,64,1792]{2,1,0:T(8,128)(2,1)S(1)}, bf16[2,64,1792]{2,1,0:T(8,128)(2,1)S(1)}, u32[]{:S(2)}, u32[]{:S(2)}) collective-permute-start(bf16[2,64,1792]{2,1,0:T(8,128)(2,1)S(1)} %get-tuple-element.77), channel_id=1, source_target_pairs={{0,16},{8,24},{16,0},{24,8},{1,17},{9,25},{17,1},{25,9},{2,18},{10... | collective-permute-start | bytes 1376264 | tf_op jit(solution)/shard_map/ppermute | solution.py:354
  58.2 14.5 %collective-permute-start.18 = (bf16[2,32,3328]{2,1,0:T(8,128)(2,1)S(1)}, bf16[2,32,3328]{2,1,0:T(8,128)(2,1)S(1)}, u32[]{:S(2)}, u32[]{:S(2)}) collective-permute-start(bf16[2,32,3328]{2,1,0:T(8,128)(2,1)S(1)} %pad_maximum_fusion.4.refs_0_), channel_id=1, source_target_pairs={{0,8},{8,0},{16,24},{24,16},{1,9},{9,1},{17,25},{25,17},{2,10},{10... | collective-permute-start | bytes 1277960 | tf_op jit(solution)/shard_map/ppermute | solution.py:354
  58.9 13.9 %collective-permute-start.19 = (bf16[2,32,3328]{2,1,0:T(8,128)(2,1)S(1)}, bf16[2,32,3328]{2,1,0:T(8,128)(2,1)S(1)}, u32[]{:S(2)}, u32[]{:S(2)}) collective-permute-start(bf16[2,32,3328]{2,1,0:T(8,128)(2,1)S(1)} %pad_maximum_fusion.5.refs_1_), channel_id=1, source_target_pairs={{0,16},{8,24},{16,0},{24,8},{1,17},{9,25},{17,1},{25,9},{2,18},{10... | collective-permute-start | bytes 1277960 | tf_op jit(solution)/shard_map/ppermute | solution.py:354
  66.0 11.5 %collective-permute-start.13 = (bf16[1,64,1536]{2,1,0:T(8,128)(2,1)S(1)}, bf16[1,64,1536]{2,1,0:T(8,128)(2,1)S(1)}, u32[]{:S(2)}, u32[]{:S(2)}) collective-permute-start(bf16[1,64,1536]{2,1,0:T(8,128)(2,1)S(1)} %get-tuple-element.82), channel_id=1, source_target_pairs={{0,16},{8,24},{16,0},{24,8},{1,17},{9,25},{17,1},{25,9},{2,18},{10... | collective-permute-start | bytes 589832 | tf_op jit(solution)/shard_map/ppermute | solution.py:354
  73.3 18.6 %collective-permute-start.21 = (bf16[1,64,3328]{2,1,0:T(8,128)(2,1)S(1)}, bf16[1,64,3328]{2,1,0:T(8,128)(2,1)S(1)}, u32[]{:S(2)}, u32[]{:S(2)}) collective-permute-start(bf16[1,64,3328]{2,1,0:T(8,128)(2,1)S(1)} %fusion.4.refs_0_), channel_id=1, source_target_pairs={{0,16},{8,24},{16,0},{24,8},{1,17},{9,25},{17,1},{25,9},{2,18},{10... | collective-permute-start | bytes 1277960 | tf_op jit(solution)/shard_map/ppermute | solution.py:354
  73.9 19.6 %collective-permute-start.20 = (bf16[1,64,3328]{2,1,0:T(8,128)(2,1)S(1)}, bf16[1,64,3328]{2,1,0:T(8,128)(2,1)S(1)}, u32[]{:S(2)}, u32[]{:S(2)}) collective-permute-start(bf16[1,64,3328]{2,1,0:T(8,128)(2,1)S(1)} %fusion.4.refs_0_), channel_id=1, source_target_pairs={{0,8},{8,0},{16,24},{24,16},{1,9},{9,1},{17,25},{25,17},{2,10},{10... | collective-permute-start | bytes 1277960 | tf_op jit(solution)/shard_map/ppermute | solution.py:354
  74.9 14.8 %collective-permute-start.14 = (bf16[1,64,1792]{2,1,0:T(8,128)(2,1)S(1)}, bf16[1,64,1792]{2,1,0:T(8,128)(2,1)S(1)}, u32[]{:S(2)}, u32[]{:S(2)}) collective-permute-start(bf16[1,64,1792]{2,1,0:T(8,128)(2,1)S(1)} %get-tuple-element.85), channel_id=1, source_target_pairs={{0,8},{8,0},{16,24},{24,16},{1,9},{9,1},{17,25},{25,17},{2,10},{10... | collective-permute-start | bytes 688136 | tf_op jit(solution)/shard_map/ppermute | solution.py:354
  75.9 13.7 %collective-permute-start.16 = (bf16[1,64,1792]{2,1,0:T(8,128)(2,1)S(1)}, bf16[1,64,1792]{2,1,0:T(8,128)(2,1)S(1)}, u32[]{:S(2)}, u32[]{:S(2)}) collective-permute-start(bf16[1,64,1792]{2,1,0:T(8,128)(2,1)S(1)} %get-tuple-element.89), channel_id=1, source_target_pairs={{0,16},{8,24},{16,0},{24,8},{1,17},{9,25},{17,1},{25,9},{2,18},{10... | collective-permute-start | bytes 688136 | tf_op jit(solution)/shard_map/ppermute | solution.py:354
  92.0 12.0 %collective-permute-start.23 = (bf16[1,32,3328]{2,1,0:T(8,128)(2,1)S(1)}, bf16[1,32,3328]{2,1,0:T(8,128)(2,1)S(1)}, u32[]{:S(2)}, u32[]{:S(2)}) collective-permute-start(bf16[1,32,3328]{2,1,0:T(8,128)(2,1)S(1)} %slice.179), channel_id=1, source_target_pairs={{0,8},{8,0},{16,24},{24,16},{1,9},{9,1},{17,25},{25,17},{2,10},{10... | collective-permute-start | bytes 638984 | tf_op jit(solution)/shard_map/ppermute | solution.py:354
  99.9 18.7 %collective-permute-start.31 = (bf16[2,64,1024]{2,1,0:T(8,128)(2,1)S(1)}, bf16[2,64,1024]{2,1,0:T(8,128)(2,1)S(1)}, u32[]{:S(2)}, u32[]{:S(2)}) collective-permute-start(bf16[2,64,1024]{2,1,0:T(8,128)(2,1)S(1)} %get-tuple-element.123.refs_8_.refs_0_), channel_id=1, source_target_pairs={{0,16},{8,24},{16,0},{24,8},{1,17},{9,25},{17,1},{25,9},{2,18},{10... | collective-permute-start | bytes 786440 | tf_op jit(solution)/shard_map/ppermute | solution.py:354
  100.3 18.4 %collective-permute-start.30 = (bf16[2,64,1024]{2,1,0:T(8,128)(2,1)S(1)}, bf16[2,64,1024]{2,1,0:T(8,128)(2,1)S(1)}, u32[]{:S(2)}, u32[]{:S(2)}) collective-permute-start(bf16[2,64,1024]{2,1,0:T(8,128)(2,1)S(1)} %get-tuple-element.123.refs_8_.refs_0_), channel_id=1, source_target_pairs={{0,8},{8,0},{16,24},{24,16},{1,9},{9,1},{17,25},{25,17},{2,10},{10... | collective-permute-start | bytes 786440 | tf_op jit(solution)/shard_map/ppermute | solution.py:354
  101.9 12.6 %collective-permute-start.27 = (bf16[2,64,1024]{2,1,0:T(8,128)(2,1)S(1)}, bf16[2,64,1024]{2,1,0:T(8,128)(2,1)S(1)}, u32[]{:S(2)}, u32[]{:S(2)}) collective-permute-start(bf16[2,64,1024]{2,1,0:T(8,128)(2,1)S(1)} %get-tuple-element.124.refs_7_.refs_0_), channel_id=1, source_target_pairs={{0,16},{8,24},{16,0},{24,8},{1,17},{9,25},{17,1},{25,9},{2,18},{10... | collective-permute-start | bytes 786440 | tf_op jit(solution)/shard_map/ppermute | solution.py:354
  145.3 20.0 %collective-permute-start.37 = (bf16[32,2560]{1,0:T(8,128)(2,1)S(1)}, bf16[32,2560]{1,0:T(8,128)(2,1)S(1)}, u32[]{:S(2)}, u32[]{:S(2)}) collective-permute-start(bf16[32,2560]{1,0:T(8,128)(2,1)S(1)} %get-tuple-element.114.refs_7_), channel_id=1, source_target_pairs={{0,2},{1,3},{2,0},{3,1},{4,6},{5,7},{6,4},{7,5},{8,10},{9,11},{10,... | collective-permute-start | bytes 491528 | tf_op jit(solution)/shard_map/ppermute | solution.py:575
  145.4 19.9 %collective-permute-start.39 = (bf16[32,2560]{1,0:T(8,128)(2,1)S(1)}, bf16[32,2560]{1,0:T(8,128)(2,1)S(1)}, u32[]{:S(2)}, u32[]{:S(2)}) collective-permute-start(bf16[32,2560]{1,0:T(8,128)(2,1)S(1)} %get-tuple-element.115.refs_9_), channel_id=1, source_target_pairs={{0,6},{1,7},{2,4},{3,5},{4,2},{5,3},{6,0},{7,1},{8,14},{9,15},{10,... | collective-permute-start | bytes 491528 | tf_op jit(solution)/shard_map/ppermute | solution.py:575
  148.0 17.3 %collective-permute-start.38 = (bf16[32,2560]{1,0:T(8,128)(2,1)S(1)}, bf16[32,2560]{1,0:T(8,128)(2,1)S(1)}, u32[]{:S(2)}, u32[]{:S(2)}) collective-permute-start(bf16[32,2560]{1,0:T(8,128)(2,1)S(1)} %get-tuple-element.116.refs_8_), channel_id=1, source_target_pairs={{0,4},{1,5},{2,6},{3,7},{4,0},{5,1},{6,2},{7,3},{8,12},{9,13},{10,... | collective-permute-start | bytes 491528 | tf_op jit(solution)/shard_map/ppermute | solution.py:575
  (25 other events, 283.5 us)

commit v3 on v2

--- a/solution.py
+++ b/solution.py
@@ -15,8 +15,7 @@
 HBM = pl.BlockSpec(memory_space=pltpu.HBM)
 WHOLE = pl.BlockSpec(memory_space=pltpu.VMEM)
 GATE_UP_CUTS = (6, 13)
-BACK_CUTS = (6, 13)
-GRAD_CUTS = (4, 8, 13)
+BACK_CUTS = (4, 13)
 
 
 def expand_mask(block_ids):
@@ -602,7 +601,7 @@
     tok = order_groups(tok_mine, tok_theirs, order)
     gate_up = lambda c, after: gate_up_sums(tok, gate_weight, up_weight, gate_up_bits, *c, after=after)
     back = lambda c, after: back_sums(grads, down_weight, down_bits, *c, after=after)
-    gate_up_red, back_red = Reduction(), Reduction()
+    gate_up_red, back_red = Reduction(), [Reduction(), Reduction()]
 
     cuts = chunks_of(tiles, GATE_UP_CUTS)
     sums0 = gate_up(cuts[0], [])
@@ -620,47 +619,47 @@
     grads = order_groups(grad_mine, grad_theirs, order)
     cuts = chunks_of(tiles, BACK_CUTS)
     sums0 = back(cuts[0], [gate_up_red.mixed_x, gate_up_red.mixed_y])
-    back_red.first(sums0)
+    back_red[0].first(sums0)
     sums1 = back(cuts[1], [sums0[0]])
-    back_red.hold_first(sums1[0])
+    back_red[0].hold_first(sums1[0])
+    sums1 = _hold(sums1, back_red[0].received[0])
     gate_up_red.hold_second(sums1[0])
-    back_red.first(sums1)
+    back_red[0].mixed()
+    back_red[0].second()
+    back_red[1].first(sums1)
     gate_up_total = gate_up_red.total()
     hidden = Gathering(swiglu(*gate_up_total)[None])
     gate_up_total = _hold(gate_up_total, hidden.block)
-    hidden.first()
-    hidden.cut()
-    hidden.second()
-    back_red.mixed()
-    back_red.second()
-    block = swiglu_back(*gate_up_total, *back_red.total())
-    chunks = chunks_of(tiles, GRAD_CUTS)
-    gath = [Gathering(block[:, :, a * TILE : (a + n) * TILE]) for a, n in chunks]
+    split = cuts[1][0] * TILE
+    gath = [Gathering(swiglu_back(*gate_up_total[:, :, :split], *back_red[0].total()))]
     gath[0].first()
-    gath[1].first()
-    down_out = down_grad(hidden.blocks, grads, down_bits, [gath[0].block, gath[1].block])
-    gath[0].hold_first(down_out)
-    gath[1].hold_first(down_out)
+    back_red[1].hold_first(gath[0].block)
+    back_red[1].mixed()
+    back_red[1].second()
+    gath[0].hold_first(back_red[1].mixed_x)
     gath[0].cut()
     gath[0].second()
+    gath.append(Gathering(swiglu_back(*gate_up_total[:, :, split:], *back_red[1].total())))
+    gath[1].first()
+    pair = (gate_weight, up_weight)
+    acc = backward(gath[0].blocks, gate_up_bits, *cuts[0], inputs=(*pair, None), after=[gath[1].block])
+    gath[1].hold_first(acc[0])
     gath[1].cut()
     gath[1].second()
-    gath[2].block = _hold(gath[2].block, down_out)
-    gath[2].first()
-    pair = (gate_weight, up_weight)
-    acc = backward(gath[0].blocks, gate_up_bits, *chunks[0], inputs=(*pair, None), after=[gath[1].cut_x, gath[1].cut_y])
-    gath[2].hold_first(acc[0])
-    gath[2].cut()
-    gath[2].second()
-    acc = backward(gath[1].blocks, gate_up_bits, *chunks[1], inputs=(*pair, acc), after=[gath[2].cut_x, gath[2].cut_y])
-    acc = backward(gath[2].blocks, gate_up_bits, *chunks[2], inputs=(*pair, acc))
+    hidden.block = _hold(hidden.block, gath[1].blocks[3:])
+    hidden.first()
+    outs = backward(gath[0].blocks, gate_up_bits, *cuts[0], weights=(tok, None), after=[gath[1].cut_x, gath[1].cut_y])
+    acc = backward(gath[1].blocks, gate_up_bits, *cuts[1], inputs=(*pair, acc), after=[outs[0]])
+    hidden.hold_first(acc[0])
+    hidden.cut()
+    acc = _hold(acc, (hidden.cut_x, hidden.cut_y))
+    hidden.second()
     pairs = acc[0] + _col_swap(acc[1], 1)
     own = lax.dynamic_index_in_dim(pairs, order, 0, keepdims=False)
     sent = [lax.dynamic_index_in_dim(pairs, k ^ order, 0, keepdims=False).astype(BF16) for k in (1, 2, 3)]
     received = [_col_swap(value, 2 * k) for k, value in zip((1, 2, 3), sent)]
-    outs = backward(gath[0].blocks, gate_up_bits, *chunks[0], weights=(tok, None), after=sent)
-    outs = backward(gath[1].blocks, gate_up_bits, *chunks[1], weights=(tok, outs))
-    outs = backward(gath[2].blocks, gate_up_bits, *chunks[2], weights=(tok, outs))
+    outs = backward(gath[1].blocks, gate_up_bits, *cuts[1], weights=(tok, outs), after=sent)
+    down_out = down_grad(hidden.blocks, grads, down_bits, [outs[0]])
     for value in received:
         own = own + value
     return (own.astype(BF16), *outs, down_out)

time: 166 us -> 161 us (0.970)
  waiting for transfers between devices: 28.8 us -> 21.3 us
  starting transfers between devices: 42.1 us -> 47.3 us
  Pallas kernels: 86.3 us -> 83.4 us
    ppermute x28 -> x26, waiting for transfers between devices: 19.4 us -> 13.8 us  [_swap(): return lax.ppermute(value, 'row', [(i, i ^ bit) for i in range(4)])]
    ppermute x28 -> x26, starting transfers between devices: 28.2 us -> 32 us  [_swap(): return lax.ppermute(value, 'row', [(i, i ^ bit) for i in range(4)])]
    pallas_call x6 -> x4, Pallas kernels: 34 us -> 30.8 us  [backward(): pl.pallas_call(functools.partial(_backward_kernel, first, count, inputs i...]
    ppermute x12, waiting for transfers between devices: 9.44 us -> 7.5 us  [_col_swap(): return lax.ppermute(value, 'col', [(i, i ^ bits) for i in range(8)])]
    unnamed x32 -> x28, local copies, waits for them, and re-layouts: 3.5 us -> 3.49 us
  transfers between devices with their start and end apart: 40 -> 38, of which waited for: 9 -> 15; matrix products, arithmetic and copies ran while one was open for 2% -> 2% of each run, Pallas kernels for 44% -> 47%
where the time goes in v3:
time: 161 us
  Pallas kernels  83.4 us (52%)
  starting transfers between devices  47.3 us (29%)
  waiting for transfers between devices  21.3 us (13%)
  other arithmetic  3.69 us (2%)
  local copies, waits for them, and re-layouts  3.68 us (2%)
    ppermute x26, starting transfers between devices, _swap(): return lax.ppermute(value, 'row', [(i, i ^ bit) for i in range(4)])  32 us
    pallas_call x4, Pallas kernels, backward(): pl.pallas_call(functools.partial(_backward_kernel, first, count, inputs i...  30.8 us
    ppermute x12, starting transfers between devices, _col_swap(): return lax.ppermute(value, 'col', [(i, i ^ bits) for i in range(8)])  15.3 us
    pallas_call x2, Pallas kernels, gate_up_sums(): pl.pallas_call(functools.partial(_gate_up_kernel, first, count, len(after...  15.2 us
    ppermute x26, waiting for transfers between devices, _swap(): return lax.ppermute(value, 'row', [(i, i ^ bit) for i in range(4)])  13.8 us
    pallas_call x1, Pallas kernels, down_grad(): pl.pallas_call(functools.partial(_down_grad_kernel, count, len(after)), i...  10.4 us
    pallas_call x2, Pallas kernels, back_sums(): pl.pallas_call(functools.partial(_back_kernel, first, count, len(after)),...  10.2 us
    pallas_call x1, Pallas kernels, pack_gate_up(): pl.pallas_call(_pack_rows_kernel, grid=(pl.cdiv(code_cols, 128),), in_spe...  8.86 us
  transfers between devices with their start and end apart: 38, of which 15 were waited for; matrix products, arithmetic and copies ran while one was open for 2% of the time, Pallas kernels for 47%

profile of v3, /device:TPU:0, one launch (start us, length us, event | category | flops | bytes accessed | tf_op | source)
XLA Modules:
  0.0 160.7 jit_solution(2101844621053058862)
XLA Ops:
  0.6 3.1 %collective-permute-start = (bf16[32,2560]{1,0:T(8,128)(2,1)}, bf16[32,2560]{1,0:T(8,128)(2,1)S(1)}, u32[]{:S(2)}, u32[]{:S(2)}) collective-permute-start(bf16[32,2560]{1,0:T(8,128)(2,1)} %param.8), channel_id=1, source_target_pairs={{0,2},{1,3},{2,0},{3,1},{4,6},{5,7},{6,4},{7,5},{8,10},{9,11},{10,... | collective-permute-start | bytes 491528 | tf_op jit(solution)/shard_map/ppermute | solution.py:574
  3.7 2.6 %collective-permute-start.1 = (bf16[32,2560]{1,0:T(8,128)(2,1)}, bf16[32,2560]{1,0:T(8,128)(2,1)S(1)}, u32[]{:S(2)}, u32[]{:S(2)}) collective-permute-start(bf16[32,2560]{1,0:T(8,128)(2,1)} %param.8), channel_id=1, source_target_pairs={{0,4},{1,5},{2,6},{3,7},{4,0},{5,1},{6,2},{7,3},{8,12},{9,13},{10,... | collective-permute-start | bytes 491528 | tf_op jit(solution)/shard_map/ppermute | solution.py:574
  10.0 8.9 %pack_gate_up.1.bits_any.refs_5_ = s8[640,3328]{1,0:T(32,128)(4,1)S(1)} custom-call(s32[832,640]{1,0:T(8,128)S(1)} %bitcast.56, s32[832,640]{1,0:T(8,128)S(1)} %bitcast.57, bf16[512,512]{1,0:T(8,128)(2,1)S(1)} %fusion.lane_ref, bf16[128,64]{1,0:T(8,128)(2,1)S(1)} %select_convert_fusion.1.row_ref), custom_call_target="tpu_custom_call" | custom-call | flops 10000000000 | bytes 100000000 | tf_op jit(solution)/shard_map/pack_gate_up/pallas_call | solution.py:186
  21.4 7.1 %gate_up_sums.2 = (f32[2,64,1536]{2,1,0:T(8,128)S(1)}, bf16[2,64,1536]{2,1,0:T(8,128)(2,1)S(1)}, bf16[2,64,1536]{2,1,0:T(8,128)(2,1)S(1)}, f32[2,64,1536]{2,1,0:T(8,128)S(1)}) custom-call(bf16[256,2560]{1,0:T(8,128)(2,1)S(1)} %bitcast_dynamic-update-slice_fusion.8.tok_ref.refs_6_, bf16[2560,3328]{1,0:T(8,128)(2,1)} %refs_6_.3, bf16[2560,3328]{1,0:T(8,128)(2,1)} %refs_7_.3, ...), custom_call_target="tpu_custom_call" | custom-call | flops 10000000000 | bytes 100000000 | tf_op jit(solution)/shard_map/gate_up_sums/pallas_call | solution.py:325
  28.5 1.7 %collective-permute-start.7 = (bf16[2,64,1536]{2,1,0:T(8,128)(2,1)S(1)}, bf16[2,64,1536]{2,1,0:T(8,128)(2,1)S(1)}, u32[]{:S(2)}, u32[]{:S(2)}) collective-permute-start(bf16[2,64,1536]{2,1,0:T(8,128)(2,1)S(1)} %get-tuple-element.70), channel_id=1, source_target_pairs={{0,8},{8,0},{16,24},{24,16},{1,9},{9,1},{17,25},{25,17},{2,10},{10... | collective-permute-start | bytes 1179656 | tf_op jit(solution)/shard_map/ppermute | solution.py:353
  31.8 8.1 %gate_up_sums.3 = (f32[2,64,1792]{2,1,0:T(8,128)S(1)}, bf16[2,64,1792]{2,1,0:T(8,128)(2,1)S(1)}, bf16[2,64,1792]{2,1,0:T(8,128)(2,1)S(1)}, f32[2,64,1792]{2,1,0:T(8,128)S(1)}) custom-call(bf16[256,2560]{1,0:T(8,128)(2,1)S(1)} %bitcast_dynamic-update-slice_fusion.8.tok_ref.refs_6_, bf16[2560,3328]{1,0:T(8,128)(2,1)} %refs_6_.3, bf16[2560,3328]{1,0:T(8,128)(2,1)} %refs_7_.3, ...), custom_call_target="tpu_custom_call" | custom-call | flops 10000000000 | bytes 100000000 | tf_op jit(solution)/shard_map/gate_up_sums/pallas_call | solution.py:325
  40.0 2.5 %collective-permute-start.4 = (bf16[32,2560]{1,0:T(8,128)(2,1)S(1)}, bf16[32,2560]{1,0:T(8,128)(2,1)S(1)}, u32[]{:S(2)}, u32[]{:S(2)}) collective-permute-start(bf16[32,2560]{1,0:T(8,128)(2,1)S(1)} %copy-done.6), channel_id=1, source_target_pairs={{0,2},{1,3},{2,0},{3,1},{4,6},{5,7},{6,4},{7,5},{8,10},{9,11},{10,... | collective-permute-start | bytes 491528 | tf_op jit(solution)/shard_map/ppermute | solution.py:574
  46.0 7.8 %pack_down.1.bits_any.refs_6_ = s8[3328,512]{1,0:T(32,128)(4,1)S(1)} custom-call(s32[832,640]{1,0:T(8,128)S(1)} %copy-done.4, bf16[512,512]{1,0:T(8,128)(2,1)S(1)} %fusion.lane_ref, bf16[256,128]{1,0:T(8,128)(2,1)S(1)} %select_convert_fusion.row_ref, f32[2,64,1792]{2,1,0:T(8,128)S(1)} %get-tuple-element.68.refs_0_, ...), custom_call_target="tpu_custom_call" | custom-call | flops 10000000000 | bytes 100000000 | tf_op jit(solution)/shard_map/pack_down/pallas_call | solution.py:204
  53.8 3.7 %collective-permute-done.5 = bf16[32,2560]{1,0:T(8,128)(2,1)S(1)} collective-permute-done((bf16[32,2560]{1,0:T(8,128)(2,1)S(1)}, bf16[32,2560]{1,0:T(8,128)(2,1)S(1)}, u32[]{:S(2)}, u32[]{:S(2)}) %collective-permute-start.5) | collective-permute-done | bytes 163872 | tf_op jit(solution)/shard_map/ppermute | solution.py:574
  60.0 3.6 %back_sums.2 = (f32[1,64,1024]{2,1,0:T(8,128)S(1)}, bf16[1,64,1024]{2,1,0:T(8,128)(2,1)S(1)}, bf16[1,64,1024]{2,1,0:T(8,128)(2,1)S(1)}, f32[1,64,1024]{2,1,0:T(8,128)S(1)}) custom-call(bf16[256,2560]{1,0:T(8,128)(2,1)S(1)} %bitcast_dynamic-update-slice_fusion.grad_ref.refs_5_, bf16[3328,2560]{1,0:T(8,128)(2,1)} %down_any.3, ...), custom_call_target="tpu_custom_call" | custom-call | flops 10000000000 | bytes 100000000 | tf_op jit(solution)/shard_map/back_sums/pallas_call | solution.py:340
  66.3 6.6 %back_sums.3 = (f32[1,64,2304]{2,1,0:T(8,128)S(1)}, bf16[1,64,2304]{2,1,0:T(8,128)(2,1)S(1)}, bf16[1,64,2304]{2,1,0:T(8,128)(2,1)S(1)}, f32[1,64,2304]{2,1,0:T(8,128)S(1)}) custom-call(bf16[256,2560]{1,0:T(8,128)(2,1)S(1)} %bitcast_dynamic-update-slice_fusion.grad_ref.refs_5_, bf16[3328,2560]{1,0:T(8,128)(2,1)} %down_any.3, ...), custom_call_target="tpu_custom_call" | custom-call | flops 10000000000 | bytes 100000000 | tf_op jit(solution)/shard_map/back_sums/pallas_call | solution.py:340
  82.5 3.7 %collective-permute-done.14 = bf16[1,64,2304]{2,1,0:T(8,128)(2,1)S(1)} collective-permute-done((bf16[1,64,2304]{2,1,0:T(8,128)(2,1)S(1)}, bf16[1,64,2304]{2,1,0:T(8,128)(2,1)S(1)}, u32[]{:S(2)}, u32[]{:S(2)}) %collective-permute-start.14) | collective-permute-done | bytes 294944 | tf_op jit(solution)/shard_map/ppermute | solution.py:353
  89.9 2.0 %collective-permute-done.24.refs_1_ = bf16[2,64,1024]{2,1,0:T(8,128)(2,1)S(1)} collective-permute-done((bf16[2,64,1024]{2,1,0:T(8,128)(2,1)S(1)}, bf16[2,64,1024]{2,1,0:T(8,128)(2,1)S(1)}, u32[]{:S(2)}, u32[]{:S(2)}) %collective-permute-start.24) | collective-permute-done | bytes 262176 | tf_op jit(solution)/shard_map/ppermute | solution.py:353
  93.5 2.1 %collective-permute-start.27 = (bf16[2,32,1024]{2,1,0:T(8,128)(2,1)S(1)}, bf16[2,32,1024]{2,1,0:T(8,128)(2,1)S(1)}, u32[]{:S(2)}, u32[]{:S(2)}) collective-permute-start(bf16[2,32,1024]{2,1,0:T(8,128)(2,1)S(1)} %slice.153), channel_id=1, source_target_pairs={{0,8},{8,0},{16,24},{24,16},{1,9},{9,1},{17,25},{25,17},{2,10},{10... | collective-permute-start | bytes 393224 | tf_op jit(solution)/shard_map/ppermute | solution.py:353
  100.0 5.4 %backward.4 = (f32[4,32,2560]{2,1,0:T(8,128)S(1)}, f32[4,32,2560]{2,1,0:T(8,128)S(1)}) custom-call(bf16[2,64,1024]{2,1,0:T(8,128)(2,1)S(1)} %pad_maximum_fusion.8.refs_0_, bf16[2,64,1024]{2,1,0:T(8,128)(2,1)S(1)} %collective-permute-done.24.refs_1_, bf16[2,64,1024]{2,1,0:T(8,128)(2,1)S(1)} %collective-permute-done.25.refs_2_, ...), custom_call_target="tpu_custom_call" | custom-call | flops 10000000000 | bytes 100000000 | tf_op jit(solution)/shard_map/backward/pallas_call | solution.py:515
  105.4 3.8 %collective-permute-done.22.refs_1_ = bf16[2,64,2304]{2,1,0:T(8,128)(2,1)S(1)} collective-permute-done((bf16[2,64,2304]{2,1,0:T(8,128)(2,1)S(1)}, bf16[2,64,2304]{2,1,0:T(8,128)(2,1)S(1)}, u32[]{:S(2)}, u32[]{:S(2)}) %collective-permute-start.22) | collective-permute-done | bytes 589856 | tf_op jit(solution)/shard_map/ppermute | solution.py:353
  112.8 5.2 %backward.5 = (bf16[2560,3328]{1,0:T(8,128)(2,1)}, bf16[2560,3328]{1,0:T(8,128)(2,1)}) custom-call(bf16[2,64,1024]{2,1,0:T(8,128)(2,1)S(1)} %pad_maximum_fusion.8.refs_0_, bf16[2,64,1024]{2,1,0:T(8,128)(2,1)S(1)} %collective-permute-done.24.refs_1_, bf16[2,64,1024]{2,1,0:T(8,128)(2,1)S(1)} %collective-permute-done.25.refs_2_, ...), custom_call_target="tpu_custom_call" | custom-call | flops 10000000000 | bytes 100000000 | tf_op jit(solution)/shard_map/backward/pallas_call | solution.py:515
  118.1 2.4 %collective-permute-start.30 = (bf16[1,64,3328]{2,1,0:T(8,128)(2,1)S(1)}, bf16[1,64,3328]{2,1,0:T(8,128)(2,1)S(1)}, u32[]{:S(2)}, u32[]{:S(2)}) collective-permute-start(bf16[1,64,3328]{2,1,0:T(8,128)(2,1)S(1)} %fusion.4.refs_0_), channel_id=1, source_target_pairs={{0,8},{8,0},{16,24},{24,16},{1,9},{9,1},{17,25},{25,17},{2,10},{10... | collective-permute-start | bytes 1277960 | tf_op jit(solution)/shard_map/ppermute | solution.py:353
  121.4 10.4 %backward.6 = (f32[4,32,2560]{2,1,0:T(8,128)S(1)}, f32[4,32,2560]{2,1,0:T(8,128)S(1)}) custom-call(bf16[2,64,2304]{2,1,0:T(8,128)(2,1)S(1)} %pad_maximum_fusion.4.refs_8_.refs_0_, bf16[2,64,2304]{2,1,0:T(8,128)(2,1)S(1)} %collective-permute-done.22.refs_1_, bf16[2,64,2304]{2,1,0:T(8,128)(2,1)S(1)} %collective-permute-done.23.refs_2_, ...), custom_call_target="tpu_custom_call" | custom-call | flops 10000000000 | bytes 100000000 | tf_op jit(solution)/shard_map/backward/pallas_call | solution.py:515
  133.2 1.8 %collective-permute-done.32 = f32[4,32,2560]{2,1,0:T(8,128)S(1)} collective-permute-done((f32[4,32,2560]{2,1,0:T(8,128)S(1)}, f32[4,32,2560]{2,1,0:T(8,128)S(1)}, u32[]{:S(2)}, u32[]{:S(2)}) %collective-permute-start.32) | collective-permute-done | bytes 1310752 | tf_op jit(solution)/shard_map/ppermute | solution.py:574
  135.3 2.0 %collective-permute-start.35 = (bf16[32,2560]{1,0:T(8,128)(2,1)S(1)}, bf16[32,2560]{1,0:T(8,128)(2,1)S(1)}, u32[]{:S(2)}, u32[]{:S(2)}) collective-permute-start(bf16[32,2560]{1,0:T(8,128)(2,1)S(1)} %get-tuple-element.125.refs_11_), channel_id=1, source_target_pairs={{0,6},{1,7},{2,4},{3,5},{4,2},{5,3},{6,0},{7,1},{8,14},{9,15},{10,... | collective-permute-start | bytes 491528 | tf_op jit(solution)/shard_map/ppermute | solution.py:574
  137.3 1.8 %collective-permute-start.34 = (bf16[32,2560]{1,0:T(8,128)(2,1)S(1)}, bf16[32,2560]{1,0:T(8,128)(2,1)S(1)}, u32[]{:S(2)}, u32[]{:S(2)}) collective-permute-start(bf16[32,2560]{1,0:T(8,128)(2,1)S(1)} %get-tuple-element.126.refs_10_), channel_id=1, source_target_pairs={{0,4},{1,5},{2,6},{3,7},{4,0},{5,1},{6,2},{7,3},{8,12},{9,13},{10,... | collective-permute-start | bytes 491528 | tf_op jit(solution)/shard_map/ppermute | solution.py:574
  139.7 9.7 %backward.7 = (bf16[2560,3328]{1,0:T(8,128)(2,1)}, bf16[2560,3328]{1,0:T(8,128)(2,1)}) custom-call(bf16[2,64,2304]{2,1,0:T(8,128)(2,1)S(1)} %pad_maximum_fusion.4.refs_8_.refs_0_, bf16[2,64,2304]{2,1,0:T(8,128)(2,1)S(1)} %collective-permute-done.22.refs_1_, ...), custom_call_target="tpu_custom_call", output_to_operand_aliasing={{0}: (7, {}), {1}: (8, {})} | custom-call | flops 10000000000 | bytes 100000000 | tf_op jit(solution)/shard_map/backward/pallas_call | solution.py:515
  149.5 10.4 %down_grad.1 = bf16[3328,2560]{1,0:T(8,128)(2,1)} custom-call(bf16[1,64,3328]{2,1,0:T(8,128)(2,1)S(1)} %fusion.4.refs_0_, bf16[1,64,3328]{2,1,0:T(8,128)(2,1)S(1)} %collective-permute-done.30.refs_1_, bf16[1,64,3328]{2,1,0:T(8,128)(2,1)S(1)} %collective-permute-done.31.refs_2_, bf16[1,32,3328]{2,1,0:T(8,128)(2,1)S(1)} %collective-permute-done.36.refs_3_, ...), custom_call_target="tpu_custom_call" | custom-call | flops 10000000000 | bytes 100000000 | tf_op jit(solution)/shard_map/down_grad/pallas_call | solution.py:561
  (136 shorter events, 42.7 us)
Async XLA Ops:
  0.6 18.3 %collective-permute-start = (bf16[32,2560]{1,0:T(8,128)(2,1)}, bf16[32,2560]{1,0:T(8,128)(2,1)S(1)}, u32[]{:S(2)}, u32[]{:S(2)}) collective-permute-start(bf16[32,2560]{1,0:T(8,128)(2,1)} %param.8), channel_id=1, source_target_pairs={{0,2},{1,3},{2,0},{3,1},{4,6},{5,7},{6,4},{7,5},{8,10},{9,11},{10,... | collective-permute-start | bytes 491528 | tf_op jit(solution)/shard_map/ppermute | solution.py:574
  3.7 15.3 %collective-permute-start.1 = (bf16[32,2560]{1,0:T(8,128)(2,1)}, bf16[32,2560]{1,0:T(8,128)(2,1)S(1)}, u32[]{:S(2)}, u32[]{:S(2)}) collective-permute-start(bf16[32,2560]{1,0:T(8,128)(2,1)} %param.8), channel_id=1, source_target_pairs={{0,4},{1,5},{2,6},{3,7},{4,0},{5,1},{6,2},{7,3},{8,12},{9,13},{10,... | collective-permute-start | bytes 491528 | tf_op jit(solution)/shard_map/ppermute | solution.py:574
  6.3 12.7 %collective-permute-start.2 = (bf16[32,2560]{1,0:T(8,128)(2,1)}, bf16[32,2560]{1,0:T(8,128)(2,1)S(1)}, u32[]{:S(2)}, u32[]{:S(2)}) collective-permute-start(bf16[32,2560]{1,0:T(8,128)(2,1)} %param.8), channel_id=1, source_target_pairs={{0,6},{1,7},{2,4},{3,5},{4,2},{5,3},{6,0},{7,1},{8,14},{9,15},{10,... | collective-permute-start | bytes 491528 | tf_op jit(solution)/shard_map/ppermute | solution.py:574
  28.5 16.4 %collective-permute-start.7 = (bf16[2,64,1536]{2,1,0:T(8,128)(2,1)S(1)}, bf16[2,64,1536]{2,1,0:T(8,128)(2,1)S(1)}, u32[]{:S(2)}, u32[]{:S(2)}) collective-permute-start(bf16[2,64,1536]{2,1,0:T(8,128)(2,1)S(1)} %get-tuple-element.70), channel_id=1, source_target_pairs={{0,8},{8,0},{16,24},{24,16},{1,9},{9,1},{17,25},{25,17},{2,10},{10... | collective-permute-start | bytes 1179656 | tf_op jit(solution)/shard_map/ppermute | solution.py:353
  30.3 15.2 %collective-permute-start.8 = (bf16[2,64,1536]{2,1,0:T(8,128)(2,1)S(1)}, bf16[2,64,1536]{2,1,0:T(8,128)(2,1)S(1)}, u32[]{:S(2)}, u32[]{:S(2)}) collective-permute-start(bf16[2,64,1536]{2,1,0:T(8,128)(2,1)S(1)} %get-tuple-element.71), channel_id=1, source_target_pairs={{0,16},{8,24},{16,0},{24,8},{1,17},{9,25},{17,1},{25,9},{2,18},{10... | collective-permute-start | bytes 1179656 | tf_op jit(solution)/shard_map/ppermute | solution.py:353
  40.0 13.9 %collective-permute-start.4 = (bf16[32,2560]{1,0:T(8,128)(2,1)S(1)}, bf16[32,2560]{1,0:T(8,128)(2,1)S(1)}, u32[]{:S(2)}, u32[]{:S(2)}) collective-permute-start(bf16[32,2560]{1,0:T(8,128)(2,1)S(1)} %copy-done.6), channel_id=1, source_target_pairs={{0,2},{1,3},{2,0},{3,1},{4,6},{5,7},{6,4},{7,5},{8,10},{9,11},{10,... | collective-permute-start | bytes 491528 | tf_op jit(solution)/shard_map/ppermute | solution.py:574
  42.5 15.1 %collective-permute-start.5 = (bf16[32,2560]{1,0:T(8,128)(2,1)S(1)}, bf16[32,2560]{1,0:T(8,128)(2,1)S(1)}, u32[]{:S(2)}, u32[]{:S(2)}) collective-permute-start(bf16[32,2560]{1,0:T(8,128)(2,1)S(1)} %copy-done.6), channel_id=1, source_target_pairs={{0,4},{1,5},{2,6},{3,7},{4,0},{5,1},{6,2},{7,3},{8,12},{9,13},{10,... | collective-permute-start | bytes 491528 | tf_op jit(solution)/shard_map/ppermute | solution.py:574
  44.2 13.4 %collective-permute-start.6 = (bf16[32,2560]{1,0:T(8,128)(2,1)S(1)}, bf16[32,2560]{1,0:T(8,128)(2,1)S(1)}, u32[]{:S(2)}, u32[]{:S(2)}) collective-permute-start(bf16[32,2560]{1,0:T(8,128)(2,1)S(1)} %copy-done.6), channel_id=1, source_target_pairs={{0,6},{1,7},{2,4},{3,5},{4,2},{5,3},{6,0},{7,1},{8,14},{9,15},{10,... | collective-permute-start | bytes 491528 | tf_op jit(solution)/shard_map/ppermute | solution.py:574
  45.0 13.0 %collective-permute-start.10 = (bf16[2,64,1792]{2,1,0:T(8,128)(2,1)S(1)}, bf16[2,64,1792]{2,1,0:T(8,128)(2,1)S(1)}, u32[]{:S(2)}, u32[]{:S(2)}) collective-permute-start(bf16[2,64,1792]{2,1,0:T(8,128)(2,1)S(1)} %get-tuple-element.80), channel_id=1, source_target_pairs={{0,8},{8,0},{16,24},{24,16},{1,9},{9,1},{17,25},{25,17},{2,10},{10... | collective-permute-start | bytes 1376264 | tf_op jit(solution)/shard_map/ppermute | solution.py:353
  45.5 12.5 %collective-permute-start.11 = (bf16[2,64,1792]{2,1,0:T(8,128)(2,1)S(1)}, bf16[2,64,1792]{2,1,0:T(8,128)(2,1)S(1)}, u32[]{:S(2)}, u32[]{:S(2)}) collective-permute-start(bf16[2,64,1792]{2,1,0:T(8,128)(2,1)S(1)} %get-tuple-element.81), channel_id=1, source_target_pairs={{0,16},{8,24},{16,0},{24,8},{1,17},{9,25},{17,1},{25,9},{2,18},{10... | collective-permute-start | bytes 1376264 | tf_op jit(solution)/shard_map/ppermute | solution.py:353
  58.2 15.4 %collective-permute-start.18 = (bf16[2,32,3328]{2,1,0:T(8,128)(2,1)S(1)}, bf16[2,32,3328]{2,1,0:T(8,128)(2,1)S(1)}, u32[]{:S(2)}, u32[]{:S(2)}) collective-permute-start(bf16[2,32,3328]{2,1,0:T(8,128)(2,1)S(1)} %pad_maximum_fusion.5.refs_0_), channel_id=1, source_target_pairs={{0,8},{8,0},{16,24},{24,16},{1,9},{9,1},{17,25},{25,17},{2,10},{10... | collective-permute-start | bytes 1277960 | tf_op jit(solution)/shard_map/ppermute | solution.py:353
  58.8 14.8 %collective-permute-start.19 = (bf16[2,32,3328]{2,1,0:T(8,128)(2,1)S(1)}, bf16[2,32,3328]{2,1,0:T(8,128)(2,1)S(1)}, u32[]{:S(2)}, u32[]{:S(2)}) collective-permute-start(bf16[2,32,3328]{2,1,0:T(8,128)(2,1)S(1)} %pad_maximum_fusion.6.refs_1_), channel_id=1, source_target_pairs={{0,16},{8,24},{16,0},{24,8},{1,17},{9,25},{17,1},{25,9},{2,18},{10... | collective-permute-start | bytes 1277960 | tf_op jit(solution)/shard_map/ppermute | solution.py:353
  76.2 10.0 %collective-permute-start.14 = (bf16[1,64,2304]{2,1,0:T(8,128)(2,1)S(1)}, bf16[1,64,2304]{2,1,0:T(8,128)(2,1)S(1)}, u32[]{:S(2)}, u32[]{:S(2)}) collective-permute-start(bf16[1,64,2304]{2,1,0:T(8,128)(2,1)S(1)} %get-tuple-element.94), channel_id=1, source_target_pairs={{0,8},{8,0},{16,24},{24,16},{1,9},{9,1},{17,25},{25,17},{2,10},{10... | collective-permute-start | bytes 884744 | tf_op jit(solution)/shard_map/ppermute | solution.py:353
  79.4 12.4 %collective-permute-start.24 = (bf16[2,64,1024]{2,1,0:T(8,128)(2,1)S(1)}, bf16[2,64,1024]{2,1,0:T(8,128)(2,1)S(1)}, u32[]{:S(2)}, u32[]{:S(2)}) collective-permute-start(bf16[2,64,1024]{2,1,0:T(8,128)(2,1)S(1)} %pad_maximum_fusion.8.refs_0_), channel_id=1, source_target_pairs={{0,8},{8,0},{16,24},{24,16},{1,9},{9,1},{17,25},{25,17},{2,10},{10... | collective-permute-start | bytes 786440 | tf_op jit(solution)/shard_map/ppermute | solution.py:353
  81.0 10.9 %collective-permute-start.25 = (bf16[2,64,1024]{2,1,0:T(8,128)(2,1)S(1)}, bf16[2,64,1024]{2,1,0:T(8,128)(2,1)S(1)}, u32[]{:S(2)}, u32[]{:S(2)}) collective-permute-start(bf16[2,64,1024]{2,1,0:T(8,128)(2,1)S(1)} %pad_maximum_fusion.8.refs_0_), channel_id=1, source_target_pairs={{0,16},{8,24},{16,0},{24,8},{1,17},{9,25},{17,1},{25,9},{2,18},{10... | collective-permute-start | bytes 786440 | tf_op jit(solution)/shard_map/ppermute | solution.py:353
  96.0 13.2 %collective-permute-start.22 = (bf16[2,64,2304]{2,1,0:T(8,128)(2,1)S(1)}, bf16[2,64,2304]{2,1,0:T(8,128)(2,1)S(1)}, u32[]{:S(2)}, u32[]{:S(2)}) collective-permute-start(bf16[2,64,2304]{2,1,0:T(8,128)(2,1)S(1)} %pad_maximum_fusion.4.refs_8_.refs_0_), channel_id=1, source_target_pairs={{0,8},{8,0},{16,24},{24,16},{1,9},{9,1},{17,25},{25,17},{2,10},{10... | collective-permute-start | bytes 1769480 | tf_op jit(solution)/shard_map/ppermute | solution.py:353
  97.2 12.2 %collective-permute-start.23 = (bf16[2,64,2304]{2,1,0:T(8,128)(2,1)S(1)}, bf16[2,64,2304]{2,1,0:T(8,128)(2,1)S(1)}, u32[]{:S(2)}, u32[]{:S(2)}) collective-permute-start(bf16[2,64,2304]{2,1,0:T(8,128)(2,1)S(1)} %pad_maximum_fusion.4.refs_8_.refs_0_), channel_id=1, source_target_pairs={{0,16},{8,24},{16,0},{24,8},{1,17},{9,25},{17,1},{25,9},{2,18},{10... | collective-permute-start | bytes 1769480 | tf_op jit(solution)/shard_map/ppermute | solution.py:353
  118.1 13.7 %collective-permute-start.30 = (bf16[1,64,3328]{2,1,0:T(8,128)(2,1)S(1)}, bf16[1,64,3328]{2,1,0:T(8,128)(2,1)S(1)}, u32[]{:S(2)}, u32[]{:S(2)}) collective-permute-start(bf16[1,64,3328]{2,1,0:T(8,128)(2,1)S(1)} %fusion.4.refs_0_), channel_id=1, source_target_pairs={{0,8},{8,0},{16,24},{24,16},{1,9},{9,1},{17,25},{25,17},{2,10},{10... | collective-permute-start | bytes 1277960 | tf_op jit(solution)/shard_map/ppermute | solution.py:353
  120.5 11.3 %collective-permute-start.31 = (bf16[1,64,3328]{2,1,0:T(8,128)(2,1)S(1)}, bf16[1,64,3328]{2,1,0:T(8,128)(2,1)S(1)}, u32[]{:S(2)}, u32[]{:S(2)}) collective-permute-start(bf16[1,64,3328]{2,1,0:T(8,128)(2,1)S(1)} %fusion.4.refs_0_), channel_id=1, source_target_pairs={{0,16},{8,24},{16,0},{24,8},{1,17},{9,25},{17,1},{25,9},{2,18},{10... | collective-permute-start | bytes 1277960 | tf_op jit(solution)/shard_map/ppermute | solution.py:353
  132.0 17.5 %collective-permute-start.36 = (bf16[1,32,3328]{2,1,0:T(8,128)(2,1)S(1)}, bf16[1,32,3328]{2,1,0:T(8,128)(2,1)S(1)}, u32[]{:S(2)}, u32[]{:S(2)}) collective-permute-start(bf16[1,32,3328]{2,1,0:T(8,128)(2,1)S(1)} %slice.156), channel_id=1, source_target_pairs={{0,16},{8,24},{16,0},{24,8},{1,17},{9,25},{17,1},{25,9},{2,18},{10... | collective-permute-start | bytes 638984 | tf_op jit(solution)/shard_map/ppermute | solution.py:353
  133.2 16.2 %collective-permute-start.37 = (bf16[1,32,3328]{2,1,0:T(8,128)(2,1)S(1)}, bf16[1,32,3328]{2,1,0:T(8,128)(2,1)S(1)}, u32[]{:S(2)}, u32[]{:S(2)}) collective-permute-start(bf16[1,32,3328]{2,1,0:T(8,128)(2,1)S(1)} %slice.157), channel_id=1, source_target_pairs={{0,8},{8,0},{16,24},{24,16},{1,9},{9,1},{17,25},{25,17},{2,10},{10... | collective-permute-start | bytes 638984 | tf_op jit(solution)/shard_map/ppermute | solution.py:353
  135.3 24.7 %collective-permute-start.35 = (bf16[32,2560]{1,0:T(8,128)(2,1)S(1)}, bf16[32,2560]{1,0:T(8,128)(2,1)S(1)}, u32[]{:S(2)}, u32[]{:S(2)}) collective-permute-start(bf16[32,2560]{1,0:T(8,128)(2,1)S(1)} %get-tuple-element.125.refs_11_), channel_id=1, source_target_pairs={{0,6},{1,7},{2,4},{3,5},{4,2},{5,3},{6,0},{7,1},{8,14},{9,15},{10,... | collective-permute-start | bytes 491528 | tf_op jit(solution)/shard_map/ppermute | solution.py:574
  137.3 22.6 %collective-permute-start.34 = (bf16[32,2560]{1,0:T(8,128)(2,1)S(1)}, bf16[32,2560]{1,0:T(8,128)(2,1)S(1)}, u32[]{:S(2)}, u32[]{:S(2)}) collective-permute-start(bf16[32,2560]{1,0:T(8,128)(2,1)S(1)} %get-tuple-element.126.refs_10_), channel_id=1, source_target_pairs={{0,4},{1,5},{2,6},{3,7},{4,0},{5,1},{6,2},{7,3},{8,12},{9,13},{10,... | collective-permute-start | bytes 491528 | tf_op jit(solution)/shard_map/ppermute | solution.py:574
  139.1 20.8 %collective-permute-start.33 = (bf16[32,2560]{1,0:T(8,128)(2,1)S(1)}, bf16[32,2560]{1,0:T(8,128)(2,1)S(1)}, u32[]{:S(2)}, u32[]{:S(2)}) collective-permute-start(bf16[32,2560]{1,0:T(8,128)(2,1)S(1)} %get-tuple-element.124.refs_9_), channel_id=1, source_target_pairs={{0,2},{1,3},{2,0},{3,1},{4,6},{5,7},{6,4},{7,5},{8,10},{9,11},{10,... | collective-permute-start | bytes 491528 | tf_op jit(solution)/shard_map/ppermute | solution.py:574
  (21 other events, 223.2 us)

commit v4 on v3

--- a/solution.py
+++ b/solution.py
@@ -14,7 +14,7 @@
 ANY = pl.BlockSpec(memory_space=pl.ANY)
 HBM = pl.BlockSpec(memory_space=pltpu.HBM)
 WHOLE = pl.BlockSpec(memory_space=pltpu.VMEM)
-GATE_UP_CUTS = (6, 13)
+GATE_UP_CUTS = (7, 13)
 BACK_CUTS = (4, 13)
 
 

time: 161 us -> 159 us (0.988)
  starting transfers between devices: 47.3 us -> 41.3 us
  waiting for transfers between devices: 21.3 us -> 25.3 us
    ppermute x26, waiting for transfers between devices: 13.8 us -> 21.9 us  [_swap(): return lax.ppermute(value, 'row', [(i, i ^ bit) for i in range(4)])]
    ppermute x26, starting transfers between devices: 32 us -> 26 us  [_swap(): return lax.ppermute(value, 'row', [(i, i ^ bit) for i in range(4)])]
    ppermute x12, waiting for transfers between devices: 7.5 us -> 3.41 us  [_col_swap(): return lax.ppermute(value, 'col', [(i, i ^ bits) for i in range(8)])]
  transfers between devices with their start and end apart: 38 -> 38, of which waited for: 15 -> 18; matrix products, arithmetic and copies ran while one was open for 2% -> 2% of each run, Pallas kernels for 47% -> 47%
where the time goes in v4:
time: 159 us
  Pallas kernels  83.4 us (52%)
  starting transfers between devices  41.3 us (26%)
  waiting for transfers between devices  25.3 us (16%)
  other arithmetic  3.69 us (2%)
  local copies, waits for them, and re-layouts  3.67 us (2%)
    pallas_call x4, Pallas kernels, backward(): pl.pallas_call(functools.partial(_backward_kernel, first, count, inputs i...  30.8 us
    ppermute x26, starting transfers between devices, _swap(): return lax.ppermute(value, 'row', [(i, i ^ bit) for i in range(4)])  26 us
    ppermute x26, waiting for transfers between devices, _swap(): return lax.ppermute(value, 'row', [(i, i ^ bit) for i in range(4)])  21.9 us
    ppermute x12, starting transfers between devices, _col_swap(): return lax.ppermute(value, 'col', [(i, i ^ bits) for i in range(8)])  15.3 us
    pallas_call x2, Pallas kernels, gate_up_sums(): pl.pallas_call(functools.partial(_gate_up_kernel, first, count, len(after...  15.3 us
    pallas_call x1, Pallas kernels, down_grad(): pl.pallas_call(functools.partial(_down_grad_kernel, count, len(after)), i...  10.4 us
    pallas_call x2, Pallas kernels, back_sums(): pl.pallas_call(functools.partial(_back_kernel, first, count, len(after)),...  10.2 us
    pallas_call x1, Pallas kernels, pack_gate_up(): pl.pallas_call(_pack_rows_kernel, grid=(pl.cdiv(code_cols, 128),), in_spe...  8.86 us
  transfers between devices with their start and end apart: 38, of which 18 were waited for; matrix products, arithmetic and copies ran while one was open for 2% of the time, Pallas kernels for 47%

profile of v4, /device:TPU:0, one launch (start us, length us, event | category | flops | bytes accessed | tf_op | source)
XLA Modules:
  0.0 158.7 jit_solution(8361803514316030968)
XLA Ops:
  0.6 3.1 %collective-permute-start = (bf16[32,2560]{1,0:T(8,128)(2,1)}, bf16[32,2560]{1,0:T(8,128)(2,1)S(1)}, u32[]{:S(2)}, u32[]{:S(2)}) collective-permute-start(bf16[32,2560]{1,0:T(8,128)(2,1)} %param.8), channel_id=1, source_target_pairs={{0,2},{1,3},{2,0},{3,1},{4,6},{5,7},{6,4},{7,5},{8,10},{9,11},{10,... | collective-permute-start | bytes 491528 | tf_op jit(solution)/shard_map/ppermute | solution.py:574
  3.7 2.6 %collective-permute-start.1 = (bf16[32,2560]{1,0:T(8,128)(2,1)}, bf16[32,2560]{1,0:T(8,128)(2,1)S(1)}, u32[]{:S(2)}, u32[]{:S(2)}) collective-permute-start(bf16[32,2560]{1,0:T(8,128)(2,1)} %param.8), channel_id=1, source_target_pairs={{0,4},{1,5},{2,6},{3,7},{4,0},{5,1},{6,2},{7,3},{8,12},{9,13},{10,... | collective-permute-start | bytes 491528 | tf_op jit(solution)/shard_map/ppermute | solution.py:574
  10.0 8.9 %pack_gate_up.1.bits_any.refs_5_ = s8[640,3328]{1,0:T(32,128)(4,1)S(1)} custom-call(s32[832,640]{1,0:T(8,128)S(1)} %bitcast.56, s32[832,640]{1,0:T(8,128)S(1)} %bitcast.57, bf16[512,512]{1,0:T(8,128)(2,1)S(1)} %fusion.lane_ref, bf16[128,64]{1,0:T(8,128)(2,1)S(1)} %select_convert_fusion.1.row_ref), custom_call_target="tpu_custom_call" | custom-call | flops 10000000000 | bytes 100000000 | tf_op jit(solution)/shard_map/pack_gate_up/pallas_call | solution.py:186
  21.4 8.0 %gate_up_sums.2 = (f32[2,64,1792]{2,1,0:T(8,128)S(1)}, bf16[2,64,1792]{2,1,0:T(8,128)(2,1)S(1)}, bf16[2,64,1792]{2,1,0:T(8,128)(2,1)S(1)}, f32[2,64,1792]{2,1,0:T(8,128)S(1)}) custom-call(bf16[256,2560]{1,0:T(8,128)(2,1)S(1)} %bitcast_dynamic-update-slice_fusion.8.tok_ref.refs_6_, bf16[2560,3328]{1,0:T(8,128)(2,1)} %refs_6_.3, bf16[2560,3328]{1,0:T(8,128)(2,1)} %refs_7_.3, ...), custom_call_target="tpu_custom_call" | custom-call | flops 10000000000 | bytes 100000000 | tf_op jit(solution)/shard_map/gate_up_sums/pallas_call | solution.py:325
  29.4 1.7 %collective-permute-start.7 = (bf16[2,64,1792]{2,1,0:T(8,128)(2,1)S(1)}, bf16[2,64,1792]{2,1,0:T(8,128)(2,1)S(1)}, u32[]{:S(2)}, u32[]{:S(2)}) collective-permute-start(bf16[2,64,1792]{2,1,0:T(8,128)(2,1)S(1)} %get-tuple-element.70), channel_id=1, source_target_pairs={{0,8},{8,0},{16,24},{24,16},{1,9},{9,1},{17,25},{25,17},{2,10},{10... | collective-permute-start | bytes 1376264 | tf_op jit(solution)/shard_map/ppermute | solution.py:353
  32.7 7.2 %gate_up_sums.3 = (f32[2,64,1536]{2,1,0:T(8,128)S(1)}, bf16[2,64,1536]{2,1,0:T(8,128)(2,1)S(1)}, bf16[2,64,1536]{2,1,0:T(8,128)(2,1)S(1)}, f32[2,64,1536]{2,1,0:T(8,128)S(1)}) custom-call(bf16[256,2560]{1,0:T(8,128)(2,1)S(1)} %bitcast_dynamic-update-slice_fusion.8.tok_ref.refs_6_, bf16[2560,3328]{1,0:T(8,128)(2,1)} %refs_6_.3, bf16[2560,3328]{1,0:T(8,128)(2,1)} %refs_7_.3, ...), custom_call_target="tpu_custom_call" | custom-call | flops 10000000000 | bytes 100000000 | tf_op jit(solution)/shard_map/gate_up_sums/pallas_call | solution.py:325
  40.0 2.5 %collective-permute-start.4 = (bf16[32,2560]{1,0:T(8,128)(2,1)S(1)}, bf16[32,2560]{1,0:T(8,128)(2,1)S(1)}, u32[]{:S(2)}, u32[]{:S(2)}) collective-permute-start(bf16[32,2560]{1,0:T(8,128)(2,1)S(1)} %copy-done.6), channel_id=1, source_target_pairs={{0,2},{1,3},{2,0},{3,1},{4,6},{5,7},{6,4},{7,5},{8,10},{9,11},{10,... | collective-permute-start | bytes 491528 | tf_op jit(solution)/shard_map/ppermute | solution.py:574
  42.5 1.7 %collective-permute-start.5 = (bf16[32,2560]{1,0:T(8,128)(2,1)S(1)}, bf16[32,2560]{1,0:T(8,128)(2,1)S(1)}, u32[]{:S(2)}, u32[]{:S(2)}) collective-permute-start(bf16[32,2560]{1,0:T(8,128)(2,1)S(1)} %copy-done.6), channel_id=1, source_target_pairs={{0,4},{1,5},{2,6},{3,7},{4,0},{5,1},{6,2},{7,3},{8,12},{9,13},{10,... | collective-permute-start | bytes 491528 | tf_op jit(solution)/shard_map/ppermute | solution.py:574
  46.0 7.8 %pack_down.1.bits_any.refs_6_ = s8[3328,512]{1,0:T(32,128)(4,1)S(1)} custom-call(s32[832,640]{1,0:T(8,128)S(1)} %copy-done.4, bf16[512,512]{1,0:T(8,128)(2,1)S(1)} %fusion.lane_ref, bf16[256,128]{1,0:T(8,128)(2,1)S(1)} %select_convert_fusion.row_ref, f32[2,64,1536]{2,1,0:T(8,128)S(1)} %get-tuple-element.68.refs_0_, ...), custom_call_target="tpu_custom_call" | custom-call | flops 10000000000 | bytes 100000000 | tf_op jit(solution)/shard_map/pack_down/pallas_call | solution.py:204
  60.0 3.6 %back_sums.2 = (f32[1,64,1024]{2,1,0:T(8,128)S(1)}, bf16[1,64,1024]{2,1,0:T(8,128)(2,1)S(1)}, bf16[1,64,1024]{2,1,0:T(8,128)(2,1)S(1)}, f32[1,64,1024]{2,1,0:T(8,128)S(1)}) custom-call(bf16[256,2560]{1,0:T(8,128)(2,1)S(1)} %bitcast_dynamic-update-slice_fusion.grad_ref.refs_5_, bf16[3328,2560]{1,0:T(8,128)(2,1)} %down_any.3, ...), custom_call_target="tpu_custom_call" | custom-call | flops 10000000000 | bytes 100000000 | tf_op jit(solution)/shard_map/back_sums/pallas_call | solution.py:340
  64.7 6.6 %back_sums.3 = (f32[1,64,2304]{2,1,0:T(8,128)S(1)}, bf16[1,64,2304]{2,1,0:T(8,128)(2,1)S(1)}, bf16[1,64,2304]{2,1,0:T(8,128)(2,1)S(1)}, f32[1,64,2304]{2,1,0:T(8,128)S(1)}) custom-call(bf16[256,2560]{1,0:T(8,128)(2,1)S(1)} %bitcast_dynamic-update-slice_fusion.grad_ref.refs_5_, bf16[3328,2560]{1,0:T(8,128)(2,1)} %down_any.3, ...), custom_call_target="tpu_custom_call" | custom-call | flops 10000000000 | bytes 100000000 | tf_op jit(solution)/shard_map/back_sums/pallas_call | solution.py:340
  80.5 4.5 %collective-permute-done.14 = bf16[1,64,2304]{2,1,0:T(8,128)(2,1)S(1)} collective-permute-done((bf16[1,64,2304]{2,1,0:T(8,128)(2,1)S(1)}, bf16[1,64,2304]{2,1,0:T(8,128)(2,1)S(1)}, u32[]{:S(2)}, u32[]{:S(2)}) %collective-permute-start.14) | collective-permute-done | bytes 294944 | tf_op jit(solution)/shard_map/ppermute | solution.py:353
  88.2 2.4 %collective-permute-done.24.refs_1_ = bf16[2,64,1024]{2,1,0:T(8,128)(2,1)S(1)} collective-permute-done((bf16[2,64,1024]{2,1,0:T(8,128)(2,1)S(1)}, bf16[2,64,1024]{2,1,0:T(8,128)(2,1)S(1)}, u32[]{:S(2)}, u32[]{:S(2)}) %collective-permute-start.24) | collective-permute-done | bytes 262176 | tf_op jit(solution)/shard_map/ppermute | solution.py:353
  91.3 1.9 %collective-permute-start.26 = (bf16[2,32,1024]{2,1,0:T(8,128)(2,1)S(1)}, bf16[2,32,1024]{2,1,0:T(8,128)(2,1)S(1)}, u32[]{:S(2)}, u32[]{:S(2)}) collective-permute-start(bf16[2,32,1024]{2,1,0:T(8,128)(2,1)S(1)} %slice.152), channel_id=1, source_target_pairs={{0,16},{8,24},{16,0},{24,8},{1,17},{9,25},{17,1},{25,9},{2,18},{10... | collective-permute-start | bytes 393224 | tf_op jit(solution)/shard_map/ppermute | solution.py:353
  97.5 2.2 %collective-permute-done.27.refs_4_ = bf16[2,32,1024]{2,1,0:T(8,128)(2,1)S(1)} collective-permute-done((bf16[2,32,1024]{2,1,0:T(8,128)(2,1)S(1)}, bf16[2,32,1024]{2,1,0:T(8,128)(2,1)S(1)}, u32[]{:S(2)}, u32[]{:S(2)}) %collective-permute-start.27) | collective-permute-done | bytes 131104 | tf_op jit(solution)/shard_map/ppermute | solution.py:353
  99.8 5.4 %backward.4 = (f32[4,32,2560]{2,1,0:T(8,128)S(1)}, f32[4,32,2560]{2,1,0:T(8,128)S(1)}) custom-call(bf16[2,64,1024]{2,1,0:T(8,128)(2,1)S(1)} %pad_maximum_fusion.8.refs_0_, bf16[2,64,1024]{2,1,0:T(8,128)(2,1)S(1)} %collective-permute-done.24.refs_1_, bf16[2,64,1024]{2,1,0:T(8,128)(2,1)S(1)} %collective-permute-done.25.refs_2_, ...), custom_call_target="tpu_custom_call" | custom-call | flops 10000000000 | bytes 100000000 | tf_op jit(solution)/shard_map/backward/pallas_call | solution.py:515
  105.2 3.0 %collective-permute-done.22.refs_1_ = bf16[2,64,2304]{2,1,0:T(8,128)(2,1)S(1)} collective-permute-done((bf16[2,64,2304]{2,1,0:T(8,128)(2,1)S(1)}, bf16[2,64,2304]{2,1,0:T(8,128)(2,1)S(1)}, u32[]{:S(2)}, u32[]{:S(2)}) %collective-permute-start.22) | collective-permute-done | bytes 589856 | tf_op jit(solution)/shard_map/ppermute | solution.py:353
  111.0 5.2 %backward.5 = (bf16[2560,3328]{1,0:T(8,128)(2,1)}, bf16[2560,3328]{1,0:T(8,128)(2,1)}) custom-call(bf16[2,64,1024]{2,1,0:T(8,128)(2,1)S(1)} %pad_maximum_fusion.8.refs_0_, bf16[2,64,1024]{2,1,0:T(8,128)(2,1)S(1)} %collective-permute-done.24.refs_1_, bf16[2,64,1024]{2,1,0:T(8,128)(2,1)S(1)} %collective-permute-done.25.refs_2_, ...), custom_call_target="tpu_custom_call" | custom-call | flops 10000000000 | bytes 100000000 | tf_op jit(solution)/shard_map/backward/pallas_call | solution.py:515
  116.2 2.0 %collective-permute-done.29.refs_4_ = bf16[2,32,2304]{2,1,0:T(8,128)(2,1)S(1)} collective-permute-done((bf16[2,32,2304]{2,1,0:T(8,128)(2,1)S(1)}, bf16[2,32,2304]{2,1,0:T(8,128)(2,1)S(1)}, u32[]{:S(2)}, u32[]{:S(2)}) %collective-permute-start.29) | collective-permute-done | bytes 294944 | tf_op jit(solution)/shard_map/ppermute | solution.py:353
  119.3 10.5 %backward.6 = (f32[4,32,2560]{2,1,0:T(8,128)S(1)}, f32[4,32,2560]{2,1,0:T(8,128)S(1)}) custom-call(bf16[2,64,2304]{2,1,0:T(8,128)(2,1)S(1)} %pad_maximum_fusion.4.refs_8_.refs_0_, bf16[2,64,2304]{2,1,0:T(8,128)(2,1)S(1)} %collective-permute-done.22.refs_1_, bf16[2,64,2304]{2,1,0:T(8,128)(2,1)S(1)} %collective-permute-done.23.refs_2_, ...), custom_call_target="tpu_custom_call" | custom-call | flops 10000000000 | bytes 100000000 | tf_op jit(solution)/shard_map/backward/pallas_call | solution.py:515
  130.9 2.0 %collective-permute-start.37 = (bf16[1,32,3328]{2,1,0:T(8,128)(2,1)S(1)}, bf16[1,32,3328]{2,1,0:T(8,128)(2,1)S(1)}, u32[]{:S(2)}, u32[]{:S(2)}) collective-permute-start(bf16[1,32,3328]{2,1,0:T(8,128)(2,1)S(1)} %slice.157), channel_id=1, source_target_pairs={{0,8},{8,0},{16,24},{24,16},{1,9},{9,1},{17,25},{25,17},{2,10},{10... | collective-permute-start | bytes 638984 | tf_op jit(solution)/shard_map/ppermute | solution.py:353
  133.2 2.6 %collective-permute-start.35 = (bf16[32,2560]{1,0:T(8,128)(2,1)S(1)}, bf16[32,2560]{1,0:T(8,128)(2,1)S(1)}, u32[]{:S(2)}, u32[]{:S(2)}) collective-permute-start(bf16[32,2560]{1,0:T(8,128)(2,1)S(1)} %get-tuple-element.125.refs_11_), channel_id=1, source_target_pairs={{0,6},{1,7},{2,4},{3,5},{4,2},{5,3},{6,0},{7,1},{8,14},{9,15},{10,... | collective-permute-start | bytes 491528 | tf_op jit(solution)/shard_map/ppermute | solution.py:574
  137.7 9.7 %backward.7 = (bf16[2560,3328]{1,0:T(8,128)(2,1)}, bf16[2560,3328]{1,0:T(8,128)(2,1)}) custom-call(bf16[2,64,2304]{2,1,0:T(8,128)(2,1)S(1)} %pad_maximum_fusion.4.refs_8_.refs_0_, bf16[2,64,2304]{2,1,0:T(8,128)(2,1)S(1)} %collective-permute-done.22.refs_1_, ...), custom_call_target="tpu_custom_call", output_to_operand_aliasing={{0}: (7, {}), {1}: (8, {})} | custom-call | flops 10000000000 | bytes 100000000 | tf_op jit(solution)/shard_map/backward/pallas_call | solution.py:515
  147.4 10.4 %down_grad.1 = bf16[3328,2560]{1,0:T(8,128)(2,1)} custom-call(bf16[1,64,3328]{2,1,0:T(8,128)(2,1)S(1)} %fusion.4.refs_0_, bf16[1,64,3328]{2,1,0:T(8,128)(2,1)S(1)} %collective-permute-done.30.refs_1_, bf16[1,64,3328]{2,1,0:T(8,128)(2,1)S(1)} %collective-permute-done.31.refs_2_, bf16[1,32,3328]{2,1,0:T(8,128)(2,1)S(1)} %collective-permute-done.36.refs_3_, ...), custom_call_target="tpu_custom_call" | custom-call | flops 10000000000 | bytes 100000000 | tf_op jit(solution)/shard_map/down_grad/pallas_call | solution.py:561
  (136 shorter events, 41.6 us)
Async XLA Ops:
  0.6 18.3 %collective-permute-start = (bf16[32,2560]{1,0:T(8,128)(2,1)}, bf16[32,2560]{1,0:T(8,128)(2,1)S(1)}, u32[]{:S(2)}, u32[]{:S(2)}) collective-permute-start(bf16[32,2560]{1,0:T(8,128)(2,1)} %param.8), channel_id=1, source_target_pairs={{0,2},{1,3},{2,0},{3,1},{4,6},{5,7},{6,4},{7,5},{8,10},{9,11},{10,... | collective-permute-start | bytes 491528 | tf_op jit(solution)/shard_map/ppermute | solution.py:574
  3.7 15.3 %collective-permute-start.1 = (bf16[32,2560]{1,0:T(8,128)(2,1)}, bf16[32,2560]{1,0:T(8,128)(2,1)S(1)}, u32[]{:S(2)}, u32[]{:S(2)}) collective-permute-start(bf16[32,2560]{1,0:T(8,128)(2,1)} %param.8), channel_id=1, source_target_pairs={{0,4},{1,5},{2,6},{3,7},{4,0},{5,1},{6,2},{7,3},{8,12},{9,13},{10,... | collective-permute-start | bytes 491528 | tf_op jit(solution)/shard_map/ppermute | solution.py:574
  6.3 12.7 %collective-permute-start.2 = (bf16[32,2560]{1,0:T(8,128)(2,1)}, bf16[32,2560]{1,0:T(8,128)(2,1)S(1)}, u32[]{:S(2)}, u32[]{:S(2)}) collective-permute-start(bf16[32,2560]{1,0:T(8,128)(2,1)} %param.8), channel_id=1, source_target_pairs={{0,6},{1,7},{2,4},{3,5},{4,2},{5,3},{6,0},{7,1},{8,14},{9,15},{10,... | collective-permute-start | bytes 491528 | tf_op jit(solution)/shard_map/ppermute | solution.py:574
  29.4 15.5 %collective-permute-start.7 = (bf16[2,64,1792]{2,1,0:T(8,128)(2,1)S(1)}, bf16[2,64,1792]{2,1,0:T(8,128)(2,1)S(1)}, u32[]{:S(2)}, u32[]{:S(2)}) collective-permute-start(bf16[2,64,1792]{2,1,0:T(8,128)(2,1)S(1)} %get-tuple-element.70), channel_id=1, source_target_pairs={{0,8},{8,0},{16,24},{24,16},{1,9},{9,1},{17,25},{25,17},{2,10},{10... | collective-permute-start | bytes 1376264 | tf_op jit(solution)/shard_map/ppermute | solution.py:353
  31.2 14.3 %collective-permute-start.8 = (bf16[2,64,1792]{2,1,0:T(8,128)(2,1)S(1)}, bf16[2,64,1792]{2,1,0:T(8,128)(2,1)S(1)}, u32[]{:S(2)}, u32[]{:S(2)}) collective-permute-start(bf16[2,64,1792]{2,1,0:T(8,128)(2,1)S(1)} %get-tuple-element.71), channel_id=1, source_target_pairs={{0,16},{8,24},{16,0},{24,8},{1,17},{9,25},{17,1},{25,9},{2,18},{10... | collective-permute-start | bytes 1376264 | tf_op jit(solution)/shard_map/ppermute | solution.py:353
  40.0 17.3 %collective-permute-start.4 = (bf16[32,2560]{1,0:T(8,128)(2,1)S(1)}, bf16[32,2560]{1,0:T(8,128)(2,1)S(1)}, u32[]{:S(2)}, u32[]{:S(2)}) collective-permute-start(bf16[32,2560]{1,0:T(8,128)(2,1)S(1)} %copy-done.6), channel_id=1, source_target_pairs={{0,2},{1,3},{2,0},{3,1},{4,6},{5,7},{6,4},{7,5},{8,10},{9,11},{10,... | collective-permute-start | bytes 491528 | tf_op jit(solution)/shard_map/ppermute | solution.py:574
  42.5 15.1 %collective-permute-start.5 = (bf16[32,2560]{1,0:T(8,128)(2,1)S(1)}, bf16[32,2560]{1,0:T(8,128)(2,1)S(1)}, u32[]{:S(2)}, u32[]{:S(2)}) collective-permute-start(bf16[32,2560]{1,0:T(8,128)(2,1)S(1)} %copy-done.6), channel_id=1, source_target_pairs={{0,4},{1,5},{2,6},{3,7},{4,0},{5,1},{6,2},{7,3},{8,12},{9,13},{10,... | collective-permute-start | bytes 491528 | tf_op jit(solution)/shard_map/ppermute | solution.py:574
  44.2 13.4 %collective-permute-start.6 = (bf16[32,2560]{1,0:T(8,128)(2,1)S(1)}, bf16[32,2560]{1,0:T(8,128)(2,1)S(1)}, u32[]{:S(2)}, u32[]{:S(2)}) collective-permute-start(bf16[32,2560]{1,0:T(8,128)(2,1)S(1)} %copy-done.6), channel_id=1, source_target_pairs={{0,6},{1,7},{2,4},{3,5},{4,2},{5,3},{6,0},{7,1},{8,14},{9,15},{10,... | collective-permute-start | bytes 491528 | tf_op jit(solution)/shard_map/ppermute | solution.py:574
  45.0 10.1 %collective-permute-start.10 = (bf16[2,64,1536]{2,1,0:T(8,128)(2,1)S(1)}, bf16[2,64,1536]{2,1,0:T(8,128)(2,1)S(1)}, u32[]{:S(2)}, u32[]{:S(2)}) collective-permute-start(bf16[2,64,1536]{2,1,0:T(8,128)(2,1)S(1)} %get-tuple-element.80), channel_id=1, source_target_pairs={{0,8},{8,0},{16,24},{24,16},{1,9},{9,1},{17,25},{25,17},{2,10},{10... | collective-permute-start | bytes 1179656 | tf_op jit(solution)/shard_map/ppermute | solution.py:353
  55.6 17.2 %collective-permute-start.18 = (bf16[2,32,3328]{2,1,0:T(8,128)(2,1)S(1)}, bf16[2,32,3328]{2,1,0:T(8,128)(2,1)S(1)}, u32[]{:S(2)}, u32[]{:S(2)}) collective-permute-start(bf16[2,32,3328]{2,1,0:T(8,128)(2,1)S(1)} %pad_maximum_fusion.5.refs_0_), channel_id=1, source_target_pairs={{0,8},{8,0},{16,24},{24,16},{1,9},{9,1},{17,25},{25,17},{2,10},{10... | collective-permute-start | bytes 1277960 | tf_op jit(solution)/shard_map/ppermute | solution.py:353
  57.8 15.1 %collective-permute-start.19 = (bf16[2,32,3328]{2,1,0:T(8,128)(2,1)S(1)}, bf16[2,32,3328]{2,1,0:T(8,128)(2,1)S(1)}, u32[]{:S(2)}, u32[]{:S(2)}) collective-permute-start(bf16[2,32,3328]{2,1,0:T(8,128)(2,1)S(1)} %pad_maximum_fusion.6.refs_1_), channel_id=1, source_target_pairs={{0,16},{8,24},{16,0},{24,8},{1,17},{9,25},{17,1},{25,9},{2,18},{10... | collective-permute-start | bytes 1277960 | tf_op jit(solution)/shard_map/ppermute | solution.py:353
  75.0 10.0 %collective-permute-start.14 = (bf16[1,64,2304]{2,1,0:T(8,128)(2,1)S(1)}, bf16[1,64,2304]{2,1,0:T(8,128)(2,1)S(1)}, u32[]{:S(2)}, u32[]{:S(2)}) collective-permute-start(bf16[1,64,2304]{2,1,0:T(8,128)(2,1)S(1)} %get-tuple-element.94), channel_id=1, source_target_pairs={{0,8},{8,0},{16,24},{24,16},{1,9},{9,1},{17,25},{25,17},{2,10},{10... | collective-permute-start | bytes 884744 | tf_op jit(solution)/shard_map/ppermute | solution.py:353
  76.1 9.9 %collective-permute-start.15 = (bf16[1,64,2304]{2,1,0:T(8,128)(2,1)S(1)}, bf16[1,64,2304]{2,1,0:T(8,128)(2,1)S(1)}, u32[]{:S(2)}, u32[]{:S(2)}) collective-permute-start(bf16[1,64,2304]{2,1,0:T(8,128)(2,1)S(1)} %get-tuple-element.95), channel_id=1, source_target_pairs={{0,16},{8,24},{16,0},{24,8},{1,17},{9,25},{17,1},{25,9},{2,18},{10... | collective-permute-start | bytes 884744 | tf_op jit(solution)/shard_map/ppermute | solution.py:353
  78.6 12.0 %collective-permute-start.24 = (bf16[2,64,1024]{2,1,0:T(8,128)(2,1)S(1)}, bf16[2,64,1024]{2,1,0:T(8,128)(2,1)S(1)}, u32[]{:S(2)}, u32[]{:S(2)}) collective-permute-start(bf16[2,64,1024]{2,1,0:T(8,128)(2,1)S(1)} %pad_maximum_fusion.8.refs_0_), channel_id=1, source_target_pairs={{0,8},{8,0},{16,24},{24,16},{1,9},{9,1},{17,25},{25,17},{2,10},{10... | collective-permute-start | bytes 786440 | tf_op jit(solution)/shard_map/ppermute | solution.py:353
  79.8 11.6 %collective-permute-start.25 = (bf16[2,64,1024]{2,1,0:T(8,128)(2,1)S(1)}, bf16[2,64,1024]{2,1,0:T(8,128)(2,1)S(1)}, u32[]{:S(2)}, u32[]{:S(2)}) collective-permute-start(bf16[2,64,1024]{2,1,0:T(8,128)(2,1)S(1)} %pad_maximum_fusion.8.refs_0_), channel_id=1, source_target_pairs={{0,16},{8,24},{16,0},{24,8},{1,17},{9,25},{17,1},{25,9},{2,18},{10... | collective-permute-start | bytes 786440 | tf_op jit(solution)/shard_map/ppermute | solution.py:353
  94.5 13.7 %collective-permute-start.22 = (bf16[2,64,2304]{2,1,0:T(8,128)(2,1)S(1)}, bf16[2,64,2304]{2,1,0:T(8,128)(2,1)S(1)}, u32[]{:S(2)}, u32[]{:S(2)}) collective-permute-start(bf16[2,64,2304]{2,1,0:T(8,128)(2,1)S(1)} %pad_maximum_fusion.4.refs_8_.refs_0_), channel_id=1, source_target_pairs={{0,8},{8,0},{16,24},{24,16},{1,9},{9,1},{17,25},{25,17},{2,10},{10... | collective-permute-start | bytes 1769480 | tf_op jit(solution)/shard_map/ppermute | solution.py:353
  95.9 13.1 %collective-permute-start.23 = (bf16[2,64,2304]{2,1,0:T(8,128)(2,1)S(1)}, bf16[2,64,2304]{2,1,0:T(8,128)(2,1)S(1)}, u32[]{:S(2)}, u32[]{:S(2)}) collective-permute-start(bf16[2,64,2304]{2,1,0:T(8,128)(2,1)S(1)} %pad_maximum_fusion.4.refs_8_.refs_0_), channel_id=1, source_target_pairs={{0,16},{8,24},{16,0},{24,8},{1,17},{9,25},{17,1},{25,9},{2,18},{10... | collective-permute-start | bytes 1769480 | tf_op jit(solution)/shard_map/ppermute | solution.py:353
  118.2 11.6 %collective-permute-start.30 = (bf16[1,64,3328]{2,1,0:T(8,128)(2,1)S(1)}, bf16[1,64,3328]{2,1,0:T(8,128)(2,1)S(1)}, u32[]{:S(2)}, u32[]{:S(2)}) collective-permute-start(bf16[1,64,3328]{2,1,0:T(8,128)(2,1)S(1)} %fusion.4.refs_0_), channel_id=1, source_target_pairs={{0,8},{8,0},{16,24},{24,16},{1,9},{9,1},{17,25},{25,17},{2,10},{10... | collective-permute-start | bytes 1277960 | tf_op jit(solution)/shard_map/ppermute | solution.py:353
  118.2 11.6 %collective-permute-start.31 = (bf16[1,64,3328]{2,1,0:T(8,128)(2,1)S(1)}, bf16[1,64,3328]{2,1,0:T(8,128)(2,1)S(1)}, u32[]{:S(2)}, u32[]{:S(2)}) collective-permute-start(bf16[1,64,3328]{2,1,0:T(8,128)(2,1)S(1)} %fusion.4.refs_0_), channel_id=1, source_target_pairs={{0,16},{8,24},{16,0},{24,8},{1,17},{9,25},{17,1},{25,9},{2,18},{10... | collective-permute-start | bytes 1277960 | tf_op jit(solution)/shard_map/ppermute | solution.py:353
  129.9 17.5 %collective-permute-start.36 = (bf16[1,32,3328]{2,1,0:T(8,128)(2,1)S(1)}, bf16[1,32,3328]{2,1,0:T(8,128)(2,1)S(1)}, u32[]{:S(2)}, u32[]{:S(2)}) collective-permute-start(bf16[1,32,3328]{2,1,0:T(8,128)(2,1)S(1)} %slice.156), channel_id=1, source_target_pairs={{0,16},{8,24},{16,0},{24,8},{1,17},{9,25},{17,1},{25,9},{2,18},{10... | collective-permute-start | bytes 638984 | tf_op jit(solution)/shard_map/ppermute | solution.py:353
  130.9 16.5 %collective-permute-start.37 = (bf16[1,32,3328]{2,1,0:T(8,128)(2,1)S(1)}, bf16[1,32,3328]{2,1,0:T(8,128)(2,1)S(1)}, u32[]{:S(2)}, u32[]{:S(2)}) collective-permute-start(bf16[1,32,3328]{2,1,0:T(8,128)(2,1)S(1)} %slice.157), channel_id=1, source_target_pairs={{0,8},{8,0},{16,24},{24,16},{1,9},{9,1},{17,25},{25,17},{2,10},{10... | collective-permute-start | bytes 638984 | tf_op jit(solution)/shard_map/ppermute | solution.py:353
  133.2 24.7 %collective-permute-start.35 = (bf16[32,2560]{1,0:T(8,128)(2,1)S(1)}, bf16[32,2560]{1,0:T(8,128)(2,1)S(1)}, u32[]{:S(2)}, u32[]{:S(2)}) collective-permute-start(bf16[32,2560]{1,0:T(8,128)(2,1)S(1)} %get-tuple-element.125.refs_11_), channel_id=1, source_target_pairs={{0,6},{1,7},{2,4},{3,5},{4,2},{5,3},{6,0},{7,1},{8,14},{9,15},{10,... | collective-permute-start | bytes 491528 | tf_op jit(solution)/shard_map/ppermute | solution.py:574
  135.9 22.0 %collective-permute-start.34 = (bf16[32,2560]{1,0:T(8,128)(2,1)S(1)}, bf16[32,2560]{1,0:T(8,128)(2,1)S(1)}, u32[]{:S(2)}, u32[]{:S(2)}) collective-permute-start(bf16[32,2560]{1,0:T(8,128)(2,1)S(1)} %get-tuple-element.126.refs_10_), channel_id=1, source_target_pairs={{0,4},{1,5},{2,6},{3,7},{4,0},{5,1},{6,2},{7,3},{8,12},{9,13},{10,... | collective-permute-start | bytes 491528 | tf_op jit(solution)/shard_map/ppermute | solution.py:574
  137.2 20.7 %collective-permute-start.33 = (bf16[32,2560]{1,0:T(8,128)(2,1)S(1)}, bf16[32,2560]{1,0:T(8,128)(2,1)S(1)}, u32[]{:S(2)}, u32[]{:S(2)}) collective-permute-start(bf16[32,2560]{1,0:T(8,128)(2,1)S(1)} %get-tuple-element.124.refs_9_), channel_id=1, source_target_pairs={{0,2},{1,3},{2,0},{3,1},{4,6},{5,7},{6,4},{7,5},{8,10},{9,11},{10,... | collective-permute-start | bytes 491528 | tf_op jit(solution)/shard_map/ppermute | solution.py:574
  (21 other events, 214.6 us)
